TPU v7x, 32 devices: a whole 2x2x4 slice. The times are simulated.
32 devices in a mesh: section: 4 (over x, core), seq: 8 (over z, y).
Axes of the slice: x: 2, y: 2, z: 4, core: 2. Of those that a mesh axis runs over, the one named last changes fastest.
Arguments:
- hidden: bfloat16 [4, 128, 4096], P('section', 'seq'), may hold values from -6 to 6
- modulation: float32 [4, 3, 4096], P('section'), may hold values from -3 to 3
- w_qkv: bfloat16 [4, 4096, 3, 1024], P('section', None, None, 'seq'), may hold values from -0.09375 to 0.09375
- qk_gain: float32 [4, 2, 128], P('section'), may hold values from 1 to 2.5
- w_out: bfloat16 [4, 1024, 4096], P('section', 'seq'), may hold values from -0.375 to 0.375
- stale_kv: bfloat16 [4, 2, 256, 1024], P('section', None, None, 'seq')
- patch_start: int32 [4], P('section'), may hold values from 0 to 128
Outputs:
- passed: bfloat16 [4, 128, 4096], P('section', 'seq')
All inputs are finite; a program needn't handle non-finite values.
Results may differ from a plain program's by a relative error of at most 0.024.
Values may be sent and summed in bfloat16 or wider, within the bound.
No kernel may reach another device: no remote copies, remote signals or barrier semaphores. Data moves between devices by JAX's collectives and lax.ppermute only.
A program may use at most 64 MiB of HBM per device.

v0:
```python
import math

import jax
import jax.numpy as jnp
from jax import lax
from jax.sharding import PartitionSpec as P


def from_behind(block, axis, distance):
    devices = range(lax.axis_size(axis))
    route = [((i - distance) % len(devices), i) for i in devices]
    return lax.ppermute(block, axis, route)


def modulate(tokens_in, modulation):
    values = tokens_in.astype(jnp.float32)
    average = jnp.mean(values, axis=-1, keepdims=True)
    centred = values - average
    spread = jnp.mean(centred * centred, axis=-1, keepdims=True)
    normed = centred * lax.rsqrt(spread + 1e-06)
    return (values, (normed * (1.0 + modulation[1]) + modulation[0]).astype(jnp.bfloat16))


def head_norm(values, gains):
    return values * lax.rsqrt(jnp.mean(values * values, axis=-1, keepdims=True) + 1e-06) * gains


def per_device(hidden, modulation, w_qkv, qk_gain, w_out, stale_kv, patch_start):
    tokens_in = hidden[0]
    own_rows = tokens_in.shape[0]
    width = w_qkv.shape[1]
    head_size = w_qkv.shape[3]
    layer_mod = modulation[0]
    values, mixed = modulate(tokens_in, layer_mod)
    projection = w_qkv[0].reshape(width, 3 * head_size)
    merged = jnp.dot(
        lax.all_gather(mixed, "seq", axis=0, tiled=True),
        projection,
        preferred_element_type=jnp.float32,
    )
    patch_rows = merged.shape[0]
    merged = merged.reshape(patch_rows, 3, head_size)
    queries = head_norm(merged[:, 0], qk_gain[0, 0]).astype(jnp.bfloat16)
    keys_new = head_norm(merged[:, 1], qk_gain[0, 1]).astype(jnp.bfloat16)
    values_new = merged[:, 2].astype(jnp.bfloat16)
    anchor = patch_start[0]
    stale_keys = stale_kv[0, 0]
    stale_values = stale_kv[0, 1]
    scaling = 1.0 / math.sqrt(head_size)
    nought = jnp.zeros((), jnp.int32)
    keys_all = lax.dynamic_update_slice(stale_keys, keys_new, (anchor, nought))
    values_all = lax.dynamic_update_slice(stale_values, values_new, (anchor, nought))
    scores = jnp.dot(queries, keys_all.T, preferred_element_type=jnp.float32) * scaling
    highest = jnp.max(scores, axis=-1, keepdims=True)
    raised = jnp.exp(scores - highest)
    probs = (raised / jnp.sum(raised, axis=-1, keepdims=True)).astype(jnp.bfloat16)
    attended = jnp.dot(probs, values_all, preferred_element_type=jnp.float32).astype(jnp.bfloat16)
    out_weight = w_out[0]
    partial_value = jnp.dot(attended, out_weight, preferred_element_type=jnp.float32)
    summed = lax.psum(partial_value.astype(jnp.bfloat16), "seq").astype(jnp.float32)
    running = lax.dynamic_slice_in_dim(summed, lax.axis_index("seq") * own_rows, own_rows, 0)
    layer_out = (values + layer_mod[2] * running).astype(jnp.bfloat16)
    received = from_behind(layer_out, "section", 1)
    return received[None]


def solution(mesh):
    in_specs = (
        P("section", "seq", None),
        P("section", None, None),
        P("section", None, None, "seq"),
        P("section", None, None),
        P("section", "seq", None),
        P("section", None, None, "seq"),
        P("section"),
    )
    out_specs = P("section", "seq", None)
    return jax.shard_map(
        per_device, mesh=mesh, in_specs=in_specs, out_specs=out_specs, check_vma=False
    )
```

profile of v0, /device:TPU:0, one launch (start us, length us, event | category | flops | bytes accessed | tf_op | source)
XLA Modules:
  0.0 150.4 jit_solution(9994644400975473198)
XLA Ops:
  6.5 0.0 copy-start
  6.5 0.0 all-gather.2.cloned.1.call-start
  6.5 0.9 fusion.21
  7.4 1.0 convert_reduce_fusion
  8.5 1.1 fusion.8
  9.6 1.7 %fusion.11 = bf16[16,4096]{1,0:T(8,128)(2,1)} fusion(bf16[1,16,4096]{2,1,0:T(8,128)(2,1)} %param.7, f32[4096]{0:T(1024)S(1)} %bitcast.70, f32[4096]{0:T(1024)S(1)} %bitcast.71, f32[16]{0:T(128)S(1)} %add_rsqrt_fusion.2, f32[16]{0:T(128)S(1)} %broadcast_multiply_fusion), kind=kLoop, calls=%fused_computation.16 | loop fusion | flops 393216 | bytes 295040 | tf_op jit(solution)/shard_map/convert_element_type | solution.py:21
  11.3 0.0 all-gather.2.cloned.1.call-update
  11.3 0.0 copy-start.3
  11.3 0.0 copy-start.2
  11.3 0.0 all-reduce.2.cloned.1.call-start
  11.4 4.7 %copy.10 = bf16[1,4096,3,128]{1,3,2,0:T(8,128)(2,1)} copy(bf16[1,4096,3,128]{3,1,2,0:T(8,128)(2,1)} %param.9) | data formatting | bytes 6291456 | tf_op args[2]
  16.7 0.0 copy-done.3
  16.7 0.0 copy-done.2
  16.8 37.5 %all-gather.2.cloned.1.call-done = bf16[128,4096]{1,0:T(8,128)(2,1)} async-done(((bf16[16,4096]{1,0:T(8,128)(2,1)}), bf16[128,4096]{1,0:T(8,128)(2,1)}) %all-gather.2.cloned.1.call-update) | async-done | bytes 1048592 | tf_op jit(solution)/shard_map/all_gather | solution.py:37
  54.3 3.2 %fusion = f32[128,3,128]{0,2,1:T(8,128)S(1)} fusion(bf16[1,4096,3,128]{1,3,2,0:T(8,128)(2,1)} %copy.10, bf16[128,4096]{1,0:T(8,128)(2,1)} %all-gather.2.cloned.1.call-done), kind=kOutput, calls=%fused_computation.1 | convolution fusion | flops 402653184 | bytes 4390912 | tf_op jit(solution)/shard_map/dot_general | solution.py:36
  57.5 0.0 copy-start.1
  57.6 0.1 multiply_convert_fusion
  57.7 0.1 copy.11
  57.8 0.1 copy.12
  57.9 0.2 dynamic_update_slice.6
  58.1 0.4 fusion.22
  58.5 0.2 fusion.13
  58.7 0.2 dynamic_update_slice.7
  58.9 0.0 copy-done
  58.9 1.6 %convolution_convert_fusion = bf16[128,4096]{1,0:T(8,128)(2,1)} fusion(bf16[256,128]{1,0:T(8,128)(2,1)S(1)} %dynamic_update_slice.7, bf16[1,128,4096]{2,1,0:T(8,128)(2,1)S(1)} %copy-done, f32[128,256]{1,0:T(8,128)S(1)} %get-tuple-element.15, f32[128]{0:T(128)S(1)} %fusion.13, f32[128]{0:T(128)S(1)} %get-tuple-element.14), kind=kOutput, calls=%fused_computation | convolution fusion | flops 143245312 | bytes 2294784 | tf_op jit(solution)/shard_map/dot_general | solution.py:59
  60.6 0.0 all-reduce.2.cloned.1.call-update
  60.6 76.9 %all-reduce.2.cloned.1.call-done = bf16[128,4096]{1,0:T(8,128)(2,1)} async-done(((bf16[128,4096]{1,0:T(8,128)(2,1)}), bf16[128,4096]{1,0:T(8,128)(2,1)}) %all-reduce.2.cloned.1.call-update) | async-done | bytes 1048592 | tf_op jit(solution)/shard_map/psum | solution.py:60
  137.5 0.0 copy-done.1
  137.5 0.9 fusion.12
  138.5 0.1 collective-permute-start
  138.5 4.4 %collective-permute-done = bf16[16,4096]{1,0:T(8,128)(2,1)S(1)} collective-permute-done((bf16[16,4096]{1,0:T(8,128)(2,1)S(1)}, bf16[16,4096]{1,0:T(8,128)(2,1)S(1)}, u32[]{:S(2)}, u32[]{:S(2)}) %collective-permute-start) | collective-permute-done | bytes 131104 | tf_op jit(solution)/shard_map/ppermute | solution.py:12
  142.9 0.7 copy.18
  (7 shorter events, 0.1 us)
Async XLA Ops:
  6.5 52.4 %copy-start = (bf16[1,128,4096]{2,1,0:T(8,128)(2,1)S(1)}, bf16[1,128,4096]{2,1,0:T(8,128)(2,1)}, u32[]{:S(2)}) copy-start(bf16[1,128,4096]{2,1,0:T(8,128)(2,1)} %param.11) | copy-start | bytes 3145732
  6.5 47.8 %all-gather.2.cloned.1.call-start = ((), (), s32[]{:S(2)}) async-start(), calls=%async_computation | async-start | bytes 1179648 | tf_op jit(solution)/shard_map/all_gather | solution.py:37
  11.3 5.4 %copy-start.3 = (f32[1,2,128]{2,1,0:T(2,128)S(1)}, f32[1,2,128]{2,1,0:T(2,128)}, u32[]{:S(2)}) copy-start(f32[1,2,128]{2,1,0:T(2,128)} %param.10) | copy-start | bytes 3076
  11.3 5.4 %copy-start.2 = (bf16[1,2,256,128]{3,2,1,0:T(8,128)(2,1)S(1)}, bf16[1,2,256,128]{3,2,1,0:T(8,128)(2,1)}, u32[]{:S(2)}) copy-start(bf16[1,2,256,128]{3,2,1,0:T(8,128)(2,1)} %param.12) | copy-start | bytes 393220
  11.3 126.2 %all-reduce.2.cloned.1.call-start = ((), (), s32[]{:S(2)}) async-start(), calls=%async_computation.1 | async-start | bytes 2097152 | tf_op jit(solution)/shard_map/psum | solution.py:60
  57.5 80.0 %copy-start.1 = (bf16[1,16,4096]{2,1,0:T(8,128)(2,1)S(1)}, bf16[1,16,4096]{2,1,0:T(8,128)(2,1)}, u32[]{:S(2)}) copy-start(bf16[1,16,4096]{2,1,0:T(8,128)(2,1)} %param.7) | copy-start | bytes 393220
  138.5 4.4 %collective-permute-start = (bf16[16,4096]{1,0:T(8,128)(2,1)S(1)}, bf16[16,4096]{1,0:T(8,128)(2,1)S(1)}, u32[]{:S(2)}, u32[]{:S(2)}) collective-permute-start(bf16[16,4096]{1,0:T(8,128)(2,1)S(1)} %fusion.12), channel_id=1, source_target_pairs={{24,0},{0,8},{8,16},{16,24},{25,1},{1,9},{9,17},{17,25},{26,2},{2,... | collective-permute-start | bytes 393224 | tf_op jit(solution)/shard_map/ppermute | solution.py:12
Sparse Core Ops, SparseCore 0:
  11.4 42.8 all-gather.1
  60.7 76.7 all-reduce.1
where the time goes:
time: 151 us; the launch traced here: 150 us
  waiting for transfers between devices  119 us (79%)
  between operations  14.2 us (9%)
  local copies, waits for them, and re-layouts  6.07 us (4%)
  other arithmetic  5.98 us (4%)
  matrix products  5.18 us (3%)
    psum x1, waiting for transfers between devices, per_device(): lax.psum(partial_value.astype(jnp.bfloat16), 'seq').astype(jnp.float32)  76.9 us
    all_gather x1, waiting for transfers between devices, per_device(): lax.all_gather(mixed, 'seq', axis=0, tiled=True)  37.5 us
    unnamed x10, local copies, waits for them, and re-layouts  5.37 us
    ppermute x1, waiting for transfers between devices, from_behind(): return lax.ppermute(block, axis, route)  4.38 us
    dot_general x1, matrix products, per_device(): jnp.dot(lax.all_gather(mixed, 'seq', axis=0, tiled=True), projection, pre...  3.19 us
  transfers between devices with their start and end apart: 3, of which 3 were waited for; matrix products, arithmetic and copies ran while one was open for 3% of the time, Pallas kernels for 0%

commit v1 on v0

v1 whole, which is shorter than its diff:
```python
import functools
import math

import jax
import jax.numpy as jnp
from jax import lax
from jax.experimental import pallas as pl
from jax.experimental.pallas import tpu as pltpu
from jax.sharding import PartitionSpec as P


def route(block, distance, sections_on=0):
    sections, count = lax.axis_size("section"), lax.axis_size("seq")
    pairs = [
        (s * count + i, (s + sections_on) % sections * count + (i ^ distance))
        for s in range(sections)
        for i in range(count)
    ]
    return lax.ppermute(block, ("section", "seq"), pairs)


def parents_of(count):
    tree = {r: r & (r - 1) for r in range(1, count)}
    if count == 8:
        tree[7] = 0
    return tree


def gather(block, count):
    tree = parents_of(count)
    blocks = {0: block}
    while len(blocks) < count:
        for r, parent in tree.items():
            if r not in blocks and parent in blocks:
                blocks[r] = route(blocks[parent], r ^ parent)
    return [blocks[r] for r in range(count)]


def layer_kernel(count, start_ref, mod_ref, gain_ref, qkv_ref, stale_ref, out_w_ref, *refs):
    blocks, outs, mixed = refs[:count], refs[count : 2 * count], refs[2 * count]
    rows, width = blocks[0].shape
    head = qkv_ref.shape[2]
    clip = stale_ref.shape[1]
    patch = rows * count
    shift, scale = mod_ref[0:1, :], 1.0 + mod_ref[1:2, :]
    for i, block in enumerate(blocks):
        values = block[...].astype(jnp.float32)
        centred = values - jnp.mean(values, axis=-1, keepdims=True)
        spread = jnp.mean(centred * centred, axis=-1, keepdims=True)
        normed = centred * lax.rsqrt(spread + 1e-06)
        mixed[i * rows : (i + 1) * rows, :] = (normed * scale + shift).astype(jnp.bfloat16)

    def project(j):
        return jnp.dot(mixed[...], qkv_ref[j], preferred_element_type=jnp.float32)

    def head_norm(values, gains):
        return values * lax.rsqrt(jnp.mean(values * values, axis=-1, keepdims=True) + 1e-06) * gains

    queries = head_norm(project(0), gain_ref[0:1, :]).astype(jnp.bfloat16)
    keys_new = head_norm(project(1), gain_ref[1:2, :]).astype(jnp.bfloat16)
    values_new = project(2).astype(jnp.bfloat16)

    def scores_of(keys):
        raw = lax.dot_general(queries, keys, (((1,), (1,)), ((), ())), preferred_element_type=jnp.float32)
        return raw * (1.0 / math.sqrt(head))

    start = start_ref[0]
    clip_row = lax.broadcasted_iota(jnp.int32, (patch, clip), 1)
    replaced = (clip_row >= start) & (clip_row < start + patch)
    scores_new = scores_of(keys_new)
    scores_old = jnp.where(replaced, -jnp.inf, scores_of(stale_ref[0]))
    highest = jnp.maximum(
        jnp.max(scores_new, axis=-1, keepdims=True), jnp.max(scores_old, axis=-1, keepdims=True)
    )
    raised_new = jnp.exp(scores_new - highest)
    raised_old = jnp.exp(scores_old - highest)
    summed = jnp.sum(raised_new, axis=-1, keepdims=True) + jnp.sum(raised_old, axis=-1, keepdims=True)
    probs_new = (raised_new / summed).astype(jnp.bfloat16)
    probs_old = (raised_old / summed).astype(jnp.bfloat16)
    attended = jnp.dot(probs_new, values_new, preferred_element_type=jnp.float32) + jnp.dot(
        probs_old, stale_ref[1], preferred_element_type=jnp.float32
    )
    attended = attended.astype(jnp.bfloat16)
    step = 512
    for at in range(0, width, step):
        columns = slice(at, at + step)
        part = jnp.dot(attended, out_w_ref[:, columns], preferred_element_type=jnp.float32)
        part = part * mod_ref[2:3, columns]
        for r, out in enumerate(outs):
            piece = part[r * rows : (r + 1) * rows]
            if r == 0:
                piece = piece + blocks[0][:, columns].astype(jnp.float32)
            out[:, columns] = piece.astype(jnp.bfloat16)


def add_up(*blocks):
    total = blocks[0].astype(jnp.float32)
    for block in blocks[1:]:
        total = total + block.astype(jnp.float32)
    return total.astype(jnp.bfloat16)


def reduce_scatter(parts, count):
    tree = parents_of(count)
    arrived = {r: [] for r in range(count)}
    waiting = set(tree)
    while waiting:
        ready = [r for r in waiting if not any(tree[c] == r for c in waiting)]
        moved = [(r, route(add_up(parts[r], *arrived[r]), r ^ tree[r], int(tree[r] == 0))) for r in ready]
        for r, block in moved:
            arrived[tree[r]].append(block)
            waiting.discard(r)
    own = route(parts[0], 0, 1)
    return add_up(own, *arrived[0])


def per_device(hidden, modulation, w_qkv, qk_gain, w_out, stale_kv, patch_start):
    count = lax.axis_size("seq")
    tokens_in = hidden[0]
    rows, width = tokens_in.shape
    blocks = gather(tokens_in, count)
    vmem = pl.BlockSpec(memory_space=pltpu.VMEM)
    parts = pl.pallas_call(
        functools.partial(layer_kernel, count),
        out_shape=[jax.ShapeDtypeStruct((rows, width), jnp.bfloat16)] * count,
        in_specs=[pl.BlockSpec(memory_space=pltpu.SMEM)] + [vmem] * (5 + count),
        out_specs=[vmem] * count,
        scratch_shapes=[pltpu.VMEM((rows * count, width), jnp.bfloat16)],
        compiler_params=pltpu.CompilerParams(vmem_limit_bytes=40 * 2**20),
        name="layer",
    )(
        patch_start,
        modulation[0],
        qk_gain[0],
        w_qkv[0].transpose(1, 0, 2),
        stale_kv[0],
        w_out[0],
        *blocks,
    )
    return reduce_scatter(parts, count)[None]


def solution(mesh):
    in_specs = (
        P("section", "seq", None),
        P("section", None, None),
        P("section", None, None, "seq"),
        P("section", None, None),
        P("section", "seq", None),
        P("section", None, None, "seq"),
        P("section"),
    )
    out_specs = P("section", "seq", None)
    return jax.shard_map(
        per_device, mesh=mesh, in_specs=in_specs, out_specs=out_specs, check_vma=False
    )
```

time: 151 us -> 54.3 us (0.36)
  waiting for transfers between devices: 119 us -> 22.1 us
  starting transfers between devices: 0.1 us -> 21 us
  between operations: 14.2 us -> 0.71 us
  matrix products: 5.18 us -> 0 us
  other arithmetic: 5.98 us -> 0.82 us
  Pallas kernels: 0 us -> 2.29 us
    psum x1 -> x0, waiting for transfers between devices: 76.9 us -> none  [per_device(): lax.psum(partial_value.astype(jnp.bfloat16), 'seq').astype(jnp.float32)]
    all_gather x1 -> x0, waiting for transfers between devices: 37.5 us -> none  [per_device(): lax.all_gather(mixed, 'seq', axis=0, tiled=True)]
    ppermute x1 -> x15, starting transfers between devices: 0.06 us -> 21 us  [route(): return lax.ppermute(block, ('section', 'seq'), pairs)]
    ppermute x1 -> x15, waiting for transfers between devices: 4.38 us -> 22.1 us  [route(): return lax.ppermute(block, ('section', 'seq'), pairs)]
    dot_general x3 -> x0, matrix products: 5.18 us -> none  [the longest x1 3.19 us: per_device(): jnp.dot(lax.all_gather(mixed, 'seq', axis=0, tiled=True), projection, pre...]
    convert_element_type x3 -> x2, other arithmetic: 2.71 us -> 0.08 us  [add_up(): return total.astype(jnp.bfloat16)]
    reduce_sum x4 -> x0, other arithmetic: 2.39 us -> none  [the longest x1 1.12 us: modulate(): spread = jnp.mean(centred * centred, axis=-1, keepdims=True)]
    pallas_call x0 -> x1, Pallas kernels: none -> 2.29 us  [per_device(): pl.pallas_call(functools.partial(layer_kernel, count), out_shape=[jax.Sha...]
  transfers between devices with their start and end apart: 3 -> 15, of which waited for: 3 -> 6; matrix products, arithmetic and copies ran while one was open for 3% -> 2% of each run, Pallas kernels for 0% -> 0%
where the time goes in v1:
time: 54.3 us; the launch traced here: 53.3 us
  waiting for transfers between devices  22.1 us (41%)
  starting transfers between devices  21 us (39%)
  local copies, waits for them, and re-layouts  6.43 us (12%)
  Pallas kernels  2.29 us (4%)
  other arithmetic  0.82 us (2%)
  between operations  0.71 us (1%)
    ppermute x15, waiting for transfers between devices, route(): return lax.ppermute(block, ('section', 'seq'), pairs)  22.1 us
    ppermute x15, starting transfers between devices, route(): return lax.ppermute(block, ('section', 'seq'), pairs)  21 us
    unnamed x11, local copies, waits for them, and re-layouts  6.43 us
    pallas_call x1, Pallas kernels, per_device(): pl.pallas_call(functools.partial(layer_kernel, count), out_shape=[jax.Sha...  2.29 us
  transfers between devices with their start and end apart: 15, of which 6 were waited for; matrix products, arithmetic and copies ran while one was open for 2% of the time, Pallas kernels for 0%

profile of v1, /device:TPU:0, one launch (start us, length us, event | category | flops | bytes accessed | tf_op | source)
XLA Modules:
  0.0 53.3 jit_solution(26354435000345935)
XLA Ops:
  0.0 4.0 %collective-permute-start.3 = (bf16[16,4096]{1,0:T(8,128)(2,1)}, bf16[16,4096]{1,0:T(8,128)(2,1)S(1)}, u32[]{:S(2)}, u32[]{:S(2)}) collective-permute-start(bf16[16,4096]{1,0:T(8,128)(2,1)} %bitcast.16), channel_id=1, source_target_pairs={{0,4},{1,5},{2,6},{3,7},{4,0},{5,1},{6,2},{7,3},{8,12},{9,13},{10,... | collective-permute-start | bytes 393224 | tf_op jit(solution)/shard_map/ppermute | solution.py:19
  4.0 1.6 %collective-permute-start.1 = (bf16[16,4096]{1,0:T(8,128)(2,1)}, bf16[16,4096]{1,0:T(8,128)(2,1)S(1)}, u32[]{:S(2)}, u32[]{:S(2)}) collective-permute-start(bf16[16,4096]{1,0:T(8,128)(2,1)} %bitcast.17), channel_id=1, source_target_pairs={{0,2},{1,3},{2,0},{3,1},{4,6},{5,7},{6,4},{7,5},{8,10},{9,11},{10,... | collective-permute-start | bytes 393224 | tf_op jit(solution)/shard_map/ppermute | solution.py:19
  5.6 1.2 %collective-permute-start.6 = (bf16[16,4096]{1,0:T(8,128)(2,1)}, bf16[16,4096]{1,0:T(8,128)(2,1)S(1)}, u32[]{:S(2)}, u32[]{:S(2)}) collective-permute-start(bf16[16,4096]{1,0:T(8,128)(2,1)} %bitcast.18), channel_id=1, source_target_pairs={{0,7},{1,6},{2,5},{3,4},{4,3},{5,2},{6,1},{7,0},{8,15},{9,14},{10,... | collective-permute-start | bytes 393224 | tf_op jit(solution)/shard_map/ppermute | solution.py:19
  6.8 0.3 collective-permute-start
  7.1 5.1 %collective-permute-done.3.refs_4_ = bf16[16,4096]{1,0:T(8,128)(2,1)S(1)} collective-permute-done((bf16[16,4096]{1,0:T(8,128)(2,1)}, bf16[16,4096]{1,0:T(8,128)(2,1)S(1)}, u32[]{:S(2)}, u32[]{:S(2)}) %collective-permute-start.3) | collective-permute-done | bytes 131104 | tf_op jit(solution)/shard_map/ppermute | solution.py:19
  12.2 0.2 collective-permute-start.5
  12.4 2.0 %collective-permute-start.4 = (bf16[16,4096]{1,0:T(8,128)(2,1)S(1)}, bf16[16,4096]{1,0:T(8,128)(2,1)S(1)}, u32[]{:S(2)}, u32[]{:S(2)}) collective-permute-start(bf16[16,4096]{1,0:T(8,128)(2,1)S(1)} %collective-permute-done.3.refs_4_), channel_id=1, source_target_pairs={{0,1},{1,0},{2,3},{3,2},{4,5},{5,4},{6,7},{7,6},{8,9},{9,8},{10,11... | collective-permute-start | bytes 393224 | tf_op jit(solution)/shard_map/ppermute | solution.py:19
  14.4 0.0 collective-permute-done.1.refs_2_
  14.4 0.1 collective-permute-start.2
  15.1 0.8 %copy.10 = f32[1,3,4096]{2,1,0:T(4,128)S(1)} copy(f32[1,3,4096]{2,0,1:T(1,128)} %param.8) | data formatting | bytes 98304
  15.9 0.0 collective-permute-done.6.refs_7_
  15.9 0.0 collective-permute-done.refs_1_
  16.0 1.4 %collective-permute-done.5.refs_6_ = bf16[16,4096]{1,0:T(8,128)(2,1)S(1)} collective-permute-done((bf16[16,4096]{1,0:T(8,128)(2,1)S(1)}, bf16[16,4096]{1,0:T(8,128)(2,1)S(1)}, u32[]{:S(2)}, u32[]{:S(2)}) %collective-permute-start.5) | collective-permute-done | bytes 131104 | tf_op jit(solution)/shard_map/ppermute | solution.py:19
  17.3 1.4 %collective-permute-done.4.refs_5_ = bf16[16,4096]{1,0:T(8,128)(2,1)S(1)} collective-permute-done((bf16[16,4096]{1,0:T(8,128)(2,1)S(1)}, bf16[16,4096]{1,0:T(8,128)(2,1)S(1)}, u32[]{:S(2)}, u32[]{:S(2)}) %collective-permute-start.4) | collective-permute-done | bytes 131104 | tf_op jit(solution)/shard_map/ppermute | solution.py:19
  18.8 2.5 %collective-permute-done.2.refs_3_ = bf16[16,4096]{1,0:T(8,128)(2,1)S(1)} collective-permute-done((bf16[16,4096]{1,0:T(8,128)(2,1)S(1)}, bf16[16,4096]{1,0:T(8,128)(2,1)S(1)}, u32[]{:S(2)}, u32[]{:S(2)}) %collective-permute-start.2) | collective-permute-done | bytes 131104 | tf_op jit(solution)/shard_map/ppermute | solution.py:19
  21.2 0.0 copy-start
  21.2 1.9 %copy-done = bf16[1,4096,3,128]{3,1,2,0:T(8,128)(2,1)S(1)} copy-done((bf16[1,4096,3,128]{3,1,2,0:T(8,128)(2,1)S(1)}, bf16[1,4096,3,128]{3,1,2,0:T(8,128)(2,1)}, u32[]{:S(2)}) %copy-start) | copy-done | bytes 3145752
  23.1 0.0 copy-start.1
  23.1 1.2 %copy-done.1 = bf16[1,128,4096]{2,1,0:T(8,128)(2,1)S(1)} copy-done((bf16[1,128,4096]{2,1,0:T(8,128)(2,1)S(1)}, bf16[1,128,4096]{2,1,0:T(8,128)(2,1)}, u32[]{:S(2)}) %copy-start.1) | copy-done | bytes 1048600
  24.4 0.0 copy-start.2
  24.4 0.9 %copy-done.2 = bf16[1,2,256,128]{3,2,1,0:T(8,128)(2,1)S(1)} copy-done((bf16[1,2,256,128]{3,2,1,0:T(8,128)(2,1)S(1)}, bf16[1,2,256,128]{3,2,1,0:T(8,128)(2,1)}, u32[]{:S(2)}) %copy-start.2) | copy-done | bytes 131096
  25.3 0.0 copy-start.3
  25.3 0.9 %copy-done.3 = bf16[1,16,4096]{2,1,0:T(8,128)(2,1)S(1)} copy-done((bf16[1,16,4096]{2,1,0:T(8,128)(2,1)S(1)}, bf16[1,16,4096]{2,1,0:T(8,128)(2,1)}, u32[]{:S(2)}) %copy-start.3) | copy-done | bytes 131096
  26.2 0.0 copy-start.4
  26.2 0.7 %copy-done.4 = f32[1,2,128]{2,1,0:T(2,128)S(1)} copy-done((f32[1,2,128]{2,1,0:T(2,128)S(1)}, f32[1,2,128]{2,1,0:T(2,128)}, u32[]{:S(2)}) %copy-start.4) | copy-done | bytes 1048
  26.8 2.3 %layer.1 = (bf16[16,4096]{1,0:T(8,128)(2,1)S(1)}, bf16[16,4096]{1,0:T(8,128)(2,1)S(1)}, bf16[16,4096]{1,0:T(8,128)(2,1)S(1)}, bf16[16,4096]{1,0:T(8,128)(2,1)S(1...) custom-call(s32[1]{0:T(128)S(6)} %copy.11.start_ref, ...), custom_call_target="tpu_custom_call" | custom-call | tf_op jit(solution)/shard_map/layer/pallas_call | solution.py:123
  29.1 0.6 %collective-permute-start.10 = (bf16[16,4096]{1,0:T(8,128)(2,1)S(1)}, bf16[16,4096]{1,0:T(8,128)(2,1)S(1)}, u32[]{:S(2)}, u32[]{:S(2)}) collective-permute-start(bf16[16,4096]{1,0:T(8,128)(2,1)S(1)} %get-tuple-element.17), channel_id=1, source_target_pairs={{0,1},{1,0},{2,3},{3,2},{4,5},{5,4},{6,7},{7,6},{8,9},{9,8},{10,11... | collective-permute-start | bytes 393224 | tf_op jit(solution)/shard_map/ppermute | solution.py:19
  29.7 0.0 collective-permute-start.7
  29.7 2.7 %collective-permute-start.8 = (bf16[16,4096]{1,0:T(8,128)(2,1)S(1)}, bf16[16,4096]{1,0:T(8,128)(2,1)S(1)}, u32[]{:S(2)}, u32[]{:S(2)}) collective-permute-start(bf16[16,4096]{1,0:T(8,128)(2,1)S(1)} %get-tuple-element.14), channel_id=1, source_target_pairs={{0,9},{1,8},{2,11},{3,10},{4,13},{5,12},{6,15},{7,14},{8,17},{9,16... | collective-permute-start | bytes 393224 | tf_op jit(solution)/shard_map/ppermute | solution.py:19
  32.4 2.5 %collective-permute-start.9 = (bf16[16,4096]{1,0:T(8,128)(2,1)S(1)}, bf16[16,4096]{1,0:T(8,128)(2,1)S(1)}, u32[]{:S(2)}, u32[]{:S(2)}) collective-permute-start(bf16[16,4096]{1,0:T(8,128)(2,1)S(1)} %get-tuple-element.15), channel_id=1, source_target_pairs={{0,15},{1,14},{2,13},{3,12},{4,11},{5,10},{6,9},{7,8},{8,23},{9,22... | collective-permute-start | bytes 393224 | tf_op jit(solution)/shard_map/ppermute | solution.py:19
  35.0 1.0 %collective-permute-start.12 = (bf16[16,4096]{1,0:T(8,128)(2,1)S(1)}, bf16[16,4096]{1,0:T(8,128)(2,1)S(1)}, u32[]{:S(2)}, u32[]{:S(2)}) collective-permute-start(bf16[16,4096]{1,0:T(8,128)(2,1)S(1)} %get-tuple-element.19), channel_id=1, source_target_pairs={{0,1},{1,0},{2,3},{3,2},{4,5},{5,4},{6,7},{7,6},{8,9},{9,8},{10,11... | collective-permute-start | bytes 393224 | tf_op jit(solution)/shard_map/ppermute | solution.py:19
  36.0 0.0 collective-permute-done.10
  36.0 2.1 %collective-permute-start.13 = (bf16[16,4096]{1,0:T(8,128)(2,1)S(1)}, bf16[16,4096]{1,0:T(8,128)(2,1)S(1)}, u32[]{:S(2)}, u32[]{:S(2)}) collective-permute-start(bf16[16,4096]{1,0:T(8,128)(2,1)S(1)} %get-tuple-element.20), channel_id=1, source_target_pairs={{0,2},{1,3},{2,0},{3,1},{4,6},{5,7},{6,4},{7,5},{8,10},{9,11},{10,... | collective-permute-start | bytes 393224 | tf_op jit(solution)/shard_map/ppermute | solution.py:19
  38.1 5.7 %collective-permute-done.12 = bf16[16,4096]{1,0:T(8,128)(2,1)S(1)} collective-permute-done((bf16[16,4096]{1,0:T(8,128)(2,1)S(1)}, bf16[16,4096]{1,0:T(8,128)(2,1)S(1)}, u32[]{:S(2)}, u32[]{:S(2)}) %collective-permute-start.12) | collective-permute-done | bytes 131104 | tf_op jit(solution)/shard_map/ppermute | solution.py:19
  43.8 0.0 collective-permute-start.11
  43.9 0.0 collective-permute-done.13
  43.9 0.1 add_convert_fusion.1
  43.9 2.6 %collective-permute-start.14 = (bf16[16,4096]{1,0:T(8,128)(2,1)S(1)}, bf16[16,4096]{1,0:T(8,128)(2,1)S(1)}, u32[]{:S(2)}, u32[]{:S(2)}) collective-permute-start(bf16[16,4096]{1,0:T(8,128)(2,1)S(1)} %add_convert_fusion.1), channel_id=1, source_target_pairs={{0,12},{1,13},{2,14},{3,15},{4,8},{5,9},{6,10},{7,11},{8,20},{9,21... | collective-permute-start | bytes 393224 | tf_op jit(solution)/shard_map/ppermute | solution.py:19
  46.6 0.0 collective-permute-done.7
  46.6 0.0 collective-permute-done.8
  46.6 0.0 collective-permute-done.9
  46.6 6.0 %collective-permute-done.11 = bf16[16,4096]{1,0:T(8,128)(2,1)S(1)} collective-permute-done((bf16[16,4096]{1,0:T(8,128)(2,1)S(1)}, bf16[16,4096]{1,0:T(8,128)(2,1)S(1)}, u32[]{:S(2)}, u32[]{:S(2)}) %collective-permute-start.11) | collective-permute-done | bytes 131104 | tf_op jit(solution)/shard_map/ppermute | solution.py:19
  52.6 0.0 collective-permute-done.14
  52.6 0.7 %fusion = bf16[1,16,4096]{2,1,0:T(8,128)(2,1)} fusion(bf16[16,4096]{1,0:T(8,128)(2,1)S(1)} %collective-permute-done.14, bf16[16,4096]{1,0:T(8,128)(2,1)S(1)} %collective-permute-done.11, bf16[16,4096]{1,0:T(8,128)(2,1)S(1)} %collective-permute-done.9, bf16[16,4096]{1,0:T(8,128)(2,1)S(1)} %collective-permute-done.8, bf16[16,4096]{1,0:T(8,128)(2,1)S(1)} %collective-permute-done.7), kind=kLoop, calls=%fused_computation.3 | loop fusion | flops 655360 | bytes 786432 | tf_op jit(solution)/shard_map/broadcast_in_dim | solution.py:140
  (1 shorter events, 0.0 us)
Async XLA Ops:
  0.0 12.2 %collective-permute-start.3 = (bf16[16,4096]{1,0:T(8,128)(2,1)}, bf16[16,4096]{1,0:T(8,128)(2,1)S(1)}, u32[]{:S(2)}, u32[]{:S(2)}) collective-permute-start(bf16[16,4096]{1,0:T(8,128)(2,1)} %bitcast.16), channel_id=1, source_target_pairs={{0,4},{1,5},{2,6},{3,7},{4,0},{5,1},{6,2},{7,3},{8,12},{9,13},{10,... | collective-permute-start | bytes 393224 | tf_op jit(solution)/shard_map/ppermute | solution.py:19
  4.0 10.3 %collective-permute-start.1 = (bf16[16,4096]{1,0:T(8,128)(2,1)}, bf16[16,4096]{1,0:T(8,128)(2,1)S(1)}, u32[]{:S(2)}, u32[]{:S(2)}) collective-permute-start(bf16[16,4096]{1,0:T(8,128)(2,1)} %bitcast.17), channel_id=1, source_target_pairs={{0,2},{1,3},{2,0},{3,1},{4,6},{5,7},{6,4},{7,5},{8,10},{9,11},{10,... | collective-permute-start | bytes 393224 | tf_op jit(solution)/shard_map/ppermute | solution.py:19
  5.6 10.3 %collective-permute-start.6 = (bf16[16,4096]{1,0:T(8,128)(2,1)}, bf16[16,4096]{1,0:T(8,128)(2,1)S(1)}, u32[]{:S(2)}, u32[]{:S(2)}) collective-permute-start(bf16[16,4096]{1,0:T(8,128)(2,1)} %bitcast.18), channel_id=1, source_target_pairs={{0,7},{1,6},{2,5},{3,4},{4,3},{5,2},{6,1},{7,0},{8,15},{9,14},{10,... | collective-permute-start | bytes 393224 | tf_op jit(solution)/shard_map/ppermute | solution.py:19
  6.8 9.2 %collective-permute-start = (bf16[16,4096]{1,0:T(8,128)(2,1)}, bf16[16,4096]{1,0:T(8,128)(2,1)S(1)}, u32[]{:S(2)}, u32[]{:S(2)}) collective-permute-start(bf16[16,4096]{1,0:T(8,128)(2,1)} %bitcast.19), channel_id=1, source_target_pairs={{0,1},{1,0},{2,3},{3,2},{4,5},{5,4},{6,7},{7,6},{8,9},{9,8},{10,11... | collective-permute-start | bytes 393224 | tf_op jit(solution)/shard_map/ppermute | solution.py:19
  12.2 5.1 %collective-permute-start.5 = (bf16[16,4096]{1,0:T(8,128)(2,1)S(1)}, bf16[16,4096]{1,0:T(8,128)(2,1)S(1)}, u32[]{:S(2)}, u32[]{:S(2)}) collective-permute-start(bf16[16,4096]{1,0:T(8,128)(2,1)S(1)} %collective-permute-done.3.refs_4_), channel_id=1, source_target_pairs={{0,2},{1,3},{2,0},{3,1},{4,6},{5,7},{6,4},{7,5},{8,10},{9,11},{10,... | collective-permute-start | bytes 393224 | tf_op jit(solution)/shard_map/ppermute | solution.py:19
  12.4 6.4 %collective-permute-start.4 = (bf16[16,4096]{1,0:T(8,128)(2,1)S(1)}, bf16[16,4096]{1,0:T(8,128)(2,1)S(1)}, u32[]{:S(2)}, u32[]{:S(2)}) collective-permute-start(bf16[16,4096]{1,0:T(8,128)(2,1)S(1)} %collective-permute-done.3.refs_4_), channel_id=1, source_target_pairs={{0,1},{1,0},{2,3},{3,2},{4,5},{5,4},{6,7},{7,6},{8,9},{9,8},{10,11... | collective-permute-start | bytes 393224 | tf_op jit(solution)/shard_map/ppermute | solution.py:19
  14.4 6.9 %collective-permute-start.2 = (bf16[16,4096]{1,0:T(8,128)(2,1)S(1)}, bf16[16,4096]{1,0:T(8,128)(2,1)S(1)}, u32[]{:S(2)}, u32[]{:S(2)}) collective-permute-start(bf16[16,4096]{1,0:T(8,128)(2,1)S(1)} %collective-permute-done.1.refs_2_), channel_id=1, source_target_pairs={{0,1},{1,0},{2,3},{3,2},{4,5},{5,4},{6,7},{7,6},{8,9},{9,8},{10,11... | collective-permute-start | bytes 393224 | tf_op jit(solution)/shard_map/ppermute | solution.py:19
  21.2 1.9 %copy-start = (bf16[1,4096,3,128]{3,1,2,0:T(8,128)(2,1)S(1)}, bf16[1,4096,3,128]{3,1,2,0:T(8,128)(2,1)}, u32[]{:S(2)}) copy-start(bf16[1,4096,3,128]{3,1,2,0:T(8,128)(2,1)} %param.9) | copy-start | bytes 9437188
  23.1 1.2 %copy-start.1 = (bf16[1,128,4096]{2,1,0:T(8,128)(2,1)S(1)}, bf16[1,128,4096]{2,1,0:T(8,128)(2,1)}, u32[]{:S(2)}) copy-start(bf16[1,128,4096]{2,1,0:T(8,128)(2,1)} %param.11) | copy-start | bytes 3145732
  24.4 0.9 %copy-start.2 = (bf16[1,2,256,128]{3,2,1,0:T(8,128)(2,1)S(1)}, bf16[1,2,256,128]{3,2,1,0:T(8,128)(2,1)}, u32[]{:S(2)}) copy-start(bf16[1,2,256,128]{3,2,1,0:T(8,128)(2,1)} %param.12) | copy-start | bytes 393220
  25.3 0.9 %copy-start.3 = (bf16[1,16,4096]{2,1,0:T(8,128)(2,1)S(1)}, bf16[1,16,4096]{2,1,0:T(8,128)(2,1)}, u32[]{:S(2)}) copy-start(bf16[1,16,4096]{2,1,0:T(8,128)(2,1)} %param.7) | copy-start | bytes 393220
  26.2 0.7 %copy-start.4 = (f32[1,2,128]{2,1,0:T(2,128)S(1)}, f32[1,2,128]{2,1,0:T(2,128)}, u32[]{:S(2)}) copy-start(f32[1,2,128]{2,1,0:T(2,128)} %param.10) | copy-start | bytes 3076
  29.1 6.8 %collective-permute-start.10 = (bf16[16,4096]{1,0:T(8,128)(2,1)S(1)}, bf16[16,4096]{1,0:T(8,128)(2,1)S(1)}, u32[]{:S(2)}, u32[]{:S(2)}) collective-permute-start(bf16[16,4096]{1,0:T(8,128)(2,1)S(1)} %get-tuple-element.17), channel_id=1, source_target_pairs={{0,1},{1,0},{2,3},{3,2},{4,5},{5,4},{6,7},{7,6},{8,9},{9,8},{10,11... | collective-permute-start | bytes 393224 | tf_op jit(solution)/shard_map/ppermute | solution.py:19
  29.7 16.8 %collective-permute-start.7 = (bf16[16,4096]{1,0:T(8,128)(2,1)S(1)}, bf16[16,4096]{1,0:T(8,128)(2,1)S(1)}, u32[]{:S(2)}, u32[]{:S(2)}) collective-permute-start(bf16[16,4096]{1,0:T(8,128)(2,1)S(1)} %get-tuple-element.13), channel_id=1, source_target_pairs={{0,8},{1,9},{2,10},{3,11},{4,12},{5,13},{6,14},{7,15},{8,16},{9,17... | collective-permute-start | bytes 393224 | tf_op jit(solution)/shard_map/ppermute | solution.py:19
  29.7 16.8 %collective-permute-start.8 = (bf16[16,4096]{1,0:T(8,128)(2,1)S(1)}, bf16[16,4096]{1,0:T(8,128)(2,1)S(1)}, u32[]{:S(2)}, u32[]{:S(2)}) collective-permute-start(bf16[16,4096]{1,0:T(8,128)(2,1)S(1)} %get-tuple-element.14), channel_id=1, source_target_pairs={{0,9},{1,8},{2,11},{3,10},{4,13},{5,12},{6,15},{7,14},{8,17},{9,16... | collective-permute-start | bytes 393224 | tf_op jit(solution)/shard_map/ppermute | solution.py:19
  32.4 14.1 %collective-permute-start.9 = (bf16[16,4096]{1,0:T(8,128)(2,1)S(1)}, bf16[16,4096]{1,0:T(8,128)(2,1)S(1)}, u32[]{:S(2)}, u32[]{:S(2)}) collective-permute-start(bf16[16,4096]{1,0:T(8,128)(2,1)S(1)} %get-tuple-element.15), channel_id=1, source_target_pairs={{0,15},{1,14},{2,13},{3,12},{4,11},{5,10},{6,9},{7,8},{8,23},{9,22... | collective-permute-start | bytes 393224 | tf_op jit(solution)/shard_map/ppermute | solution.py:19
  35.0 8.9 %collective-permute-start.12 = (bf16[16,4096]{1,0:T(8,128)(2,1)S(1)}, bf16[16,4096]{1,0:T(8,128)(2,1)S(1)}, u32[]{:S(2)}, u32[]{:S(2)}) collective-permute-start(bf16[16,4096]{1,0:T(8,128)(2,1)S(1)} %get-tuple-element.19), channel_id=1, source_target_pairs={{0,1},{1,0},{2,3},{3,2},{4,5},{5,4},{6,7},{7,6},{8,9},{9,8},{10,11... | collective-permute-start | bytes 393224 | tf_op jit(solution)/shard_map/ppermute | solution.py:19
  36.0 7.9 %collective-permute-start.13 = (bf16[16,4096]{1,0:T(8,128)(2,1)S(1)}, bf16[16,4096]{1,0:T(8,128)(2,1)S(1)}, u32[]{:S(2)}, u32[]{:S(2)}) collective-permute-start(bf16[16,4096]{1,0:T(8,128)(2,1)S(1)} %get-tuple-element.20), channel_id=1, source_target_pairs={{0,2},{1,3},{2,0},{3,1},{4,6},{5,7},{6,4},{7,5},{8,10},{9,11},{10,... | collective-permute-start | bytes 393224 | tf_op jit(solution)/shard_map/ppermute | solution.py:19
  43.8 8.7 %collective-permute-start.11 = (bf16[16,4096]{1,0:T(8,128)(2,1)S(1)}, bf16[16,4096]{1,0:T(8,128)(2,1)S(1)}, u32[]{:S(2)}, u32[]{:S(2)}) collective-permute-start(bf16[16,4096]{1,0:T(8,128)(2,1)S(1)} %add_convert_fusion.2), channel_id=1, source_target_pairs={{0,10},{1,11},{2,8},{3,9},{4,14},{5,15},{6,12},{7,13},{8,18},{9,19... | collective-permute-start | bytes 393224 | tf_op jit(solution)/shard_map/ppermute | solution.py:19
  43.9 8.6 %collective-permute-start.14 = (bf16[16,4096]{1,0:T(8,128)(2,1)S(1)}, bf16[16,4096]{1,0:T(8,128)(2,1)S(1)}, u32[]{:S(2)}, u32[]{:S(2)}) collective-permute-start(bf16[16,4096]{1,0:T(8,128)(2,1)S(1)} %add_convert_fusion.1), channel_id=1, source_target_pairs={{0,12},{1,13},{2,14},{3,15},{4,8},{5,9},{6,10},{7,11},{8,20},{9,21... | collective-permute-start | bytes 393224 | tf_op jit(solution)/shard_map/ppermute | solution.py:19

commit v2 on v1

--- a/solution.py
+++ b/solution.py
@@ -19,36 +19,65 @@
     return lax.ppermute(block, ("section", "seq"), pairs)
 
 
-def parents_of(count):
-    tree = {r: r & (r - 1) for r in range(1, count)}
+def plan(count):
     if count == 8:
-        tree[7] = 0
-    return tree
+        return [(1, 0), (2, 0), (3, 2), (4, 0), (5, 4), (6, 4), (7, 1)]
+    return [(r, r & (r - 1)) for r in range(1, count)]
+
+
+def plan_back(count):
+    if count == 8:
+        return [(5, 4), (6, 4), (4, 0), (3, 2), (2, 0), (7, 1), (1, 0), (0, 0)]
+    return [(r, r & (r - 1)) for r in reversed(range(count))]
 
 
 def gather(block, count):
-    tree = parents_of(count)
     blocks = {0: block}
-    while len(blocks) < count:
-        for r, parent in tree.items():
-            if r not in blocks and parent in blocks:
-                blocks[r] = route(blocks[parent], r ^ parent)
-    return [blocks[r] for r in range(count)]
+    for r, parent in plan(count):
+        blocks[r] = route(blocks[parent], r ^ parent)
+    return blocks
 
 
-def layer_kernel(count, start_ref, mod_ref, gain_ref, qkv_ref, stale_ref, out_w_ref, *refs):
-    blocks, outs, mixed = refs[:count], refs[count : 2 * count], refs[2 * count]
+def modulated(block, mod_ref):
+    values = block.astype(jnp.float32)
+    centred = values - jnp.mean(values, axis=-1, keepdims=True)
+    spread = jnp.mean(centred * centred, axis=-1, keepdims=True)
+    normed = centred * lax.rsqrt(spread + 1e-06)
+    return (normed * (1.0 + mod_ref[1]) + mod_ref[0]).astype(jnp.bfloat16)
+
+
+def early_kernel(mod_ref, *refs):
+    blocks, mixed_ref = refs[:-1], refs[-1]
+    rows = blocks[0].shape[0]
+    for i, block in enumerate(blocks):
+        mixed_ref[i * rows : (i + 1) * rows, :] = modulated(block[...], mod_ref)
+
+
+def early_rows(mod, blocks):
     rows, width = blocks[0].shape
+    vmem = pl.BlockSpec(memory_space=pltpu.VMEM)
+    return pl.pallas_call(
+        early_kernel,
+        out_shape=jax.ShapeDtypeStruct((rows * len(blocks), width), jnp.bfloat16),
+        in_specs=[vmem] * (1 + len(blocks)),
+        out_specs=vmem,
+        compiler_params=pltpu.CompilerParams(vmem_limit_bytes=12 * 2**20),
+        cost_estimate=pl.CostEstimate(flops=2 * 10**9, bytes_accessed=blocks[0].size * 64, transcendentals=0),
+        name="early",
+    )(mod, *blocks)
+
+
+def layer_kernel(count, start_ref, mod_ref, qkv_ref, stale_ref, out_w_ref, gain_ref, mixed_ref, own_ref, *refs):
+    late = len(refs) - 1 - count
+    blocks, outs, mixed = refs[:late], refs[late : late + count], refs[late + count]
+    rows, width = own_ref.shape
     head = qkv_ref.shape[2]
     clip = stale_ref.shape[1]
     patch = rows * count
-    shift, scale = mod_ref[0:1, :], 1.0 + mod_ref[1:2, :]
+    first = mixed_ref.shape[0]
+    mixed[:first, :] = mixed_ref[...]
     for i, block in enumerate(blocks):
-        values = block[...].astype(jnp.float32)
-        centred = values - jnp.mean(values, axis=-1, keepdims=True)
-        spread = jnp.mean(centred * centred, axis=-1, keepdims=True)
-        normed = centred * lax.rsqrt(spread + 1e-06)
-        mixed[i * rows : (i + 1) * rows, :] = (normed * scale + shift).astype(jnp.bfloat16)
+        mixed[first + i * rows : first + (i + 1) * rows, :] = modulated(block[...], mod_ref)
 
     def project(j):
         return jnp.dot(mixed[...], qkv_ref[j], preferred_element_type=jnp.float32)
@@ -85,11 +114,11 @@
     for at in range(0, width, step):
         columns = slice(at, at + step)
         part = jnp.dot(attended, out_w_ref[:, columns], preferred_element_type=jnp.float32)
-        part = part * mod_ref[2:3, columns]
+        part = part * mod_ref[2, :, columns]
         for r, out in enumerate(outs):
             piece = part[r * rows : (r + 1) * rows]
             if r == 0:
-                piece = piece + blocks[0][:, columns].astype(jnp.float32)
+                piece = piece + own_ref[:, columns].astype(jnp.float32)
             out[:, columns] = piece.astype(jnp.bfloat16)
 
 
@@ -101,17 +130,13 @@
 
 
 def reduce_scatter(parts, count):
-    tree = parents_of(count)
     arrived = {r: [] for r in range(count)}
-    waiting = set(tree)
-    while waiting:
-        ready = [r for r in waiting if not any(tree[c] == r for c in waiting)]
-        moved = [(r, route(add_up(parts[r], *arrived[r]), r ^ tree[r], int(tree[r] == 0))) for r in ready]
-        for r, block in moved:
-            arrived[tree[r]].append(block)
-            waiting.discard(r)
-    own = route(parts[0], 0, 1)
-    return add_up(own, *arrived[0])
+    for r, target in plan_back(count):
+        if r == 0:
+            arrived[0].append(route(parts[0], 0, 1))
+        else:
+            arrived[target].append(route(add_up(parts[r], *arrived[r]), r ^ target, int(target == 0)))
+    return add_up(*arrived[0])
 
 
 def per_device(hidden, modulation, w_qkv, qk_gain, w_out, stale_kv, patch_start):
@@ -119,25 +144,22 @@
     tokens_in = hidden[0]
     rows, width = tokens_in.shape
     blocks = gather(tokens_in, count)
+    order = [0, 2, 1, 3, 4, 5, 6, 7] if count == 8 else list(range(count))
+    mod, own = modulation.transpose(1, 0, 2), tokens_in
+    early = 2
+    mixed = early_rows(mod, [blocks[r] for r in order[:early]])
     vmem = pl.BlockSpec(memory_space=pltpu.VMEM)
+    late = [blocks[r] for r in order[early:]]
     parts = pl.pallas_call(
         functools.partial(layer_kernel, count),
         out_shape=[jax.ShapeDtypeStruct((rows, width), jnp.bfloat16)] * count,
-        in_specs=[pl.BlockSpec(memory_space=pltpu.SMEM)] + [vmem] * (5 + count),
+        in_specs=[pl.BlockSpec(memory_space=pltpu.SMEM)] + [vmem] * (7 + len(late)),
         out_specs=[vmem] * count,
         scratch_shapes=[pltpu.VMEM((rows * count, width), jnp.bfloat16)],
-        compiler_params=pltpu.CompilerParams(vmem_limit_bytes=40 * 2**20),
+        compiler_params=pltpu.CompilerParams(vmem_limit_bytes=(12 + count) * 2**20),
         name="layer",
-    )(
-        patch_start,
-        modulation[0],
-        qk_gain[0],
-        w_qkv[0].transpose(1, 0, 2),
-        stale_kv[0],
-        w_out[0],
-        *blocks,
-    )
-    return reduce_scatter(parts, count)[None]
+    )(patch_start, mod, w_qkv[0].transpose(1, 0, 2), stale_kv[0], w_out[0], qk_gain[0], mixed, own, *late)
+    return reduce_scatter(dict(zip(order, parts)), count)[None]
 
 
 def solution(mesh):

time: 54.3 us -> 41.6 us (0.77); the launches traced: 53.3 us -> 41.4 us
  waiting for transfers between devices: 22.1 us -> 12.4 us
  local copies, waits for them, and re-layouts: 6.43 us -> 1.72 us
  starting transfers between devices: 21 us -> 23.2 us
    ppermute x15, waiting for transfers between devices: 22.1 us -> 12.4 us  [route(): return lax.ppermute(block, ('section', 'seq'), pairs)]
    unnamed x11 -> x16, local copies, waits for them, and re-layouts: 6.43 us -> 1.72 us
    ppermute x15, starting transfers between devices: 21 us -> 23.2 us  [route(): return lax.ppermute(block, ('section', 'seq'), pairs)]
  transfers between devices with their start and end apart: 15 -> 15, of which waited for: 6 -> 5; matrix products, arithmetic and copies ran while one was open for 2% -> 0% of each run, Pallas kernels for 0% -> 1%
where the time goes in v2:
time: 41.6 us; the launch traced here: 41.4 us
  starting transfers between devices  23.2 us (56%)
  waiting for transfers between devices  12.4 us (30%)
  Pallas kernels  2.48 us (6%)
  local copies, waits for them, and re-layouts  1.72 us (4%)
  other arithmetic  0.84 us (2%)
  between operations  0.77 us (2%)
    ppermute x15, starting transfers between devices, route(): return lax.ppermute(block, ('section', 'seq'), pairs)  23.2 us
    ppermute x15, waiting for transfers between devices, route(): return lax.ppermute(block, ('section', 'seq'), pairs)  12.4 us
    pallas_call x1, Pallas kernels, per_device(): pl.pallas_call(functools.partial(layer_kernel, count), out_shape=[jax.Sha...  2.15 us
    unnamed x16, local copies, waits for them, and re-layouts  1.72 us
  transfers between devices with their start and end apart: 15, of which 5 were waited for; matrix products, arithmetic and copies ran while one was open for 0% of the time, Pallas kernels for 1%

profile of v2, /device:TPU:0, one launch (start us, length us, event | category | flops | bytes accessed | tf_op | source)
XLA Modules:
  0.0 41.4 jit_solution(14427945196267386458)
XLA Ops:
  0.0 4.0 %collective-permute-start.3 = (bf16[16,4096]{1,0:T(8,128)(2,1)}, bf16[16,4096]{1,0:T(8,128)(2,1)S(1)}, u32[]{:S(2)}, u32[]{:S(2)}) collective-permute-start(bf16[16,4096]{1,0:T(8,128)(2,1)} %bitcast.13), channel_id=1, source_target_pairs={{0,4},{1,5},{2,6},{3,7},{4,0},{5,1},{6,2},{7,3},{8,12},{9,13},{10,... | collective-permute-start | bytes 393224 | tf_op jit(solution)/shard_map/ppermute | solution.py:19
  4.0 1.5 %collective-permute-start.1 = (bf16[16,4096]{1,0:T(8,128)(2,1)}, bf16[16,4096]{1,0:T(8,128)(2,1)S(1)}, u32[]{:S(2)}, u32[]{:S(2)}) collective-permute-start(bf16[16,4096]{1,0:T(8,128)(2,1)} %bitcast.14), channel_id=1, source_target_pairs={{0,1},{1,0},{2,3},{3,2},{4,5},{5,4},{6,7},{7,6},{8,9},{9,8},{10,11... | collective-permute-start | bytes 393224 | tf_op jit(solution)/shard_map/ppermute | solution.py:19
  5.6 1.6 %collective-permute-start = (bf16[16,4096]{1,0:T(8,128)(2,1)}, bf16[16,4096]{1,0:T(8,128)(2,1)S(1)}, u32[]{:S(2)}, u32[]{:S(2)}) collective-permute-start(bf16[16,4096]{1,0:T(8,128)(2,1)} %bitcast.15), channel_id=1, source_target_pairs={{0,2},{1,3},{2,0},{3,1},{4,6},{5,7},{6,4},{7,5},{8,10},{9,11},{10,... | collective-permute-start | bytes 393224 | tf_op jit(solution)/shard_map/ppermute | solution.py:19
  7.8 2.9 %collective-permute-done.3.refs_2_ = bf16[16,4096]{1,0:T(8,128)(2,1)S(1)} collective-permute-done((bf16[16,4096]{1,0:T(8,128)(2,1)}, bf16[16,4096]{1,0:T(8,128)(2,1)S(1)}, u32[]{:S(2)}, u32[]{:S(2)}) %collective-permute-start.3) | collective-permute-done | bytes 131104 | tf_op jit(solution)/shard_map/ppermute | solution.py:19
  10.7 0.8 %collective-permute-start.5 = (bf16[16,4096]{1,0:T(8,128)(2,1)S(1)}, bf16[16,4096]{1,0:T(8,128)(2,1)S(1)}, u32[]{:S(2)}, u32[]{:S(2)}) collective-permute-start(bf16[16,4096]{1,0:T(8,128)(2,1)S(1)} %collective-permute-done.3.refs_2_), channel_id=1, source_target_pairs={{0,2},{1,3},{2,0},{3,1},{4,6},{5,7},{6,4},{7,5},{8,10},{9,11},{10,... | collective-permute-start | bytes 393224 | tf_op jit(solution)/shard_map/ppermute | solution.py:19
  11.4 1.5 %collective-permute-start.4 = (bf16[16,4096]{1,0:T(8,128)(2,1)S(1)}, bf16[16,4096]{1,0:T(8,128)(2,1)S(1)}, u32[]{:S(2)}, u32[]{:S(2)}) collective-permute-start(bf16[16,4096]{1,0:T(8,128)(2,1)S(1)} %collective-permute-done.3.refs_2_), channel_id=1, source_target_pairs={{0,1},{1,0},{2,3},{3,2},{4,5},{5,4},{6,7},{7,6},{8,9},{9,8},{10,11... | collective-permute-start | bytes 393224 | tf_op jit(solution)/shard_map/ppermute | solution.py:19
  12.9 0.0 collective-permute-done.1.refs_0_
  12.9 2.7 %collective-permute-start.6 = (bf16[16,4096]{1,0:T(8,128)(2,1)S(1)}, bf16[16,4096]{1,0:T(8,128)(2,1)S(1)}, u32[]{:S(2)}, u32[]{:S(2)}) collective-permute-start(bf16[16,4096]{1,0:T(8,128)(2,1)S(1)} %collective-permute-done.1.refs_0_), channel_id=1, source_target_pairs={{0,6},{1,7},{2,4},{3,5},{4,2},{5,3},{6,0},{7,1},{8,14},{9,15},{10,... | collective-permute-start | bytes 393224 | tf_op jit(solution)/shard_map/ppermute | solution.py:19
  15.6 0.0 collective-permute-done.refs_1_
  15.6 0.6 %collective-permute-start.2 = (bf16[16,4096]{1,0:T(8,128)(2,1)S(1)}, bf16[16,4096]{1,0:T(8,128)(2,1)S(1)}, u32[]{:S(2)}, u32[]{:S(2)}) collective-permute-start(bf16[16,4096]{1,0:T(8,128)(2,1)S(1)} %collective-permute-done.refs_1_), channel_id=1, source_target_pairs={{0,1},{1,0},{2,3},{3,2},{4,5},{5,4},{6,7},{7,6},{8,9},{9,8},{10,11... | collective-permute-start | bytes 393224 | tf_op jit(solution)/shard_map/ppermute | solution.py:19
  16.2 0.0 copy-start.3
  16.2 0.9 %copy-done.3 = bf16[1,16,4096]{2,1,0:T(8,128)(2,1)S(1)} copy-done((bf16[1,16,4096]{2,1,0:T(8,128)(2,1)S(1)}, bf16[1,16,4096]{2,1,0:T(8,128)(2,1)}, u32[]{:S(2)}) %copy-start.3) | copy-done | bytes 131096
  17.1 0.0 copy-start.5
  17.1 0.8 %copy-done.5 = f32[1,3,4096]{2,0,1:T(1,128)S(1)} copy-done((f32[1,3,4096]{2,0,1:T(1,128)S(1)}, f32[1,3,4096]{2,0,1:T(1,128)}, u32[]{:S(2)}) %copy-start.5) | copy-done | bytes 49176
  17.9 0.0 copy-start
  17.9 0.0 copy-start.1
  17.9 0.0 copy-start.2
  17.9 0.0 copy-start.4
  17.9 0.0 copy-start.6
  18.0 0.0 copy-start.7
  18.0 0.3 early.1.mixed_ref
  18.3 0.0 collective-permute-done.5.refs_4_
  18.3 0.0 collective-permute-done.4.refs_3_
  18.3 2.4 %collective-permute-done.6.refs_5_ = bf16[16,4096]{1,0:T(8,128)(2,1)S(1)} collective-permute-done((bf16[16,4096]{1,0:T(8,128)(2,1)S(1)}, bf16[16,4096]{1,0:T(8,128)(2,1)S(1)}, u32[]{:S(2)}, u32[]{:S(2)}) %collective-permute-start.6) | collective-permute-done | bytes 131104 | tf_op jit(solution)/shard_map/ppermute | solution.py:19
  20.7 0.0 collective-permute-done.2.refs_1_
  20.7 0.0 copy-done
  20.7 0.0 copy-done.1
  20.7 0.0 copy-done.2
  20.7 0.0 copy-done.4
  20.8 0.0 copy-done.6
  20.8 0.0 copy-done.7
  20.8 2.1 %layer.1 = (bf16[16,4096]{1,0:T(8,128)(2,1)S(1)}, bf16[16,4096]{1,0:T(8,128)(2,1)S(1)}, bf16[16,4096]{1,0:T(8,128)(2,1)S(1)}, bf16[16,4096]{1,0:T(8,128)(2,1)S(1...) custom-call(s32[1]{0:T(128)S(6)} %copy.8.start_ref, ...), custom_call_target="tpu_custom_call" | custom-call | tf_op jit(solution)/shard_map/layer/pallas_call | solution.py:153
  22.9 1.5 %collective-permute-start.7 = (bf16[16,4096]{1,0:T(8,128)(2,1)S(1)}, bf16[16,4096]{1,0:T(8,128)(2,1)S(1)}, u32[]{:S(2)}, u32[]{:S(2)}) collective-permute-start(bf16[16,4096]{1,0:T(8,128)(2,1)S(1)} %get-tuple-element.14), channel_id=1, source_target_pairs={{0,1},{1,0},{2,3},{3,2},{4,5},{5,4},{6,7},{7,6},{8,9},{9,8},{10,11... | collective-permute-start | bytes 393224 | tf_op jit(solution)/shard_map/ppermute | solution.py:19
  24.5 1.0 %collective-permute-start.8 = (bf16[16,4096]{1,0:T(8,128)(2,1)S(1)}, bf16[16,4096]{1,0:T(8,128)(2,1)S(1)}, u32[]{:S(2)}, u32[]{:S(2)}) collective-permute-start(bf16[16,4096]{1,0:T(8,128)(2,1)S(1)} %get-tuple-element.15), channel_id=1, source_target_pairs={{0,2},{1,3},{2,0},{3,1},{4,6},{5,7},{6,4},{7,5},{8,10},{9,11},{10,... | collective-permute-start | bytes 393224 | tf_op jit(solution)/shard_map/ppermute | solution.py:19
  25.5 1.5 %collective-permute-start.10 = (bf16[16,4096]{1,0:T(8,128)(2,1)S(1)}, bf16[16,4096]{1,0:T(8,128)(2,1)S(1)}, u32[]{:S(2)}, u32[]{:S(2)}) collective-permute-start(bf16[16,4096]{1,0:T(8,128)(2,1)S(1)} %get-tuple-element.17), channel_id=1, source_target_pairs={{0,1},{1,0},{2,3},{3,2},{4,5},{5,4},{6,7},{7,6},{8,9},{9,8},{10,11... | collective-permute-start | bytes 393224 | tf_op jit(solution)/shard_map/ppermute | solution.py:19
  27.0 2.7 %collective-permute-start.12 = (bf16[16,4096]{1,0:T(8,128)(2,1)S(1)}, bf16[16,4096]{1,0:T(8,128)(2,1)S(1)}, u32[]{:S(2)}, u32[]{:S(2)}) collective-permute-start(bf16[16,4096]{1,0:T(8,128)(2,1)S(1)} %get-tuple-element.19), channel_id=1, source_target_pairs={{0,6},{1,7},{2,4},{3,5},{4,2},{5,3},{6,0},{7,1},{8,14},{9,15},{10,... | collective-permute-start | bytes 393224 | tf_op jit(solution)/shard_map/ppermute | solution.py:19
  29.6 0.0 collective-permute-start.14
  29.6 0.0 collective-permute-done.7
  29.6 0.0 collective-permute-done.8
  29.6 0.1 add_convert_fusion.3
  29.7 0.1 collective-permute-start.9
  29.8 0.9 %collective-permute-done.10 = bf16[16,4096]{1,0:T(8,128)(2,1)S(1)} collective-permute-done((bf16[16,4096]{1,0:T(8,128)(2,1)S(1)}, bf16[16,4096]{1,0:T(8,128)(2,1)S(1)}, u32[]{:S(2)}, u32[]{:S(2)}) %collective-permute-start.10) | collective-permute-done | bytes 131104 | tf_op jit(solution)/shard_map/ppermute | solution.py:19
  30.7 2.7 %collective-permute-start.11 = (bf16[16,4096]{1,0:T(8,128)(2,1)S(1)}, bf16[16,4096]{1,0:T(8,128)(2,1)S(1)}, u32[]{:S(2)}, u32[]{:S(2)}) collective-permute-start(bf16[16,4096]{1,0:T(8,128)(2,1)S(1)} %add_convert_fusion.2), channel_id=1, source_target_pairs={{0,10},{1,11},{2,8},{3,9},{4,14},{5,15},{6,12},{7,13},{8,18},{9,19... | collective-permute-start | bytes 393224 | tf_op jit(solution)/shard_map/ppermute | solution.py:19
  33.4 0.5 %collective-permute-done.12 = bf16[16,4096]{1,0:T(8,128)(2,1)S(1)} collective-permute-done((bf16[16,4096]{1,0:T(8,128)(2,1)S(1)}, bf16[16,4096]{1,0:T(8,128)(2,1)S(1)}, u32[]{:S(2)}, u32[]{:S(2)}) %collective-permute-start.12) | collective-permute-done | bytes 131104 | tf_op jit(solution)/shard_map/ppermute | solution.py:19
  34.0 0.9 %collective-permute-start.13 = (bf16[16,4096]{1,0:T(8,128)(2,1)S(1)}, bf16[16,4096]{1,0:T(8,128)(2,1)S(1)}, u32[]{:S(2)}, u32[]{:S(2)}) collective-permute-start(bf16[16,4096]{1,0:T(8,128)(2,1)S(1)} %add_convert_fusion.1), channel_id=1, source_target_pairs={{0,9},{1,8},{2,11},{3,10},{4,13},{5,12},{6,15},{7,14},{8,17},{9,16... | collective-permute-start | bytes 393224 | tf_op jit(solution)/shard_map/ppermute | solution.py:19
  35.0 0.0 collective-permute-done.14
  35.0 5.7 %collective-permute-done.9 = bf16[16,4096]{1,0:T(8,128)(2,1)S(1)} collective-permute-done((bf16[16,4096]{1,0:T(8,128)(2,1)S(1)}, bf16[16,4096]{1,0:T(8,128)(2,1)S(1)}, u32[]{:S(2)}, u32[]{:S(2)}) %collective-permute-start.9) | collective-permute-done | bytes 131104 | tf_op jit(solution)/shard_map/ppermute | solution.py:19
  40.7 0.0 collective-permute-done.11
  40.7 0.0 collective-permute-done.13
  40.7 0.7 %fusion = bf16[1,16,4096]{2,1,0:T(8,128)(2,1)} fusion(bf16[16,4096]{1,0:T(8,128)(2,1)S(1)} %collective-permute-done.14, bf16[16,4096]{1,0:T(8,128)(2,1)S(1)} %collective-permute-done.13, bf16[16,4096]{1,0:T(8,128)(2,1)S(1)} %collective-permute-done.11, bf16[16,4096]{1,0:T(8,128)(2,1)S(1)} %collective-permute-done.9), kind=kLoop, calls=%fused_computation.4 | loop fusion | flops 524288 | bytes 655360 | tf_op jit(solution)/shard_map/broadcast_in_dim | solution.py:162
  (2 shorter events, 0.1 us)
Async XLA Ops:
  0.0 10.7 %collective-permute-start.3 = (bf16[16,4096]{1,0:T(8,128)(2,1)}, bf16[16,4096]{1,0:T(8,128)(2,1)S(1)}, u32[]{:S(2)}, u32[]{:S(2)}) collective-permute-start(bf16[16,4096]{1,0:T(8,128)(2,1)} %bitcast.13), channel_id=1, source_target_pairs={{0,4},{1,5},{2,6},{3,7},{4,0},{5,1},{6,2},{7,3},{8,12},{9,13},{10,... | collective-permute-start | bytes 393224 | tf_op jit(solution)/shard_map/ppermute | solution.py:19
  4.0 8.9 %collective-permute-start.1 = (bf16[16,4096]{1,0:T(8,128)(2,1)}, bf16[16,4096]{1,0:T(8,128)(2,1)S(1)}, u32[]{:S(2)}, u32[]{:S(2)}) collective-permute-start(bf16[16,4096]{1,0:T(8,128)(2,1)} %bitcast.14), channel_id=1, source_target_pairs={{0,1},{1,0},{2,3},{3,2},{4,5},{5,4},{6,7},{7,6},{8,9},{9,8},{10,11... | collective-permute-start | bytes 393224 | tf_op jit(solution)/shard_map/ppermute | solution.py:19
  5.6 10.1 %collective-permute-start = (bf16[16,4096]{1,0:T(8,128)(2,1)}, bf16[16,4096]{1,0:T(8,128)(2,1)S(1)}, u32[]{:S(2)}, u32[]{:S(2)}) collective-permute-start(bf16[16,4096]{1,0:T(8,128)(2,1)} %bitcast.15), channel_id=1, source_target_pairs={{0,2},{1,3},{2,0},{3,1},{4,6},{5,7},{6,4},{7,5},{8,10},{9,11},{10,... | collective-permute-start | bytes 393224 | tf_op jit(solution)/shard_map/ppermute | solution.py:19
  10.7 7.7 %collective-permute-start.5 = (bf16[16,4096]{1,0:T(8,128)(2,1)S(1)}, bf16[16,4096]{1,0:T(8,128)(2,1)S(1)}, u32[]{:S(2)}, u32[]{:S(2)}) collective-permute-start(bf16[16,4096]{1,0:T(8,128)(2,1)S(1)} %collective-permute-done.3.refs_2_), channel_id=1, source_target_pairs={{0,2},{1,3},{2,0},{3,1},{4,6},{5,7},{6,4},{7,5},{8,10},{9,11},{10,... | collective-permute-start | bytes 393224 | tf_op jit(solution)/shard_map/ppermute | solution.py:19
  11.4 6.9 %collective-permute-start.4 = (bf16[16,4096]{1,0:T(8,128)(2,1)S(1)}, bf16[16,4096]{1,0:T(8,128)(2,1)S(1)}, u32[]{:S(2)}, u32[]{:S(2)}) collective-permute-start(bf16[16,4096]{1,0:T(8,128)(2,1)S(1)} %collective-permute-done.3.refs_2_), channel_id=1, source_target_pairs={{0,1},{1,0},{2,3},{3,2},{4,5},{5,4},{6,7},{7,6},{8,9},{9,8},{10,11... | collective-permute-start | bytes 393224 | tf_op jit(solution)/shard_map/ppermute | solution.py:19
  12.9 7.8 %collective-permute-start.6 = (bf16[16,4096]{1,0:T(8,128)(2,1)S(1)}, bf16[16,4096]{1,0:T(8,128)(2,1)S(1)}, u32[]{:S(2)}, u32[]{:S(2)}) collective-permute-start(bf16[16,4096]{1,0:T(8,128)(2,1)S(1)} %collective-permute-done.1.refs_0_), channel_id=1, source_target_pairs={{0,6},{1,7},{2,4},{3,5},{4,2},{5,3},{6,0},{7,1},{8,14},{9,15},{10,... | collective-permute-start | bytes 393224 | tf_op jit(solution)/shard_map/ppermute | solution.py:19
  15.6 5.1 %collective-permute-start.2 = (bf16[16,4096]{1,0:T(8,128)(2,1)S(1)}, bf16[16,4096]{1,0:T(8,128)(2,1)S(1)}, u32[]{:S(2)}, u32[]{:S(2)}) collective-permute-start(bf16[16,4096]{1,0:T(8,128)(2,1)S(1)} %collective-permute-done.refs_1_), channel_id=1, source_target_pairs={{0,1},{1,0},{2,3},{3,2},{4,5},{5,4},{6,7},{7,6},{8,9},{9,8},{10,11... | collective-permute-start | bytes 393224 | tf_op jit(solution)/shard_map/ppermute | solution.py:19
  16.2 0.9 %copy-start.3 = (bf16[1,16,4096]{2,1,0:T(8,128)(2,1)S(1)}, bf16[1,16,4096]{2,1,0:T(8,128)(2,1)}, u32[]{:S(2)}) copy-start(bf16[1,16,4096]{2,1,0:T(8,128)(2,1)} %param.7) | copy-start | bytes 393220
  17.1 0.8 %copy-start.5 = (f32[1,3,4096]{2,0,1:T(1,128)S(1)}, f32[1,3,4096]{2,0,1:T(1,128)}, u32[]{:S(2)}) copy-start(f32[1,3,4096]{2,0,1:T(1,128)} %param.8) | copy-start | bytes 147460
  17.9 2.8 %copy-start = (bf16[1,4096,3,128]{3,1,2,0:T(8,128)(2,1)S(1)}, bf16[1,4096,3,128]{3,1,2,0:T(8,128)(2,1)}, u32[]{:S(2)}) copy-start(bf16[1,4096,3,128]{3,1,2,0:T(8,128)(2,1)} %param.9) | copy-start | bytes 9437188
  17.9 2.8 %copy-start.1 = (bf16[1,128,4096]{2,1,0:T(8,128)(2,1)S(1)}, bf16[1,128,4096]{2,1,0:T(8,128)(2,1)}, u32[]{:S(2)}) copy-start(bf16[1,128,4096]{2,1,0:T(8,128)(2,1)} %param.11) | copy-start | bytes 3145732
  17.9 2.8 %copy-start.2 = (bf16[1,2,256,128]{3,2,1,0:T(8,128)(2,1)S(1)}, bf16[1,2,256,128]{3,2,1,0:T(8,128)(2,1)}, u32[]{:S(2)}) copy-start(bf16[1,2,256,128]{3,2,1,0:T(8,128)(2,1)} %param.12) | copy-start | bytes 393220
  17.9 2.8 %copy-start.4 = (bf16[1,16,4096]{2,1,0:T(8,128)(2,1)S(1)}, bf16[1,16,4096]{2,1,0:T(8,128)(2,1)}, u32[]{:S(2)}) copy-start(bf16[1,16,4096]{2,1,0:T(8,128)(2,1)} %param.7) | copy-start | bytes 393220
  17.9 2.8 %copy-start.6 = (f32[1,3,4096]{2,0,1:T(1,128)S(1)}, f32[1,3,4096]{2,0,1:T(1,128)}, u32[]{:S(2)}) copy-start(f32[1,3,4096]{2,0,1:T(1,128)} %param.8) | copy-start | bytes 147460
  18.0 2.8 %copy-start.7 = (f32[1,2,128]{2,1,0:T(2,128)S(1)}, f32[1,2,128]{2,1,0:T(2,128)}, u32[]{:S(2)}) copy-start(f32[1,2,128]{2,1,0:T(2,128)} %param.10) | copy-start | bytes 3076
  22.9 6.7 %collective-permute-start.7 = (bf16[16,4096]{1,0:T(8,128)(2,1)S(1)}, bf16[16,4096]{1,0:T(8,128)(2,1)S(1)}, u32[]{:S(2)}, u32[]{:S(2)}) collective-permute-start(bf16[16,4096]{1,0:T(8,128)(2,1)S(1)} %get-tuple-element.14), channel_id=1, source_target_pairs={{0,1},{1,0},{2,3},{3,2},{4,5},{5,4},{6,7},{7,6},{8,9},{9,8},{10,11... | collective-permute-start | bytes 393224 | tf_op jit(solution)/shard_map/ppermute | solution.py:19
  24.5 5.2 %collective-permute-start.8 = (bf16[16,4096]{1,0:T(8,128)(2,1)S(1)}, bf16[16,4096]{1,0:T(8,128)(2,1)S(1)}, u32[]{:S(2)}, u32[]{:S(2)}) collective-permute-start(bf16[16,4096]{1,0:T(8,128)(2,1)S(1)} %get-tuple-element.15), channel_id=1, source_target_pairs={{0,2},{1,3},{2,0},{3,1},{4,6},{5,7},{6,4},{7,5},{8,10},{9,11},{10,... | collective-permute-start | bytes 393224 | tf_op jit(solution)/shard_map/ppermute | solution.py:19
  25.5 5.2 %collective-permute-start.10 = (bf16[16,4096]{1,0:T(8,128)(2,1)S(1)}, bf16[16,4096]{1,0:T(8,128)(2,1)S(1)}, u32[]{:S(2)}, u32[]{:S(2)}) collective-permute-start(bf16[16,4096]{1,0:T(8,128)(2,1)S(1)} %get-tuple-element.17), channel_id=1, source_target_pairs={{0,1},{1,0},{2,3},{3,2},{4,5},{5,4},{6,7},{7,6},{8,9},{9,8},{10,11... | collective-permute-start | bytes 393224 | tf_op jit(solution)/shard_map/ppermute | solution.py:19
  27.0 7.0 %collective-permute-start.12 = (bf16[16,4096]{1,0:T(8,128)(2,1)S(1)}, bf16[16,4096]{1,0:T(8,128)(2,1)S(1)}, u32[]{:S(2)}, u32[]{:S(2)}) collective-permute-start(bf16[16,4096]{1,0:T(8,128)(2,1)S(1)} %get-tuple-element.19), channel_id=1, source_target_pairs={{0,6},{1,7},{2,4},{3,5},{4,2},{5,3},{6,0},{7,1},{8,14},{9,15},{10,... | collective-permute-start | bytes 393224 | tf_op jit(solution)/shard_map/ppermute | solution.py:19
  29.6 5.3 %collective-permute-start.14 = (bf16[16,4096]{1,0:T(8,128)(2,1)S(1)}, bf16[16,4096]{1,0:T(8,128)(2,1)S(1)}, u32[]{:S(2)}, u32[]{:S(2)}) collective-permute-start(bf16[16,4096]{1,0:T(8,128)(2,1)S(1)} %get-tuple-element.20), channel_id=1, source_target_pairs={{0,8},{1,9},{2,10},{3,11},{4,12},{5,13},{6,14},{7,15},{8,16},{9,17... | collective-permute-start | bytes 393224 | tf_op jit(solution)/shard_map/ppermute | solution.py:19
  29.7 11.0 %collective-permute-start.9 = (bf16[16,4096]{1,0:T(8,128)(2,1)S(1)}, bf16[16,4096]{1,0:T(8,128)(2,1)S(1)}, u32[]{:S(2)}, u32[]{:S(2)}) collective-permute-start(bf16[16,4096]{1,0:T(8,128)(2,1)S(1)} %add_convert_fusion.3), channel_id=1, source_target_pairs={{0,12},{1,13},{2,14},{3,15},{4,8},{5,9},{6,10},{7,11},{8,20},{9,21... | collective-permute-start | bytes 393224 | tf_op jit(solution)/shard_map/ppermute | solution.py:19
  30.7 10.0 %collective-permute-start.11 = (bf16[16,4096]{1,0:T(8,128)(2,1)S(1)}, bf16[16,4096]{1,0:T(8,128)(2,1)S(1)}, u32[]{:S(2)}, u32[]{:S(2)}) collective-permute-start(bf16[16,4096]{1,0:T(8,128)(2,1)S(1)} %add_convert_fusion.2), channel_id=1, source_target_pairs={{0,10},{1,11},{2,8},{3,9},{4,14},{5,15},{6,12},{7,13},{8,18},{9,19... | collective-permute-start | bytes 393224 | tf_op jit(solution)/shard_map/ppermute | solution.py:19
  34.0 6.7 %collective-permute-start.13 = (bf16[16,4096]{1,0:T(8,128)(2,1)S(1)}, bf16[16,4096]{1,0:T(8,128)(2,1)S(1)}, u32[]{:S(2)}, u32[]{:S(2)}) collective-permute-start(bf16[16,4096]{1,0:T(8,128)(2,1)S(1)} %add_convert_fusion.1), channel_id=1, source_target_pairs={{0,9},{1,8},{2,11},{3,10},{4,13},{5,12},{6,15},{7,14},{8,17},{9,16... | collective-permute-start | bytes 393224 | tf_op jit(solution)/shard_map/ppermute | solution.py:19

commit v3 on v2

--- a/solution.py
+++ b/solution.py
@@ -21,7 +21,7 @@
 
 def plan(count):
     if count == 8:
-        return [(1, 0), (2, 0), (3, 2), (4, 0), (5, 4), (6, 4), (7, 1)]
+        return [(1, 0), (2, 0), (3, 0), (4, 0), (5, 4), (6, 4), (7, 1)]
     return [(r, r & (r - 1)) for r in range(1, count)]
 
 
@@ -31,10 +31,16 @@
     return [(r, r & (r - 1)) for r in reversed(range(count))]
 
 
-def gather(block, count):
+def after(block, other):
+    return lax.optimization_barrier((block, other))[0]
+
+
+def gather(block, count, mixed):
     blocks = {0: block}
     for r, parent in plan(count):
         blocks[r] = route(blocks[parent], r ^ parent)
+        if r == 4:
+            blocks[r] = after(blocks[r], mixed)
     return blocks
 
 
@@ -62,32 +68,66 @@
         in_specs=[vmem] * (1 + len(blocks)),
         out_specs=vmem,
         compiler_params=pltpu.CompilerParams(vmem_limit_bytes=12 * 2**20),
-        cost_estimate=pl.CostEstimate(flops=2 * 10**9, bytes_accessed=blocks[0].size * 64, transcendentals=0),
+        cost_estimate=pl.CostEstimate(flops=2 * 10**9, bytes_accessed=64 * blocks[0].size, transcendentals=0),
         name="early",
     )(mod, *blocks)
 
 
-def layer_kernel(count, start_ref, mod_ref, qkv_ref, stale_ref, out_w_ref, gain_ref, mixed_ref, own_ref, *refs):
-    late = len(refs) - 1 - count
-    blocks, outs, mixed = refs[:late], refs[late : late + count], refs[late + count]
+def heads_of(mixed, gain_ref, qkv_ref):
+    def part(j):
+        return jnp.dot(mixed, qkv_ref[j], preferred_element_type=jnp.float32)
+
+    def head_norm(values, gains):
+        return values * lax.rsqrt(jnp.mean(values * values, axis=-1, keepdims=True) + 1e-06) * gains
+
+    queries = head_norm(part(0), gain_ref[0:1, :]).astype(jnp.bfloat16)
+    keys = head_norm(part(1), gain_ref[1:2, :]).astype(jnp.bfloat16)
+    return queries, keys, part(2).astype(jnp.bfloat16)
+
+
+def modulate_into(mixed, at, blocks, mod_ref):
+    for block in blocks:
+        mixed[at : at + block.shape[0], :] = modulated(block[...], mod_ref)
+        at += block.shape[0]
+
+
+def middle_kernel(mod_ref, gain_ref, qkv_ref, mixed_ref, *refs):
+    blocks, heads_ref, mixed = refs[:-2], refs[-2], refs[-1]
+    first = mixed_ref.shape[0]
+    mixed[:first, :] = mixed_ref[...]
+    modulate_into(mixed, first, blocks, mod_ref)
+    for j, part in enumerate(heads_of(mixed[...], gain_ref, qkv_ref)):
+        heads_ref[j] = part
+
+
+def middle_heads(mod, gains, qkv, mixed, blocks):
+    vmem = pl.BlockSpec(memory_space=pltpu.VMEM)
+    tokens = mixed.shape[0] + sum(block.shape[0] for block in blocks)
+    width, head = qkv.shape[1:]
+    return pl.pallas_call(
+        middle_kernel,
+        out_shape=jax.ShapeDtypeStruct((3, tokens, head), jnp.bfloat16),
+        in_specs=[vmem] * (4 + len(blocks)),
+        out_specs=vmem,
+        scratch_shapes=[pltpu.VMEM((tokens, width), jnp.bfloat16)],
+        compiler_params=pltpu.CompilerParams(vmem_limit_bytes=24 * 2**20),
+        cost_estimate=pl.CostEstimate(flops=10**9, bytes_accessed=2 * qkv.size, transcendentals=0),
+        name="middle",
+    )(mod, gains, qkv, mixed, *blocks)
+
+
+def layer_kernel(count, outs_of, start_ref, mod_ref, qkv_ref, stale_ref, out_w_ref, gain_ref, heads_ref, own_ref, *refs):
     rows, width = own_ref.shape
+    number = len(outs_of) + 1
+    blocks, outs, attended_ref, mixed = refs[: -1 - number], refs[-1 - number : -2], refs[-2], refs[-1]
     head = qkv_ref.shape[2]
     clip = stale_ref.shape[1]
     patch = rows * count
-    first = mixed_ref.shape[0]
-    mixed[:first, :] = mixed_ref[...]
-    for i, block in enumerate(blocks):
-        mixed[first + i * rows : first + (i + 1) * rows, :] = modulated(block[...], mod_ref)
-
-    def project(j):
-        return jnp.dot(mixed[...], qkv_ref[j], preferred_element_type=jnp.float32)
-
-    def head_norm(values, gains):
-        return values * lax.rsqrt(jnp.mean(values * values, axis=-1, keepdims=True) + 1e-06) * gains
-
-    queries = head_norm(project(0), gain_ref[0:1, :]).astype(jnp.bfloat16)
-    keys_new = head_norm(project(1), gain_ref[1:2, :]).astype(jnp.bfloat16)
-    values_new = project(2).astype(jnp.bfloat16)
+    modulate_into(mixed, 0, blocks, mod_ref)
+    queries, keys_new, values_new = [
+        jnp.concatenate([heads_ref[j], part], axis=0)
+        for j, part in enumerate(heads_of(mixed[...], gain_ref, qkv_ref))
+    ]
 
     def scores_of(keys):
         raw = lax.dot_general(queries, keys, (((1,), (1,)), ((), ())), preferred_element_type=jnp.float32)
@@ -110,16 +150,27 @@
         probs_old, stale_ref[1], preferred_element_type=jnp.float32
     )
     attended = attended.astype(jnp.bfloat16)
+    attended_ref[...] = attended
+    project_out(attended, outs_of, outs, mod_ref, out_w_ref, own_ref)
+
+
+def project_out(attended, outs_of, outs, mod_ref, out_w_ref, own_ref):
+    rows, width = own_ref.shape
+    chosen = jnp.concatenate([attended[i * rows : (i + 1) * rows] for i in outs_of], axis=0)
     step = 512
     for at in range(0, width, step):
         columns = slice(at, at + step)
-        part = jnp.dot(attended, out_w_ref[:, columns], preferred_element_type=jnp.float32)
+        part = jnp.dot(chosen, out_w_ref[:, columns], preferred_element_type=jnp.float32)
         part = part * mod_ref[2, :, columns]
-        for r, out in enumerate(outs):
-            piece = part[r * rows : (r + 1) * rows]
-            if r == 0:
+        for k, out in enumerate(outs):
+            piece = part[k * rows : (k + 1) * rows]
+            if outs_of[k] == 0:
                 piece = piece + own_ref[:, columns].astype(jnp.float32)
             out[:, columns] = piece.astype(jnp.bfloat16)
+
+
+def rest_kernel(outs_of, mod_ref, out_w_ref, own_ref, attended_ref, *outs):
+    project_out(attended_ref[...], outs_of, outs, mod_ref, out_w_ref, own_ref)
 
 
 def add_up(*blocks):
@@ -132,10 +183,8 @@
 def reduce_scatter(parts, count):
     arrived = {r: [] for r in range(count)}
     for r, target in plan_back(count):
-        if r == 0:
-            arrived[0].append(route(parts[0], 0, 1))
-        else:
-            arrived[target].append(route(add_up(parts[r], *arrived[r]), r ^ target, int(target == 0)))
+        total = add_up(parts[r], *arrived[r]) if r and arrived[r] else parts[r]
+        arrived[target].append(route(total, r ^ target, int(target == 0)))
     return add_up(*arrived[0])
 
 
@@ -143,23 +192,39 @@
     count = lax.axis_size("seq")
     tokens_in = hidden[0]
     rows, width = tokens_in.shape
-    blocks = gather(tokens_in, count)
-    order = [0, 2, 1, 3, 4, 5, 6, 7] if count == 8 else list(range(count))
+    order = [0, 1, 2, 3, 7, 4, 5, 6] if count == 8 else list(range(count))
     mod, own = modulation.transpose(1, 0, 2), tokens_in
-    early = 2
-    mixed = early_rows(mod, [blocks[r] for r in order[:early]])
+    mixed = early_rows(mod, [own])
+    blocks = gather(tokens_in, count, mixed)
     vmem = pl.BlockSpec(memory_space=pltpu.VMEM)
-    late = [blocks[r] for r in order[early:]]
-    parts = pl.pallas_call(
-        functools.partial(layer_kernel, count),
-        out_shape=[jax.ShapeDtypeStruct((rows, width), jnp.bfloat16)] * count,
+    middle = count - 2
+    qkv, gains = w_qkv[0].transpose(1, 0, 2), qk_gain[0]
+    heads = middle_heads(mod, gains, qkv, mixed, [blocks[r] for r in order[1:middle]])
+    late = [blocks[r] for r in order[middle:]]
+    first = [order.index(r) for r in (count - 3, count - 2)]
+    rest = [i for i in range(count) if i not in first]
+    shape = jax.ShapeDtypeStruct((rows, width), jnp.bfloat16)
+    head = qkv.shape[2]
+    *parts, attended = pl.pallas_call(
+        functools.partial(layer_kernel, count, first),
+        out_shape=[shape] * len(first) + [jax.ShapeDtypeStruct((rows * count, head), jnp.bfloat16)],
         in_specs=[pl.BlockSpec(memory_space=pltpu.SMEM)] + [vmem] * (7 + len(late)),
-        out_specs=[vmem] * count,
-        scratch_shapes=[pltpu.VMEM((rows * count, width), jnp.bfloat16)],
-        compiler_params=pltpu.CompilerParams(vmem_limit_bytes=(12 + count) * 2**20),
+        out_specs=[vmem] * (len(first) + 1),
+        scratch_shapes=[pltpu.VMEM((rows * (count - middle), width), jnp.bfloat16)],
+        compiler_params=pltpu.CompilerParams(vmem_limit_bytes=24 * 2**20),
         name="layer",
-    )(patch_start, mod, w_qkv[0].transpose(1, 0, 2), stale_kv[0], w_out[0], qk_gain[0], mixed, own, *late)
-    return reduce_scatter(dict(zip(order, parts)), count)[None]
+    )(patch_start, mod, qkv, stale_kv[0], w_out[0], gains, heads, own, *late)
+    if rest:
+        parts += pl.pallas_call(
+            functools.partial(rest_kernel, rest),
+            out_shape=[shape] * len(rest),
+            in_specs=[vmem] * 4,
+            out_specs=[vmem] * len(rest),
+            compiler_params=pltpu.CompilerParams(vmem_limit_bytes=24 * 2**20),
+            name="rest",
+        )(mod, w_out[0], own, attended)
+    parts = {order[i]: part for i, part in zip(first + rest, parts)}
+    return reduce_scatter(parts, count)[None]
 
 
 def solution(mesh):

time: 41.6 us -> 41 us (0.986); the launches traced: 41.4 us -> 40.2 us
  waiting for transfers between devices: 12.4 us -> 10.6 us
  Pallas kernels: 2.48 us -> 3.35 us
    ppermute x15, waiting for transfers between devices: 12.4 us -> 10.6 us  [route(): return lax.ppermute(block, ('section', 'seq'), pairs)]
    pallas_call x1 -> x3, Pallas kernels: 2.15 us -> 3.08 us  [the longest x1 1.49 us: per_device(): pl.pallas_call(functools.partial(layer_kernel, count, first), out_shape=[...]
  transfers between devices with their start and end apart: 15 -> 15, of which waited for: 5 -> 5; matrix products, arithmetic and copies ran while one was open for 0% -> 0% of each run, Pallas kernels for 1% -> 5%
where the time goes in v3:
time: 41 us; the launch traced here: 40.2 us
  starting transfers between devices  22.9 us (56%)
  waiting for transfers between devices  10.6 us (26%)
  Pallas kernels  3.35 us (8%)
  local copies, waits for them, and re-layouts  1.73 us (4%)
  other arithmetic  0.84 us (2%)
  between operations  0.81 us (2%)
    ppermute x15, starting transfers between devices, route(): return lax.ppermute(block, ('section', 'seq'), pairs)  22.9 us
    ppermute x15, waiting for transfers between devices, route(): return lax.ppermute(block, ('section', 'seq'), pairs)  10.6 us
    unnamed x16, local copies, waits for them, and re-layouts  1.73 us
    pallas_call x1, Pallas kernels, per_device(): pl.pallas_call(functools.partial(layer_kernel, count, first), out_shape=[...  1.49 us
    pallas_call x1, Pallas kernels, middle_heads(): pl.pallas_call(middle_kernel, out_shape=jax.ShapeDtypeStruct((3, tokens,...  1.22 us
  transfers between devices with their start and end apart: 15, of which 5 were waited for; matrix products, arithmetic and copies ran while one was open for 0% of the time, Pallas kernels for 5%

profile of v3, /device:TPU:0, one launch (start us, length us, event | category | flops | bytes accessed | tf_op | source)
XLA Modules:
  0.0 40.2 jit_solution(15581032204550985573)
XLA Ops:
  0.0 3.0 %collective-permute-start = (bf16[16,4096]{1,0:T(8,128)(2,1)}, bf16[16,4096]{1,0:T(8,128)(2,1)S(1)}, u32[]{:S(2)}, u32[]{:S(2)}) collective-permute-start(bf16[16,4096]{1,0:T(8,128)(2,1)} %bitcast.14), channel_id=1, source_target_pairs={{0,1},{1,0},{2,3},{3,2},{4,5},{5,4},{6,7},{7,6},{8,9},{9,8},{10,11... | collective-permute-start | bytes 393224 | tf_op jit(solution)/shard_map/ppermute | solution.py:19
  3.0 2.6 %collective-permute-start.4 = (bf16[16,4096]{1,0:T(8,128)(2,1)}, bf16[16,4096]{1,0:T(8,128)(2,1)S(1)}, u32[]{:S(2)}, u32[]{:S(2)}) collective-permute-start(bf16[16,4096]{1,0:T(8,128)(2,1)} %bitcast.15), channel_id=1, source_target_pairs={{0,4},{1,5},{2,6},{3,7},{4,0},{5,1},{6,2},{7,3},{8,12},{9,13},{10,... | collective-permute-start | bytes 393224 | tf_op jit(solution)/shard_map/ppermute | solution.py:19
  5.6 1.5 %collective-permute-start.2 = (bf16[16,4096]{1,0:T(8,128)(2,1)}, bf16[16,4096]{1,0:T(8,128)(2,1)S(1)}, u32[]{:S(2)}, u32[]{:S(2)}) collective-permute-start(bf16[16,4096]{1,0:T(8,128)(2,1)} %bitcast.16), channel_id=1, source_target_pairs={{0,3},{1,2},{2,1},{3,0},{4,7},{5,6},{6,5},{7,4},{8,11},{9,10},{10,... | collective-permute-start | bytes 393224 | tf_op jit(solution)/shard_map/ppermute | solution.py:19
  7.1 0.4 %collective-permute-start.1 = (bf16[16,4096]{1,0:T(8,128)(2,1)}, bf16[16,4096]{1,0:T(8,128)(2,1)S(1)}, u32[]{:S(2)}, u32[]{:S(2)}) collective-permute-start(bf16[16,4096]{1,0:T(8,128)(2,1)} %bitcast.17), channel_id=1, source_target_pairs={{0,2},{1,3},{2,0},{3,1},{4,6},{5,7},{6,4},{7,5},{8,10},{9,11},{10,... | collective-permute-start | bytes 393224 | tf_op jit(solution)/shard_map/ppermute | solution.py:19
  7.5 0.0 collective-permute-done.refs_0_
  7.5 4.6 %collective-permute-start.3 = (bf16[16,4096]{1,0:T(8,128)(2,1)S(1)}, bf16[16,4096]{1,0:T(8,128)(2,1)S(1)}, u32[]{:S(2)}, u32[]{:S(2)}) collective-permute-start(bf16[16,4096]{1,0:T(8,128)(2,1)S(1)} %collective-permute-done.refs_0_), channel_id=1, source_target_pairs={{0,6},{1,7},{2,4},{3,5},{4,2},{5,3},{6,0},{7,1},{8,14},{9,15},{10,... | collective-permute-start | bytes 393224 | tf_op jit(solution)/shard_map/ppermute | solution.py:19
  12.1 0.0 copy-start.2
  12.1 0.9 %copy-done.2 = bf16[1,16,4096]{2,1,0:T(8,128)(2,1)S(1)} copy-done((bf16[1,16,4096]{2,1,0:T(8,128)(2,1)S(1)}, bf16[1,16,4096]{2,1,0:T(8,128)(2,1)}, u32[]{:S(2)}) %copy-start.2) | copy-done | bytes 131096
  13.0 0.0 copy-start.4
  13.0 0.8 %copy-done.4 = f32[1,3,4096]{2,0,1:T(1,128)S(1)} copy-done((f32[1,3,4096]{2,0,1:T(1,128)S(1)}, f32[1,3,4096]{2,0,1:T(1,128)}, u32[]{:S(2)}) %copy-start.4) | copy-done | bytes 49176
  13.8 0.0 copy-start
  13.8 0.0 copy-start.5
  13.8 0.0 copy-start.7
  13.8 0.3 early.1.mixed_ref
  14.1 0.0 copy-start.1
  14.1 0.0 copy-start.3
  14.1 0.0 copy-start.6
  14.1 0.0 collective-permute-done.4.refs_4_
  14.1 0.1 collective-permute-start.6
  14.2 2.0 %collective-permute-start.5 = (bf16[16,4096]{1,0:T(8,128)(2,1)S(1)}, bf16[16,4096]{1,0:T(8,128)(2,1)S(1)}, u32[]{:S(2)}, u32[]{:S(2)}) collective-permute-start(bf16[16,4096]{1,0:T(8,128)(2,1)S(1)} %collective-permute-done.4.refs_4_), channel_id=1, source_target_pairs={{0,1},{1,0},{2,3},{3,2},{4,5},{5,4},{6,7},{7,6},{8,9},{9,8},{10,11... | collective-permute-start | bytes 393224 | tf_op jit(solution)/shard_map/ppermute | solution.py:19
  16.9 0.0 collective-permute-done.2.refs_2_
  16.9 0.1 collective-permute-done.1.refs_1_
  16.9 3.0 %collective-permute-done.3.refs_3_ = bf16[16,4096]{1,0:T(8,128)(2,1)S(1)} collective-permute-done((bf16[16,4096]{1,0:T(8,128)(2,1)S(1)}, bf16[16,4096]{1,0:T(8,128)(2,1)S(1)}, u32[]{:S(2)}, u32[]{:S(2)}) %collective-permute-start.3) | collective-permute-done | bytes 131104 | tf_op jit(solution)/shard_map/ppermute | solution.py:19
  19.9 0.0 copy-done
  19.9 0.0 copy-done.5
  19.9 0.0 copy-done.7
  20.0 1.2 %middle.1.heads_ref = bf16[3,96,128]{2,1,0:T(8,128)(2,1)S(1)} custom-call(f32[3,1,4096]{2,1,0:T(1,128)S(1)} %bitcast.22, f32[2,128]{1,0:T(2,128)S(1)} %bitcast.26, bf16[3,4096,128]{2,1,0:T(8,128)(2,1)S(1)} %bitcast.10, bf16[16,4096]{1,0:T(8,128)(2,1)S(1)} %early.1.mixed_ref, bf16[16,4096]{1,0:T(8,128)(2,1)S(1)} %collective-permute-done.refs_0_, ...), custom_call_target="tpu_custom_call" | custom-call | flops 1000000000 | bytes 3145728 | tf_op jit(solution)/shard_map/middle/pallas_call | solution.py:107
  21.2 0.0 collective-permute-done.6.refs_1_
  21.2 0.0 collective-permute-done.5.refs_0_
  21.2 0.0 copy-done.1
  21.2 0.0 copy-done.3
  21.2 0.0 copy-done.6
  21.2 1.5 %layer.1 = (bf16[16,4096]{1,0:T(8,128)(2,1)S(1)}, bf16[16,4096]{1,0:T(8,128)(2,1)S(1)}, bf16[128,128]{1,0:T(8,128)(2,1)S(1)}) custom-call(s32[1]{0:T(128)S(6)} %copy.8.start_ref, f32[3,1,4096]{2,1,0:T(1,128)S(1)} %bitcast.23, bf16[3,4096,128]{2,1,0:T(8,128)(2,1)S(1)} %bitcast.11, bf16[2,256,128]{2,1,0:T(8,128)(2,1)S(1)} %bitcast.25, ...), custom_call_target="tpu_custom_call" | custom-call | tf_op jit(solution)/shard_map/layer/pallas_call | solution.py:208
  22.7 0.8 %collective-permute-start.7 = (bf16[16,4096]{1,0:T(8,128)(2,1)S(1)}, bf16[16,4096]{1,0:T(8,128)(2,1)S(1)}, u32[]{:S(2)}, u32[]{:S(2)}) collective-permute-start(bf16[16,4096]{1,0:T(8,128)(2,1)S(1)} %get-tuple-element.18), channel_id=1, source_target_pairs={{0,1},{1,0},{2,3},{3,2},{4,5},{5,4},{6,7},{7,6},{8,9},{9,8},{10,11... | collective-permute-start | bytes 393224 | tf_op jit(solution)/shard_map/ppermute | solution.py:19
  23.6 1.1 %collective-permute-start.8 = (bf16[16,4096]{1,0:T(8,128)(2,1)S(1)}, bf16[16,4096]{1,0:T(8,128)(2,1)S(1)}, u32[]{:S(2)}, u32[]{:S(2)}) collective-permute-start(bf16[16,4096]{1,0:T(8,128)(2,1)S(1)} %get-tuple-element.19), channel_id=1, source_target_pairs={{0,2},{1,3},{2,0},{3,1},{4,6},{5,7},{6,4},{7,5},{8,10},{9,11},{10,... | collective-permute-start | bytes 393224 | tf_op jit(solution)/shard_map/ppermute | solution.py:19
  24.7 0.4 rest.1
  25.1 0.9 %collective-permute-start.10 = (bf16[16,4096]{1,0:T(8,128)(2,1)S(1)}, bf16[16,4096]{1,0:T(8,128)(2,1)S(1)}, u32[]{:S(2)}, u32[]{:S(2)}) collective-permute-start(bf16[16,4096]{1,0:T(8,128)(2,1)S(1)} %get-tuple-element.21), channel_id=1, source_target_pairs={{0,1},{1,0},{2,3},{3,2},{4,5},{5,4},{6,7},{7,6},{8,9},{9,8},{10,11... | collective-permute-start | bytes 393224 | tf_op jit(solution)/shard_map/ppermute | solution.py:19
  26.0 1.8 %collective-permute-start.12 = (bf16[16,4096]{1,0:T(8,128)(2,1)S(1)}, bf16[16,4096]{1,0:T(8,128)(2,1)S(1)}, u32[]{:S(2)}, u32[]{:S(2)}) collective-permute-start(bf16[16,4096]{1,0:T(8,128)(2,1)S(1)} %get-tuple-element.23), channel_id=1, source_target_pairs={{0,6},{1,7},{2,4},{3,5},{4,2},{5,3},{6,0},{7,1},{8,14},{9,15},{10,... | collective-permute-start | bytes 393224 | tf_op jit(solution)/shard_map/ppermute | solution.py:19
  27.8 0.0 collective-permute-start.14
  27.8 0.5 %collective-permute-done.7 = bf16[16,4096]{1,0:T(8,128)(2,1)S(1)} collective-permute-done((bf16[16,4096]{1,0:T(8,128)(2,1)S(1)}, bf16[16,4096]{1,0:T(8,128)(2,1)S(1)}, u32[]{:S(2)}, u32[]{:S(2)}) %collective-permute-start.7) | collective-permute-done | bytes 131104 | tf_op jit(solution)/shard_map/ppermute | solution.py:19
  28.3 0.6 %collective-permute-done.8 = bf16[16,4096]{1,0:T(8,128)(2,1)S(1)} collective-permute-done((bf16[16,4096]{1,0:T(8,128)(2,1)S(1)}, bf16[16,4096]{1,0:T(8,128)(2,1)S(1)}, u32[]{:S(2)}, u32[]{:S(2)}) %collective-permute-start.8) | collective-permute-done | bytes 131104 | tf_op jit(solution)/shard_map/ppermute | solution.py:19
  28.9 0.1 add_convert_fusion.3
  29.0 1.1 %collective-permute-start.9 = (bf16[16,4096]{1,0:T(8,128)(2,1)S(1)}, bf16[16,4096]{1,0:T(8,128)(2,1)S(1)}, u32[]{:S(2)}, u32[]{:S(2)}) collective-permute-start(bf16[16,4096]{1,0:T(8,128)(2,1)S(1)} %add_convert_fusion.3), channel_id=1, source_target_pairs={{0,12},{1,13},{2,14},{3,15},{4,8},{5,9},{6,10},{7,11},{8,20},{9,21... | collective-permute-start | bytes 393224 | tf_op jit(solution)/shard_map/ppermute | solution.py:19
  30.1 0.0 collective-permute-done.10
  30.1 2.9 %collective-permute-start.11 = (bf16[16,4096]{1,0:T(8,128)(2,1)S(1)}, bf16[16,4096]{1,0:T(8,128)(2,1)S(1)}, u32[]{:S(2)}, u32[]{:S(2)}) collective-permute-start(bf16[16,4096]{1,0:T(8,128)(2,1)S(1)} %add_convert_fusion.2), channel_id=1, source_target_pairs={{0,10},{1,11},{2,8},{3,9},{4,14},{5,15},{6,12},{7,13},{8,18},{9,19... | collective-permute-start | bytes 393224 | tf_op jit(solution)/shard_map/ppermute | solution.py:19
  33.0 0.0 collective-permute-done.12
  33.1 0.1 collective-permute-start.13
  33.1 0.0 collective-permute-done.14
  33.1 6.4 %collective-permute-done.9 = bf16[16,4096]{1,0:T(8,128)(2,1)S(1)} collective-permute-done((bf16[16,4096]{1,0:T(8,128)(2,1)S(1)}, bf16[16,4096]{1,0:T(8,128)(2,1)S(1)}, u32[]{:S(2)}, u32[]{:S(2)}) %collective-permute-start.9) | collective-permute-done | bytes 131104 | tf_op jit(solution)/shard_map/ppermute | solution.py:19
  39.5 0.0 collective-permute-done.11
  39.5 0.0 collective-permute-done.13
  39.5 0.7 %fusion = bf16[1,16,4096]{2,1,0:T(8,128)(2,1)} fusion(bf16[16,4096]{1,0:T(8,128)(2,1)S(1)} %collective-permute-done.14, bf16[16,4096]{1,0:T(8,128)(2,1)S(1)} %collective-permute-done.13, bf16[16,4096]{1,0:T(8,128)(2,1)S(1)} %collective-permute-done.11, bf16[16,4096]{1,0:T(8,128)(2,1)S(1)} %collective-permute-done.9), kind=kLoop, calls=%fused_computation.4 | loop fusion | flops 524288 | bytes 655360 | tf_op jit(solution)/shard_map/broadcast_in_dim | solution.py:227
  (2 shorter events, 0.1 us)
Async XLA Ops:
  0.0 7.5 %collective-permute-start = (bf16[16,4096]{1,0:T(8,128)(2,1)}, bf16[16,4096]{1,0:T(8,128)(2,1)S(1)}, u32[]{:S(2)}, u32[]{:S(2)}) collective-permute-start(bf16[16,4096]{1,0:T(8,128)(2,1)} %bitcast.14), channel_id=1, source_target_pairs={{0,1},{1,0},{2,3},{3,2},{4,5},{5,4},{6,7},{7,6},{8,9},{9,8},{10,11... | collective-permute-start | bytes 393224 | tf_op jit(solution)/shard_map/ppermute | solution.py:19
  3.0 11.2 %collective-permute-start.4 = (bf16[16,4096]{1,0:T(8,128)(2,1)}, bf16[16,4096]{1,0:T(8,128)(2,1)S(1)}, u32[]{:S(2)}, u32[]{:S(2)}) collective-permute-start(bf16[16,4096]{1,0:T(8,128)(2,1)} %bitcast.15), channel_id=1, source_target_pairs={{0,4},{1,5},{2,6},{3,7},{4,0},{5,1},{6,2},{7,3},{8,12},{9,13},{10,... | collective-permute-start | bytes 393224 | tf_op jit(solution)/shard_map/ppermute | solution.py:19
  5.6 11.3 %collective-permute-start.2 = (bf16[16,4096]{1,0:T(8,128)(2,1)}, bf16[16,4096]{1,0:T(8,128)(2,1)S(1)}, u32[]{:S(2)}, u32[]{:S(2)}) collective-permute-start(bf16[16,4096]{1,0:T(8,128)(2,1)} %bitcast.16), channel_id=1, source_target_pairs={{0,3},{1,2},{2,1},{3,0},{4,7},{5,6},{6,5},{7,4},{8,11},{9,10},{10,... | collective-permute-start | bytes 393224 | tf_op jit(solution)/shard_map/ppermute | solution.py:19
  7.1 9.9 %collective-permute-start.1 = (bf16[16,4096]{1,0:T(8,128)(2,1)}, bf16[16,4096]{1,0:T(8,128)(2,1)S(1)}, u32[]{:S(2)}, u32[]{:S(2)}) collective-permute-start(bf16[16,4096]{1,0:T(8,128)(2,1)} %bitcast.17), channel_id=1, source_target_pairs={{0,2},{1,3},{2,0},{3,1},{4,6},{5,7},{6,4},{7,5},{8,10},{9,11},{10,... | collective-permute-start | bytes 393224 | tf_op jit(solution)/shard_map/ppermute | solution.py:19
  7.5 12.4 %collective-permute-start.3 = (bf16[16,4096]{1,0:T(8,128)(2,1)S(1)}, bf16[16,4096]{1,0:T(8,128)(2,1)S(1)}, u32[]{:S(2)}, u32[]{:S(2)}) collective-permute-start(bf16[16,4096]{1,0:T(8,128)(2,1)S(1)} %collective-permute-done.refs_0_), channel_id=1, source_target_pairs={{0,6},{1,7},{2,4},{3,5},{4,2},{5,3},{6,0},{7,1},{8,14},{9,15},{10,... | collective-permute-start | bytes 393224 | tf_op jit(solution)/shard_map/ppermute | solution.py:19
  12.1 0.9 %copy-start.2 = (bf16[1,16,4096]{2,1,0:T(8,128)(2,1)S(1)}, bf16[1,16,4096]{2,1,0:T(8,128)(2,1)}, u32[]{:S(2)}) copy-start(bf16[1,16,4096]{2,1,0:T(8,128)(2,1)} %param.7) | copy-start | bytes 393220
  13.0 0.8 %copy-start.4 = (f32[1,3,4096]{2,0,1:T(1,128)S(1)}, f32[1,3,4096]{2,0,1:T(1,128)}, u32[]{:S(2)}) copy-start(f32[1,3,4096]{2,0,1:T(1,128)} %param.8) | copy-start | bytes 147460
  13.8 6.1 %copy-start = (bf16[1,4096,3,128]{3,1,2,0:T(8,128)(2,1)S(1)}, bf16[1,4096,3,128]{3,1,2,0:T(8,128)(2,1)}, u32[]{:S(2)}) copy-start(bf16[1,4096,3,128]{3,1,2,0:T(8,128)(2,1)} %param.9) | copy-start | bytes 9437188
  13.8 6.1 %copy-start.5 = (f32[1,3,4096]{2,0,1:T(1,128)S(1)}, f32[1,3,4096]{2,0,1:T(1,128)}, u32[]{:S(2)}) copy-start(f32[1,3,4096]{2,0,1:T(1,128)} %param.8) | copy-start | bytes 147460
  13.8 6.1 %copy-start.7 = (f32[1,2,128]{2,1,0:T(2,128)S(1)}, f32[1,2,128]{2,1,0:T(2,128)}, u32[]{:S(2)}) copy-start(f32[1,2,128]{2,1,0:T(2,128)} %param.10) | copy-start | bytes 3076
  14.1 7.1 %copy-start.1 = (bf16[1,128,4096]{2,1,0:T(8,128)(2,1)S(1)}, bf16[1,128,4096]{2,1,0:T(8,128)(2,1)}, u32[]{:S(2)}) copy-start(bf16[1,128,4096]{2,1,0:T(8,128)(2,1)} %param.11) | copy-start | bytes 3145732
  14.1 7.1 %copy-start.3 = (bf16[1,16,4096]{2,1,0:T(8,128)(2,1)S(1)}, bf16[1,16,4096]{2,1,0:T(8,128)(2,1)}, u32[]{:S(2)}) copy-start(bf16[1,16,4096]{2,1,0:T(8,128)(2,1)} %param.7) | copy-start | bytes 393220
  14.1 7.1 %copy-start.6 = (bf16[1,2,256,128]{3,2,1,0:T(8,128)(2,1)S(1)}, bf16[1,2,256,128]{3,2,1,0:T(8,128)(2,1)}, u32[]{:S(2)}) copy-start(bf16[1,2,256,128]{3,2,1,0:T(8,128)(2,1)} %param.12) | copy-start | bytes 393220
  14.1 7.0 %collective-permute-start.6 = (bf16[16,4096]{1,0:T(8,128)(2,1)S(1)}, bf16[16,4096]{1,0:T(8,128)(2,1)S(1)}, u32[]{:S(2)}, u32[]{:S(2)}) collective-permute-start(bf16[16,4096]{1,0:T(8,128)(2,1)S(1)} %collective-permute-done.4.refs_4_), channel_id=1, source_target_pairs={{0,2},{1,3},{2,0},{3,1},{4,6},{5,7},{6,4},{7,5},{8,10},{9,11},{10,... | collective-permute-start | bytes 393224 | tf_op jit(solution)/shard_map/ppermute | solution.py:19
  14.2 7.0 %collective-permute-start.5 = (bf16[16,4096]{1,0:T(8,128)(2,1)S(1)}, bf16[16,4096]{1,0:T(8,128)(2,1)S(1)}, u32[]{:S(2)}, u32[]{:S(2)}) collective-permute-start(bf16[16,4096]{1,0:T(8,128)(2,1)S(1)} %collective-permute-done.4.refs_4_), channel_id=1, source_target_pairs={{0,1},{1,0},{2,3},{3,2},{4,5},{5,4},{6,7},{7,6},{8,9},{9,8},{10,11... | collective-permute-start | bytes 393224 | tf_op jit(solution)/shard_map/ppermute | solution.py:19
  22.7 5.6 %collective-permute-start.7 = (bf16[16,4096]{1,0:T(8,128)(2,1)S(1)}, bf16[16,4096]{1,0:T(8,128)(2,1)S(1)}, u32[]{:S(2)}, u32[]{:S(2)}) collective-permute-start(bf16[16,4096]{1,0:T(8,128)(2,1)S(1)} %get-tuple-element.18), channel_id=1, source_target_pairs={{0,1},{1,0},{2,3},{3,2},{4,5},{5,4},{6,7},{7,6},{8,9},{9,8},{10,11... | collective-permute-start | bytes 393224 | tf_op jit(solution)/shard_map/ppermute | solution.py:19
  23.6 5.4 %collective-permute-start.8 = (bf16[16,4096]{1,0:T(8,128)(2,1)S(1)}, bf16[16,4096]{1,0:T(8,128)(2,1)S(1)}, u32[]{:S(2)}, u32[]{:S(2)}) collective-permute-start(bf16[16,4096]{1,0:T(8,128)(2,1)S(1)} %get-tuple-element.19), channel_id=1, source_target_pairs={{0,2},{1,3},{2,0},{3,1},{4,6},{5,7},{6,4},{7,5},{8,10},{9,11},{10,... | collective-permute-start | bytes 393224 | tf_op jit(solution)/shard_map/ppermute | solution.py:19
  25.1 5.0 %collective-permute-start.10 = (bf16[16,4096]{1,0:T(8,128)(2,1)S(1)}, bf16[16,4096]{1,0:T(8,128)(2,1)S(1)}, u32[]{:S(2)}, u32[]{:S(2)}) collective-permute-start(bf16[16,4096]{1,0:T(8,128)(2,1)S(1)} %get-tuple-element.21), channel_id=1, source_target_pairs={{0,1},{1,0},{2,3},{3,2},{4,5},{5,4},{6,7},{7,6},{8,9},{9,8},{10,11... | collective-permute-start | bytes 393224 | tf_op jit(solution)/shard_map/ppermute | solution.py:19
  26.0 7.0 %collective-permute-start.12 = (bf16[16,4096]{1,0:T(8,128)(2,1)S(1)}, bf16[16,4096]{1,0:T(8,128)(2,1)S(1)}, u32[]{:S(2)}, u32[]{:S(2)}) collective-permute-start(bf16[16,4096]{1,0:T(8,128)(2,1)S(1)} %get-tuple-element.23), channel_id=1, source_target_pairs={{0,6},{1,7},{2,4},{3,5},{4,2},{5,3},{6,0},{7,1},{8,14},{9,15},{10,... | collective-permute-start | bytes 393224 | tf_op jit(solution)/shard_map/ppermute | solution.py:19
  27.8 5.4 %collective-permute-start.14 = (bf16[16,4096]{1,0:T(8,128)(2,1)S(1)}, bf16[16,4096]{1,0:T(8,128)(2,1)S(1)}, u32[]{:S(2)}, u32[]{:S(2)}) collective-permute-start(bf16[16,4096]{1,0:T(8,128)(2,1)S(1)} %get-tuple-element.24), channel_id=1, source_target_pairs={{0,8},{1,9},{2,10},{3,11},{4,12},{5,13},{6,14},{7,15},{8,16},{9,17... | collective-permute-start | bytes 393224 | tf_op jit(solution)/shard_map/ppermute | solution.py:19
  29.0 10.5 %collective-permute-start.9 = (bf16[16,4096]{1,0:T(8,128)(2,1)S(1)}, bf16[16,4096]{1,0:T(8,128)(2,1)S(1)}, u32[]{:S(2)}, u32[]{:S(2)}) collective-permute-start(bf16[16,4096]{1,0:T(8,128)(2,1)S(1)} %add_convert_fusion.3), channel_id=1, source_target_pairs={{0,12},{1,13},{2,14},{3,15},{4,8},{5,9},{6,10},{7,11},{8,20},{9,21... | collective-permute-start | bytes 393224 | tf_op jit(solution)/shard_map/ppermute | solution.py:19
  30.1 9.4 %collective-permute-start.11 = (bf16[16,4096]{1,0:T(8,128)(2,1)S(1)}, bf16[16,4096]{1,0:T(8,128)(2,1)S(1)}, u32[]{:S(2)}, u32[]{:S(2)}) collective-permute-start(bf16[16,4096]{1,0:T(8,128)(2,1)S(1)} %add_convert_fusion.2), channel_id=1, source_target_pairs={{0,10},{1,11},{2,8},{3,9},{4,14},{5,15},{6,12},{7,13},{8,18},{9,19... | collective-permute-start | bytes 393224 | tf_op jit(solution)/shard_map/ppermute | solution.py:19
  33.1 6.4 %collective-permute-start.13 = (bf16[16,4096]{1,0:T(8,128)(2,1)S(1)}, bf16[16,4096]{1,0:T(8,128)(2,1)S(1)}, u32[]{:S(2)}, u32[]{:S(2)}) collective-permute-start(bf16[16,4096]{1,0:T(8,128)(2,1)S(1)} %add_convert_fusion.1), channel_id=1, source_target_pairs={{0,9},{1,8},{2,11},{3,10},{4,13},{5,12},{6,15},{7,14},{8,17},{9,16... | collective-permute-start | bytes 393224 | tf_op jit(solution)/shard_map/ppermute | solution.py:19

commit v4 on v3

--- a/solution.py
+++ b/solution.py
@@ -21,7 +21,7 @@
 
 def plan(count):
     if count == 8:
-        return [(1, 0), (2, 0), (3, 0), (4, 0), (5, 4), (6, 4), (7, 1)]
+        return [(1, 0), (2, 0), (3, 0), (4, 0), (5, 4), (6, 4), (7, 4)]
     return [(r, r & (r - 1)) for r in range(1, count)]
 
 
@@ -192,7 +192,7 @@
     count = lax.axis_size("seq")
     tokens_in = hidden[0]
     rows, width = tokens_in.shape
-    order = [0, 1, 2, 3, 7, 4, 5, 6] if count == 8 else list(range(count))
+    order = [0, 1, 2, 3, 4, 7, 6, 5] if count == 8 else list(range(count))
     mod, own = modulation.transpose(1, 0, 2), tokens_in
     mixed = early_rows(mod, [own])
     blocks = gather(tokens_in, count, mixed)

time: 41 us -> 40.5 us (0.988); the launches traced: 40.2 us -> 40.2 us
  waiting for transfers between devices: 10.6 us -> 12.3 us
  starting transfers between devices: 22.9 us -> 21.2 us
    ppermute x15, starting transfers between devices: 22.9 us -> 21.2 us  [route(): return lax.ppermute(block, ('section', 'seq'), pairs)]
    ppermute x15, waiting for transfers between devices: 10.6 us -> 12.3 us  [route(): return lax.ppermute(block, ('section', 'seq'), pairs)]
  transfers between devices with their start and end apart: 15 -> 15, of which waited for: 5 -> 9; matrix products, arithmetic and copies ran while one was open for 0% -> 0% of each run, Pallas kernels for 5% -> 5%
where the time goes in v4:
time: 40.5 us; the launch traced here: 40.2 us
  starting transfers between devices  21.2 us (52%)
  waiting for transfers between devices  12.3 us (30%)
  Pallas kernels  3.35 us (8%)
  local copies, waits for them, and re-layouts  1.77 us (4%)
  other arithmetic  0.84 us (2%)
  between operations  0.74 us (2%)
    ppermute x15, starting transfers between devices, route(): return lax.ppermute(block, ('section', 'seq'), pairs)  21.2 us
    ppermute x15, waiting for transfers between devices, route(): return lax.ppermute(block, ('section', 'seq'), pairs)  12.3 us
    unnamed x16, local copies, waits for them, and re-layouts  1.77 us
    pallas_call x1, Pallas kernels, per_device(): pl.pallas_call(functools.partial(layer_kernel, count, first), out_shape=[...  1.49 us
    pallas_call x1, Pallas kernels, middle_heads(): pl.pallas_call(middle_kernel, out_shape=jax.ShapeDtypeStruct((3, tokens,...  1.22 us
  transfers between devices with their start and end apart: 15, of which 9 were waited for; matrix products, arithmetic and copies ran while one was open for 0% of the time, Pallas kernels for 5%

profile of v4, /device:TPU:0, one launch (start us, length us, event | category | flops | bytes accessed | tf_op | source)
XLA Modules:
  0.0 40.2 jit_solution(2602556575922695207)
XLA Ops:
  0.0 4.0 %collective-permute-start.3 = (bf16[16,4096]{1,0:T(8,128)(2,1)}, bf16[16,4096]{1,0:T(8,128)(2,1)S(1)}, u32[]{:S(2)}, u32[]{:S(2)}) collective-permute-start(bf16[16,4096]{1,0:T(8,128)(2,1)} %bitcast.14), channel_id=1, source_target_pairs={{0,4},{1,5},{2,6},{3,7},{4,0},{5,1},{6,2},{7,3},{8,12},{9,13},{10,... | collective-permute-start | bytes 393224 | tf_op jit(solution)/shard_map/ppermute | solution.py:19
  4.0 2.5 %collective-permute-start.2 = (bf16[16,4096]{1,0:T(8,128)(2,1)}, bf16[16,4096]{1,0:T(8,128)(2,1)S(1)}, u32[]{:S(2)}, u32[]{:S(2)}) collective-permute-start(bf16[16,4096]{1,0:T(8,128)(2,1)} %bitcast.15), channel_id=1, source_target_pairs={{0,3},{1,2},{2,1},{3,0},{4,7},{5,6},{6,5},{7,4},{8,11},{9,10},{10,... | collective-permute-start | bytes 393224 | tf_op jit(solution)/shard_map/ppermute | solution.py:19
  6.6 0.4 %collective-permute-start.1 = (bf16[16,4096]{1,0:T(8,128)(2,1)}, bf16[16,4096]{1,0:T(8,128)(2,1)S(1)}, u32[]{:S(2)}, u32[]{:S(2)}) collective-permute-start(bf16[16,4096]{1,0:T(8,128)(2,1)} %bitcast.16), channel_id=1, source_target_pairs={{0,2},{1,3},{2,0},{3,1},{4,6},{5,7},{6,4},{7,5},{8,10},{9,11},{10,... | collective-permute-start | bytes 393224 | tf_op jit(solution)/shard_map/ppermute | solution.py:19
  7.0 0.5 %collective-permute-start = (bf16[16,4096]{1,0:T(8,128)(2,1)}, bf16[16,4096]{1,0:T(8,128)(2,1)S(1)}, u32[]{:S(2)}, u32[]{:S(2)}) collective-permute-start(bf16[16,4096]{1,0:T(8,128)(2,1)} %bitcast.17), channel_id=1, source_target_pairs={{0,1},{1,0},{2,3},{3,2},{4,5},{5,4},{6,7},{7,6},{8,9},{9,8},{10,11... | collective-permute-start | bytes 393224 | tf_op jit(solution)/shard_map/ppermute | solution.py:19
  7.5 0.0 copy-start.2
  7.5 0.9 %copy-done.2 = bf16[1,16,4096]{2,1,0:T(8,128)(2,1)S(1)} copy-done((bf16[1,16,4096]{2,1,0:T(8,128)(2,1)S(1)}, bf16[1,16,4096]{2,1,0:T(8,128)(2,1)}, u32[]{:S(2)}) %copy-start.2) | copy-done | bytes 131096
  8.5 0.0 copy-start.4
  8.5 0.8 %copy-done.4 = f32[1,3,4096]{2,0,1:T(1,128)S(1)} copy-done((f32[1,3,4096]{2,0,1:T(1,128)S(1)}, f32[1,3,4096]{2,0,1:T(1,128)}, u32[]{:S(2)}) %copy-start.4) | copy-done | bytes 49176
  9.3 0.0 copy-start
  9.3 0.0 copy-start.5
  9.3 0.0 copy-start.7
  9.3 0.3 early.1.mixed_ref
  9.5 0.0 copy-start.1
  9.6 0.0 copy-start.3
  9.6 0.0 copy-start.6
  9.6 1.1 %collective-permute-done.3.refs_3_ = bf16[16,4096]{1,0:T(8,128)(2,1)S(1)} collective-permute-done((bf16[16,4096]{1,0:T(8,128)(2,1)}, bf16[16,4096]{1,0:T(8,128)(2,1)S(1)}, u32[]{:S(2)}, u32[]{:S(2)}) %collective-permute-start.3) | collective-permute-done | bytes 131104 | tf_op jit(solution)/shard_map/ppermute | solution.py:19
  10.6 1.7 %collective-permute-start.4 = (bf16[16,4096]{1,0:T(8,128)(2,1)S(1)}, bf16[16,4096]{1,0:T(8,128)(2,1)S(1)}, u32[]{:S(2)}, u32[]{:S(2)}) collective-permute-start(bf16[16,4096]{1,0:T(8,128)(2,1)S(1)} %collective-permute-done.3.refs_3_), channel_id=1, source_target_pairs={{0,3},{1,2},{2,1},{3,0},{4,7},{5,6},{6,5},{7,4},{8,11},{9,10},{10,... | collective-permute-start | bytes 393224 | tf_op jit(solution)/shard_map/ppermute | solution.py:19
  12.4 0.5 %collective-permute-start.6 = (bf16[16,4096]{1,0:T(8,128)(2,1)S(1)}, bf16[16,4096]{1,0:T(8,128)(2,1)S(1)}, u32[]{:S(2)}, u32[]{:S(2)}) collective-permute-start(bf16[16,4096]{1,0:T(8,128)(2,1)S(1)} %collective-permute-done.3.refs_3_), channel_id=1, source_target_pairs={{0,1},{1,0},{2,3},{3,2},{4,5},{5,4},{6,7},{7,6},{8,9},{9,8},{10,11... | collective-permute-start | bytes 393224 | tf_op jit(solution)/shard_map/ppermute | solution.py:19
  12.9 0.3 collective-permute-done.2.refs_2_
  13.2 1.2 %collective-permute-start.5 = (bf16[16,4096]{1,0:T(8,128)(2,1)S(1)}, bf16[16,4096]{1,0:T(8,128)(2,1)S(1)}, u32[]{:S(2)}, u32[]{:S(2)}) collective-permute-start(bf16[16,4096]{1,0:T(8,128)(2,1)S(1)} %collective-permute-done.3.refs_3_), channel_id=1, source_target_pairs={{0,2},{1,3},{2,0},{3,1},{4,6},{5,7},{6,4},{7,5},{8,10},{9,11},{10,... | collective-permute-start | bytes 393224 | tf_op jit(solution)/shard_map/ppermute | solution.py:19
  15.1 0.6 %collective-permute-done.1.refs_1_ = bf16[16,4096]{1,0:T(8,128)(2,1)S(1)} collective-permute-done((bf16[16,4096]{1,0:T(8,128)(2,1)}, bf16[16,4096]{1,0:T(8,128)(2,1)S(1)}, u32[]{:S(2)}, u32[]{:S(2)}) %collective-permute-start.1) | collective-permute-done | bytes 131104 | tf_op jit(solution)/shard_map/ppermute | solution.py:19
  15.6 0.0 collective-permute-done.refs_0_
  15.6 3.1 %collective-permute-done.4.refs_4_ = bf16[16,4096]{1,0:T(8,128)(2,1)S(1)} collective-permute-done((bf16[16,4096]{1,0:T(8,128)(2,1)S(1)}, bf16[16,4096]{1,0:T(8,128)(2,1)S(1)}, u32[]{:S(2)}, u32[]{:S(2)}) %collective-permute-start.4) | collective-permute-done | bytes 131104 | tf_op jit(solution)/shard_map/ppermute | solution.py:19
  18.7 0.0 copy-done
  18.7 0.0 copy-done.5
  18.7 0.0 copy-done.7
  18.7 1.2 %middle.1.heads_ref = bf16[3,96,128]{2,1,0:T(8,128)(2,1)S(1)} custom-call(f32[3,1,4096]{2,1,0:T(1,128)S(1)} %bitcast.22, f32[2,128]{1,0:T(2,128)S(1)} %bitcast.26, bf16[3,4096,128]{2,1,0:T(8,128)(2,1)S(1)} %bitcast.10, bf16[16,4096]{1,0:T(8,128)(2,1)S(1)} %early.1.mixed_ref, bf16[16,4096]{1,0:T(8,128)(2,1)S(1)} %collective-permute-done.refs_0_, ...), custom_call_target="tpu_custom_call" | custom-call | flops 1000000000 | bytes 3145728 | tf_op jit(solution)/shard_map/middle/pallas_call | solution.py:107
  19.9 0.0 collective-permute-done.6.refs_1_
  20.0 0.3 collective-permute-done.5.refs_0_
  20.2 0.0 copy-done.1
  20.2 0.0 copy-done.3
  20.2 0.0 copy-done.6
  20.2 1.5 %layer.1 = (bf16[16,4096]{1,0:T(8,128)(2,1)S(1)}, bf16[16,4096]{1,0:T(8,128)(2,1)S(1)}, bf16[128,128]{1,0:T(8,128)(2,1)S(1)}) custom-call(s32[1]{0:T(128)S(6)} %copy.8.start_ref, f32[3,1,4096]{2,1,0:T(1,128)S(1)} %bitcast.23, bf16[3,4096,128]{2,1,0:T(8,128)(2,1)S(1)} %bitcast.11, bf16[2,256,128]{2,1,0:T(8,128)(2,1)S(1)} %bitcast.25, ...), custom_call_target="tpu_custom_call" | custom-call | tf_op jit(solution)/shard_map/layer/pallas_call | solution.py:208
  21.7 1.0 %collective-permute-start.7 = (bf16[16,4096]{1,0:T(8,128)(2,1)S(1)}, bf16[16,4096]{1,0:T(8,128)(2,1)S(1)}, u32[]{:S(2)}, u32[]{:S(2)}) collective-permute-start(bf16[16,4096]{1,0:T(8,128)(2,1)S(1)} %get-tuple-element.18), channel_id=1, source_target_pairs={{0,1},{1,0},{2,3},{3,2},{4,5},{5,4},{6,7},{7,6},{8,9},{9,8},{10,11... | collective-permute-start | bytes 393224 | tf_op jit(solution)/shard_map/ppermute | solution.py:19
  22.7 1.1 %collective-permute-start.8 = (bf16[16,4096]{1,0:T(8,128)(2,1)S(1)}, bf16[16,4096]{1,0:T(8,128)(2,1)S(1)}, u32[]{:S(2)}, u32[]{:S(2)}) collective-permute-start(bf16[16,4096]{1,0:T(8,128)(2,1)S(1)} %get-tuple-element.19), channel_id=1, source_target_pairs={{0,2},{1,3},{2,0},{3,1},{4,6},{5,7},{6,4},{7,5},{8,10},{9,11},{10,... | collective-permute-start | bytes 393224 | tf_op jit(solution)/shard_map/ppermute | solution.py:19
  23.8 0.4 rest.1
  24.2 1.1 %collective-permute-start.10 = (bf16[16,4096]{1,0:T(8,128)(2,1)S(1)}, bf16[16,4096]{1,0:T(8,128)(2,1)S(1)}, u32[]{:S(2)}, u32[]{:S(2)}) collective-permute-start(bf16[16,4096]{1,0:T(8,128)(2,1)S(1)} %get-tuple-element.21), channel_id=1, source_target_pairs={{0,1},{1,0},{2,3},{3,2},{4,5},{5,4},{6,7},{7,6},{8,9},{9,8},{10,11... | collective-permute-start | bytes 393224 | tf_op jit(solution)/shard_map/ppermute | solution.py:19
  25.2 2.4 %collective-permute-start.12 = (bf16[16,4096]{1,0:T(8,128)(2,1)S(1)}, bf16[16,4096]{1,0:T(8,128)(2,1)S(1)}, u32[]{:S(2)}, u32[]{:S(2)}) collective-permute-start(bf16[16,4096]{1,0:T(8,128)(2,1)S(1)} %get-tuple-element.23), channel_id=1, source_target_pairs={{0,6},{1,7},{2,4},{3,5},{4,2},{5,3},{6,0},{7,1},{8,14},{9,15},{10,... | collective-permute-start | bytes 393224 | tf_op jit(solution)/shard_map/ppermute | solution.py:19
  27.6 0.0 collective-permute-start.14
  27.7 0.3 collective-permute-done.7
  28.0 0.0 collective-permute-done.8
  28.0 0.1 add_convert_fusion.3
  28.0 1.3 %collective-permute-start.9 = (bf16[16,4096]{1,0:T(8,128)(2,1)S(1)}, bf16[16,4096]{1,0:T(8,128)(2,1)S(1)}, u32[]{:S(2)}, u32[]{:S(2)}) collective-permute-start(bf16[16,4096]{1,0:T(8,128)(2,1)S(1)} %add_convert_fusion.3), channel_id=1, source_target_pairs={{0,12},{1,13},{2,14},{3,15},{4,8},{5,9},{6,10},{7,11},{8,20},{9,21... | collective-permute-start | bytes 393224 | tf_op jit(solution)/shard_map/ppermute | solution.py:19
  29.3 0.3 collective-permute-done.10
  29.6 2.8 %collective-permute-start.11 = (bf16[16,4096]{1,0:T(8,128)(2,1)S(1)}, bf16[16,4096]{1,0:T(8,128)(2,1)S(1)}, u32[]{:S(2)}, u32[]{:S(2)}) collective-permute-start(bf16[16,4096]{1,0:T(8,128)(2,1)S(1)} %add_convert_fusion.2), channel_id=1, source_target_pairs={{0,10},{1,11},{2,8},{3,9},{4,14},{5,15},{6,12},{7,13},{8,18},{9,19... | collective-permute-start | bytes 393224 | tf_op jit(solution)/shard_map/ppermute | solution.py:19
  32.4 0.0 collective-permute-done.12
  32.4 0.6 %collective-permute-start.13 = (bf16[16,4096]{1,0:T(8,128)(2,1)S(1)}, bf16[16,4096]{1,0:T(8,128)(2,1)S(1)}, u32[]{:S(2)}, u32[]{:S(2)}) collective-permute-start(bf16[16,4096]{1,0:T(8,128)(2,1)S(1)} %add_convert_fusion.1), channel_id=1, source_target_pairs={{0,9},{1,8},{2,11},{3,10},{4,13},{5,12},{6,15},{7,14},{8,17},{9,16... | collective-permute-start | bytes 393224 | tf_op jit(solution)/shard_map/ppermute | solution.py:19
  33.1 0.0 collective-permute-done.14
  33.1 5.6 %collective-permute-done.9 = bf16[16,4096]{1,0:T(8,128)(2,1)S(1)} collective-permute-done((bf16[16,4096]{1,0:T(8,128)(2,1)S(1)}, bf16[16,4096]{1,0:T(8,128)(2,1)S(1)}, u32[]{:S(2)}, u32[]{:S(2)}) %collective-permute-start.9) | collective-permute-done | bytes 131104 | tf_op jit(solution)/shard_map/ppermute | solution.py:19
  38.7 0.0 collective-permute-done.11
  38.7 0.8 %collective-permute-done.13 = bf16[16,4096]{1,0:T(8,128)(2,1)S(1)} collective-permute-done((bf16[16,4096]{1,0:T(8,128)(2,1)S(1)}, bf16[16,4096]{1,0:T(8,128)(2,1)S(1)}, u32[]{:S(2)}, u32[]{:S(2)}) %collective-permute-start.13) | collective-permute-done | bytes 131104 | tf_op jit(solution)/shard_map/ppermute | solution.py:19
  39.5 0.7 %fusion = bf16[1,16,4096]{2,1,0:T(8,128)(2,1)} fusion(bf16[16,4096]{1,0:T(8,128)(2,1)S(1)} %collective-permute-done.14, bf16[16,4096]{1,0:T(8,128)(2,1)S(1)} %collective-permute-done.13, bf16[16,4096]{1,0:T(8,128)(2,1)S(1)} %collective-permute-done.11, bf16[16,4096]{1,0:T(8,128)(2,1)S(1)} %collective-permute-done.9), kind=kLoop, calls=%fused_computation.4 | loop fusion | flops 524288 | bytes 655360 | tf_op jit(solution)/shard_map/broadcast_in_dim | solution.py:227
  (2 shorter events, 0.1 us)
Async XLA Ops:
  0.0 10.6 %collective-permute-start.3 = (bf16[16,4096]{1,0:T(8,128)(2,1)}, bf16[16,4096]{1,0:T(8,128)(2,1)S(1)}, u32[]{:S(2)}, u32[]{:S(2)}) collective-permute-start(bf16[16,4096]{1,0:T(8,128)(2,1)} %bitcast.14), channel_id=1, source_target_pairs={{0,4},{1,5},{2,6},{3,7},{4,0},{5,1},{6,2},{7,3},{8,12},{9,13},{10,... | collective-permute-start | bytes 393224 | tf_op jit(solution)/shard_map/ppermute | solution.py:19
  4.0 9.2 %collective-permute-start.2 = (bf16[16,4096]{1,0:T(8,128)(2,1)}, bf16[16,4096]{1,0:T(8,128)(2,1)S(1)}, u32[]{:S(2)}, u32[]{:S(2)}) collective-permute-start(bf16[16,4096]{1,0:T(8,128)(2,1)} %bitcast.15), channel_id=1, source_target_pairs={{0,3},{1,2},{2,1},{3,0},{4,7},{5,6},{6,5},{7,4},{8,11},{9,10},{10,... | collective-permute-start | bytes 393224 | tf_op jit(solution)/shard_map/ppermute | solution.py:19
  6.6 9.0 %collective-permute-start.1 = (bf16[16,4096]{1,0:T(8,128)(2,1)}, bf16[16,4096]{1,0:T(8,128)(2,1)S(1)}, u32[]{:S(2)}, u32[]{:S(2)}) collective-permute-start(bf16[16,4096]{1,0:T(8,128)(2,1)} %bitcast.16), channel_id=1, source_target_pairs={{0,2},{1,3},{2,0},{3,1},{4,6},{5,7},{6,4},{7,5},{8,10},{9,11},{10,... | collective-permute-start | bytes 393224 | tf_op jit(solution)/shard_map/ppermute | solution.py:19
  7.0 8.6 %collective-permute-start = (bf16[16,4096]{1,0:T(8,128)(2,1)}, bf16[16,4096]{1,0:T(8,128)(2,1)S(1)}, u32[]{:S(2)}, u32[]{:S(2)}) collective-permute-start(bf16[16,4096]{1,0:T(8,128)(2,1)} %bitcast.17), channel_id=1, source_target_pairs={{0,1},{1,0},{2,3},{3,2},{4,5},{5,4},{6,7},{7,6},{8,9},{9,8},{10,11... | collective-permute-start | bytes 393224 | tf_op jit(solution)/shard_map/ppermute | solution.py:19
  7.5 0.9 %copy-start.2 = (bf16[1,16,4096]{2,1,0:T(8,128)(2,1)S(1)}, bf16[1,16,4096]{2,1,0:T(8,128)(2,1)}, u32[]{:S(2)}) copy-start(bf16[1,16,4096]{2,1,0:T(8,128)(2,1)} %param.7) | copy-start | bytes 393220
  8.5 0.8 %copy-start.4 = (f32[1,3,4096]{2,0,1:T(1,128)S(1)}, f32[1,3,4096]{2,0,1:T(1,128)}, u32[]{:S(2)}) copy-start(f32[1,3,4096]{2,0,1:T(1,128)} %param.8) | copy-start | bytes 147460
  9.3 9.4 %copy-start = (bf16[1,4096,3,128]{3,1,2,0:T(8,128)(2,1)S(1)}, bf16[1,4096,3,128]{3,1,2,0:T(8,128)(2,1)}, u32[]{:S(2)}) copy-start(bf16[1,4096,3,128]{3,1,2,0:T(8,128)(2,1)} %param.9) | copy-start | bytes 9437188
  9.3 9.4 %copy-start.5 = (f32[1,3,4096]{2,0,1:T(1,128)S(1)}, f32[1,3,4096]{2,0,1:T(1,128)}, u32[]{:S(2)}) copy-start(f32[1,3,4096]{2,0,1:T(1,128)} %param.8) | copy-start | bytes 147460
  9.3 9.4 %copy-start.7 = (f32[1,2,128]{2,1,0:T(2,128)S(1)}, f32[1,2,128]{2,1,0:T(2,128)}, u32[]{:S(2)}) copy-start(f32[1,2,128]{2,1,0:T(2,128)} %param.10) | copy-start | bytes 3076
  9.5 10.7 %copy-start.1 = (bf16[1,128,4096]{2,1,0:T(8,128)(2,1)S(1)}, bf16[1,128,4096]{2,1,0:T(8,128)(2,1)}, u32[]{:S(2)}) copy-start(bf16[1,128,4096]{2,1,0:T(8,128)(2,1)} %param.11) | copy-start | bytes 3145732
  9.6 10.7 %copy-start.3 = (bf16[1,16,4096]{2,1,0:T(8,128)(2,1)S(1)}, bf16[1,16,4096]{2,1,0:T(8,128)(2,1)}, u32[]{:S(2)}) copy-start(bf16[1,16,4096]{2,1,0:T(8,128)(2,1)} %param.7) | copy-start | bytes 393220
  9.6 10.7 %copy-start.6 = (bf16[1,2,256,128]{3,2,1,0:T(8,128)(2,1)S(1)}, bf16[1,2,256,128]{3,2,1,0:T(8,128)(2,1)}, u32[]{:S(2)}) copy-start(bf16[1,2,256,128]{3,2,1,0:T(8,128)(2,1)} %param.12) | copy-start | bytes 393220
  10.6 8.1 %collective-permute-start.4 = (bf16[16,4096]{1,0:T(8,128)(2,1)S(1)}, bf16[16,4096]{1,0:T(8,128)(2,1)S(1)}, u32[]{:S(2)}, u32[]{:S(2)}) collective-permute-start(bf16[16,4096]{1,0:T(8,128)(2,1)S(1)} %collective-permute-done.3.refs_3_), channel_id=1, source_target_pairs={{0,3},{1,2},{2,1},{3,0},{4,7},{5,6},{6,5},{7,4},{8,11},{9,10},{10,... | collective-permute-start | bytes 393224 | tf_op jit(solution)/shard_map/ppermute | solution.py:19
  12.4 7.6 %collective-permute-start.6 = (bf16[16,4096]{1,0:T(8,128)(2,1)S(1)}, bf16[16,4096]{1,0:T(8,128)(2,1)S(1)}, u32[]{:S(2)}, u32[]{:S(2)}) collective-permute-start(bf16[16,4096]{1,0:T(8,128)(2,1)S(1)} %collective-permute-done.3.refs_3_), channel_id=1, source_target_pairs={{0,1},{1,0},{2,3},{3,2},{4,5},{5,4},{6,7},{7,6},{8,9},{9,8},{10,11... | collective-permute-start | bytes 393224 | tf_op jit(solution)/shard_map/ppermute | solution.py:19
  13.2 7.0 %collective-permute-start.5 = (bf16[16,4096]{1,0:T(8,128)(2,1)S(1)}, bf16[16,4096]{1,0:T(8,128)(2,1)S(1)}, u32[]{:S(2)}, u32[]{:S(2)}) collective-permute-start(bf16[16,4096]{1,0:T(8,128)(2,1)S(1)} %collective-permute-done.3.refs_3_), channel_id=1, source_target_pairs={{0,2},{1,3},{2,0},{3,1},{4,6},{5,7},{6,4},{7,5},{8,10},{9,11},{10,... | collective-permute-start | bytes 393224 | tf_op jit(solution)/shard_map/ppermute | solution.py:19
  21.7 6.2 %collective-permute-start.7 = (bf16[16,4096]{1,0:T(8,128)(2,1)S(1)}, bf16[16,4096]{1,0:T(8,128)(2,1)S(1)}, u32[]{:S(2)}, u32[]{:S(2)}) collective-permute-start(bf16[16,4096]{1,0:T(8,128)(2,1)S(1)} %get-tuple-element.18), channel_id=1, source_target_pairs={{0,1},{1,0},{2,3},{3,2},{4,5},{5,4},{6,7},{7,6},{8,9},{9,8},{10,11... | collective-permute-start | bytes 393224 | tf_op jit(solution)/shard_map/ppermute | solution.py:19
  22.7 5.2 %collective-permute-start.8 = (bf16[16,4096]{1,0:T(8,128)(2,1)S(1)}, bf16[16,4096]{1,0:T(8,128)(2,1)S(1)}, u32[]{:S(2)}, u32[]{:S(2)}) collective-permute-start(bf16[16,4096]{1,0:T(8,128)(2,1)S(1)} %get-tuple-element.19), channel_id=1, source_target_pairs={{0,2},{1,3},{2,0},{3,1},{4,6},{5,7},{6,4},{7,5},{8,10},{9,11},{10,... | collective-permute-start | bytes 393224 | tf_op jit(solution)/shard_map/ppermute | solution.py:19
  24.2 5.4 %collective-permute-start.10 = (bf16[16,4096]{1,0:T(8,128)(2,1)S(1)}, bf16[16,4096]{1,0:T(8,128)(2,1)S(1)}, u32[]{:S(2)}, u32[]{:S(2)}) collective-permute-start(bf16[16,4096]{1,0:T(8,128)(2,1)S(1)} %get-tuple-element.21), channel_id=1, source_target_pairs={{0,1},{1,0},{2,3},{3,2},{4,5},{5,4},{6,7},{7,6},{8,9},{9,8},{10,11... | collective-permute-start | bytes 393224 | tf_op jit(solution)/shard_map/ppermute | solution.py:19
  25.2 7.2 %collective-permute-start.12 = (bf16[16,4096]{1,0:T(8,128)(2,1)S(1)}, bf16[16,4096]{1,0:T(8,128)(2,1)S(1)}, u32[]{:S(2)}, u32[]{:S(2)}) collective-permute-start(bf16[16,4096]{1,0:T(8,128)(2,1)S(1)} %get-tuple-element.23), channel_id=1, source_target_pairs={{0,6},{1,7},{2,4},{3,5},{4,2},{5,3},{6,0},{7,1},{8,14},{9,15},{10,... | collective-permute-start | bytes 393224 | tf_op jit(solution)/shard_map/ppermute | solution.py:19
  27.6 5.4 %collective-permute-start.14 = (bf16[16,4096]{1,0:T(8,128)(2,1)S(1)}, bf16[16,4096]{1,0:T(8,128)(2,1)S(1)}, u32[]{:S(2)}, u32[]{:S(2)}) collective-permute-start(bf16[16,4096]{1,0:T(8,128)(2,1)S(1)} %get-tuple-element.24), channel_id=1, source_target_pairs={{0,8},{1,9},{2,10},{3,11},{4,12},{5,13},{6,14},{7,15},{8,16},{9,17... | collective-permute-start | bytes 393224 | tf_op jit(solution)/shard_map/ppermute | solution.py:19
  28.0 10.6 %collective-permute-start.9 = (bf16[16,4096]{1,0:T(8,128)(2,1)S(1)}, bf16[16,4096]{1,0:T(8,128)(2,1)S(1)}, u32[]{:S(2)}, u32[]{:S(2)}) collective-permute-start(bf16[16,4096]{1,0:T(8,128)(2,1)S(1)} %add_convert_fusion.3), channel_id=1, source_target_pairs={{0,12},{1,13},{2,14},{3,15},{4,8},{5,9},{6,10},{7,11},{8,20},{9,21... | collective-permute-start | bytes 393224 | tf_op jit(solution)/shard_map/ppermute | solution.py:19
  29.6 9.1 %collective-permute-start.11 = (bf16[16,4096]{1,0:T(8,128)(2,1)S(1)}, bf16[16,4096]{1,0:T(8,128)(2,1)S(1)}, u32[]{:S(2)}, u32[]{:S(2)}) collective-permute-start(bf16[16,4096]{1,0:T(8,128)(2,1)S(1)} %add_convert_fusion.2), channel_id=1, source_target_pairs={{0,10},{1,11},{2,8},{3,9},{4,14},{5,15},{6,12},{7,13},{8,18},{9,19... | collective-permute-start | bytes 393224 | tf_op jit(solution)/shard_map/ppermute | solution.py:19
  32.4 7.0 %collective-permute-start.13 = (bf16[16,4096]{1,0:T(8,128)(2,1)S(1)}, bf16[16,4096]{1,0:T(8,128)(2,1)S(1)}, u32[]{:S(2)}, u32[]{:S(2)}) collective-permute-start(bf16[16,4096]{1,0:T(8,128)(2,1)S(1)} %add_convert_fusion.1), channel_id=1, source_target_pairs={{0,9},{1,8},{2,11},{3,10},{4,13},{5,12},{6,15},{7,14},{8,17},{9,16... | collective-permute-start | bytes 393224 | tf_op jit(solution)/shard_map/ppermute | solution.py:19

commit v5 on v4

--- a/solution.py
+++ b/solution.py
@@ -27,7 +27,7 @@
 
 def plan_back(count):
     if count == 8:
-        return [(5, 4), (6, 4), (4, 0), (3, 2), (2, 0), (7, 1), (1, 0), (0, 0)]
+        return [(5, 4), (6, 4), (7, 4), (4, 0), (3, 0), (2, 0), (1, 0), (0, 0)]
     return [(r, r & (r - 1)) for r in reversed(range(count))]
 
 

time: 40.5 us -> 40.5 us (level)
  the two profiles are of different devices: /device:TPU:0 before, /device:TPU:2 now
where the time goes in v5:
time: 40.5 us; the launch traced here: 40.3 us
  waiting for transfers between devices  17.1 us (42%)
  starting transfers between devices  16.6 us (41%)
  Pallas kernels  3.35 us (8%)
  local copies, waits for them, and re-layouts  1.77 us (4%)
  other arithmetic  0.81 us (2%)
  between operations  0.73 us (2%)
    ppermute x15, waiting for transfers between devices, route(): return lax.ppermute(block, ('section', 'seq'), pairs)  17.1 us
    ppermute x15, starting transfers between devices, route(): return lax.ppermute(block, ('section', 'seq'), pairs)  16.6 us
    unnamed x16, local copies, waits for them, and re-layouts  1.77 us
    pallas_call x1, Pallas kernels, per_device(): pl.pallas_call(functools.partial(layer_kernel, count, first), out_shape=[...  1.49 us
    pallas_call x1, Pallas kernels, middle_heads(): pl.pallas_call(middle_kernel, out_shape=jax.ShapeDtypeStruct((3, tokens,...  1.21 us
  transfers between devices with their start and end apart: 15, of which 10 were waited for; matrix products, arithmetic and copies ran while one was open for 0% of the time, Pallas kernels for 5%

profile of v5, /device:TPU:2, one launch (start us, length us, event | category | flops | bytes accessed | tf_op | source)
XLA Modules:
  0.0 40.3 jit_solution(12525041085727452466)
XLA Ops:
  0.0 2.6 %collective-permute-start.3 = (bf16[16,4096]{1,0:T(8,128)(2,1)}, bf16[16,4096]{1,0:T(8,128)(2,1)S(1)}, u32[]{:S(2)}, u32[]{:S(2)}) collective-permute-start(bf16[16,4096]{1,0:T(8,128)(2,1)} %bitcast.14), channel_id=1, source_target_pairs={{0,4},{1,5},{2,6},{3,7},{4,0},{5,1},{6,2},{7,3},{8,12},{9,13},{10,... | collective-permute-start | bytes 393224 | tf_op jit(solution)/shard_map/ppermute | solution.py:19
  2.6 2.5 %collective-permute-start.2 = (bf16[16,4096]{1,0:T(8,128)(2,1)}, bf16[16,4096]{1,0:T(8,128)(2,1)S(1)}, u32[]{:S(2)}, u32[]{:S(2)}) collective-permute-start(bf16[16,4096]{1,0:T(8,128)(2,1)} %bitcast.15), channel_id=1, source_target_pairs={{0,3},{1,2},{2,1},{3,0},{4,7},{5,6},{6,5},{7,4},{8,11},{9,10},{10,... | collective-permute-start | bytes 393224 | tf_op jit(solution)/shard_map/ppermute | solution.py:19
  5.1 0.4 %collective-permute-start.1 = (bf16[16,4096]{1,0:T(8,128)(2,1)}, bf16[16,4096]{1,0:T(8,128)(2,1)S(1)}, u32[]{:S(2)}, u32[]{:S(2)}) collective-permute-start(bf16[16,4096]{1,0:T(8,128)(2,1)} %bitcast.16), channel_id=1, source_target_pairs={{0,2},{1,3},{2,0},{3,1},{4,6},{5,7},{6,4},{7,5},{8,10},{9,11},{10,... | collective-permute-start | bytes 393224 | tf_op jit(solution)/shard_map/ppermute | solution.py:19
  5.6 0.5 %collective-permute-start = (bf16[16,4096]{1,0:T(8,128)(2,1)}, bf16[16,4096]{1,0:T(8,128)(2,1)S(1)}, u32[]{:S(2)}, u32[]{:S(2)}) collective-permute-start(bf16[16,4096]{1,0:T(8,128)(2,1)} %bitcast.17), channel_id=1, source_target_pairs={{0,1},{1,0},{2,3},{3,2},{4,5},{5,4},{6,7},{7,6},{8,9},{9,8},{10,11... | collective-permute-start | bytes 393224 | tf_op jit(solution)/shard_map/ppermute | solution.py:19
  6.1 0.0 copy-start.2
  6.1 0.9 %copy-done.2 = bf16[1,16,4096]{2,1,0:T(8,128)(2,1)S(1)} copy-done((bf16[1,16,4096]{2,1,0:T(8,128)(2,1)S(1)}, bf16[1,16,4096]{2,1,0:T(8,128)(2,1)}, u32[]{:S(2)}) %copy-start.2) | copy-done | bytes 131096
  7.0 0.0 copy-start.4
  7.0 0.8 %copy-done.4 = f32[1,3,4096]{2,0,1:T(1,128)S(1)} copy-done((f32[1,3,4096]{2,0,1:T(1,128)S(1)}, f32[1,3,4096]{2,0,1:T(1,128)}, u32[]{:S(2)}) %copy-start.4) | copy-done | bytes 49176
  7.8 0.0 copy-start
  7.8 0.0 copy-start.5
  7.8 0.0 copy-start.7
  7.8 0.3 early.1.mixed_ref
  8.1 0.0 copy-start.1
  8.1 0.0 copy-start.3
  8.1 0.0 copy-start.6
  8.1 1.1 %collective-permute-done.3.refs_3_ = bf16[16,4096]{1,0:T(8,128)(2,1)S(1)} collective-permute-done((bf16[16,4096]{1,0:T(8,128)(2,1)}, bf16[16,4096]{1,0:T(8,128)(2,1)S(1)}, u32[]{:S(2)}, u32[]{:S(2)}) %collective-permute-start.3) | collective-permute-done | bytes 131104 | tf_op jit(solution)/shard_map/ppermute | solution.py:19
  9.3 1.7 %collective-permute-start.4 = (bf16[16,4096]{1,0:T(8,128)(2,1)S(1)}, bf16[16,4096]{1,0:T(8,128)(2,1)S(1)}, u32[]{:S(2)}, u32[]{:S(2)}) collective-permute-start(bf16[16,4096]{1,0:T(8,128)(2,1)S(1)} %collective-permute-done.3.refs_3_), channel_id=1, source_target_pairs={{0,3},{1,2},{2,1},{3,0},{4,7},{5,6},{6,5},{7,4},{8,11},{9,10},{10,... | collective-permute-start | bytes 393224 | tf_op jit(solution)/shard_map/ppermute | solution.py:19
  10.9 0.5 %collective-permute-start.6 = (bf16[16,4096]{1,0:T(8,128)(2,1)S(1)}, bf16[16,4096]{1,0:T(8,128)(2,1)S(1)}, u32[]{:S(2)}, u32[]{:S(2)}) collective-permute-start(bf16[16,4096]{1,0:T(8,128)(2,1)S(1)} %collective-permute-done.3.refs_3_), channel_id=1, source_target_pairs={{0,1},{1,0},{2,3},{3,2},{4,5},{5,4},{6,7},{7,6},{8,9},{9,8},{10,11... | collective-permute-start | bytes 393224 | tf_op jit(solution)/shard_map/ppermute | solution.py:19
  11.4 0.3 collective-permute-done.2.refs_2_
  11.8 1.2 %collective-permute-start.5 = (bf16[16,4096]{1,0:T(8,128)(2,1)S(1)}, bf16[16,4096]{1,0:T(8,128)(2,1)S(1)}, u32[]{:S(2)}, u32[]{:S(2)}) collective-permute-start(bf16[16,4096]{1,0:T(8,128)(2,1)S(1)} %collective-permute-done.3.refs_3_), channel_id=1, source_target_pairs={{0,2},{1,3},{2,0},{3,1},{4,6},{5,7},{6,4},{7,5},{8,10},{9,11},{10,... | collective-permute-start | bytes 393224 | tf_op jit(solution)/shard_map/ppermute | solution.py:19
  13.6 0.6 %collective-permute-done.1.refs_1_ = bf16[16,4096]{1,0:T(8,128)(2,1)S(1)} collective-permute-done((bf16[16,4096]{1,0:T(8,128)(2,1)}, bf16[16,4096]{1,0:T(8,128)(2,1)S(1)}, u32[]{:S(2)}, u32[]{:S(2)}) %collective-permute-start.1) | collective-permute-done | bytes 131104 | tf_op jit(solution)/shard_map/ppermute | solution.py:19
  14.2 0.0 collective-permute-done.refs_0_
  14.2 3.0 %collective-permute-done.4.refs_4_ = bf16[16,4096]{1,0:T(8,128)(2,1)S(1)} collective-permute-done((bf16[16,4096]{1,0:T(8,128)(2,1)S(1)}, bf16[16,4096]{1,0:T(8,128)(2,1)S(1)}, u32[]{:S(2)}, u32[]{:S(2)}) %collective-permute-start.4) | collective-permute-done | bytes 131104 | tf_op jit(solution)/shard_map/ppermute | solution.py:19
  17.3 0.0 copy-done
  17.3 0.0 copy-done.5
  17.3 0.0 copy-done.7
  17.3 1.2 %middle.1.heads_ref = bf16[3,96,128]{2,1,0:T(8,128)(2,1)S(1)} custom-call(f32[3,1,4096]{2,1,0:T(1,128)S(1)} %bitcast.22, f32[2,128]{1,0:T(2,128)S(1)} %bitcast.26, bf16[3,4096,128]{2,1,0:T(8,128)(2,1)S(1)} %bitcast.10, bf16[16,4096]{1,0:T(8,128)(2,1)S(1)} %early.1.mixed_ref, bf16[16,4096]{1,0:T(8,128)(2,1)S(1)} %collective-permute-done.refs_0_, ...), custom_call_target="tpu_custom_call" | custom-call | flops 1000000000 | bytes 3145728 | tf_op jit(solution)/shard_map/middle/pallas_call | solution.py:107
  18.5 0.0 collective-permute-done.6.refs_1_
  18.5 0.3 collective-permute-done.5.refs_0_
  18.8 0.0 copy-done.1
  18.8 0.0 copy-done.3
  18.8 0.0 copy-done.6
  18.8 1.5 %layer.1 = (bf16[16,4096]{1,0:T(8,128)(2,1)S(1)}, bf16[16,4096]{1,0:T(8,128)(2,1)S(1)}, bf16[128,128]{1,0:T(8,128)(2,1)S(1)}) custom-call(s32[1]{0:T(128)S(6)} %copy.8.start_ref, f32[3,1,4096]{2,1,0:T(1,128)S(1)} %bitcast.23, bf16[3,4096,128]{2,1,0:T(8,128)(2,1)S(1)} %bitcast.11, bf16[2,256,128]{2,1,0:T(8,128)(2,1)S(1)} %bitcast.25, ...), custom_call_target="tpu_custom_call" | custom-call | tf_op jit(solution)/shard_map/layer/pallas_call | solution.py:208
  20.3 1.0 %collective-permute-start.7 = (bf16[16,4096]{1,0:T(8,128)(2,1)S(1)}, bf16[16,4096]{1,0:T(8,128)(2,1)S(1)}, u32[]{:S(2)}, u32[]{:S(2)}) collective-permute-start(bf16[16,4096]{1,0:T(8,128)(2,1)S(1)} %get-tuple-element.18), channel_id=1, source_target_pairs={{0,1},{1,0},{2,3},{3,2},{4,5},{5,4},{6,7},{7,6},{8,9},{9,8},{10,11... | collective-permute-start | bytes 393224 | tf_op jit(solution)/shard_map/ppermute | solution.py:19
  21.3 1.0 %collective-permute-start.8 = (bf16[16,4096]{1,0:T(8,128)(2,1)S(1)}, bf16[16,4096]{1,0:T(8,128)(2,1)S(1)}, u32[]{:S(2)}, u32[]{:S(2)}) collective-permute-start(bf16[16,4096]{1,0:T(8,128)(2,1)S(1)} %get-tuple-element.19), channel_id=1, source_target_pairs={{0,2},{1,3},{2,0},{3,1},{4,6},{5,7},{6,4},{7,5},{8,10},{9,11},{10,... | collective-permute-start | bytes 393224 | tf_op jit(solution)/shard_map/ppermute | solution.py:19
  22.4 0.4 rest.1
  22.7 1.6 %collective-permute-start.9 = (bf16[16,4096]{1,0:T(8,128)(2,1)S(1)}, bf16[16,4096]{1,0:T(8,128)(2,1)S(1)}, u32[]{:S(2)}, u32[]{:S(2)}) collective-permute-start(bf16[16,4096]{1,0:T(8,128)(2,1)S(1)} %get-tuple-element.20), channel_id=1, source_target_pairs={{0,3},{1,2},{2,1},{3,0},{4,7},{5,6},{6,5},{7,4},{8,11},{9,10},{10,... | collective-permute-start | bytes 393224 | tf_op jit(solution)/shard_map/ppermute | solution.py:19
  24.3 0.0 collective-permute-start.11
  24.3 2.0 %collective-permute-start.12 = (bf16[16,4096]{1,0:T(8,128)(2,1)S(1)}, bf16[16,4096]{1,0:T(8,128)(2,1)S(1)}, u32[]{:S(2)}, u32[]{:S(2)}) collective-permute-start(bf16[16,4096]{1,0:T(8,128)(2,1)S(1)} %get-tuple-element.22), channel_id=1, source_target_pairs={{0,10},{1,11},{2,8},{3,9},{4,14},{5,15},{6,12},{7,13},{8,18},{9,19... | collective-permute-start | bytes 393224 | tf_op jit(solution)/shard_map/ppermute | solution.py:19
  26.4 0.0 collective-permute-done.7
  26.4 0.0 collective-permute-start.13
  26.4 0.8 %collective-permute-done.8 = bf16[16,4096]{1,0:T(8,128)(2,1)S(1)} collective-permute-done((bf16[16,4096]{1,0:T(8,128)(2,1)S(1)}, bf16[16,4096]{1,0:T(8,128)(2,1)S(1)}, u32[]{:S(2)}, u32[]{:S(2)}) %collective-permute-start.8) | collective-permute-done | bytes 131104 | tf_op jit(solution)/shard_map/ppermute | solution.py:19
  27.3 1.3 %collective-permute-start.14 = (bf16[16,4096]{1,0:T(8,128)(2,1)S(1)}, bf16[16,4096]{1,0:T(8,128)(2,1)S(1)}, u32[]{:S(2)}, u32[]{:S(2)}) collective-permute-start(bf16[16,4096]{1,0:T(8,128)(2,1)S(1)} %get-tuple-element.24), channel_id=1, source_target_pairs={{0,8},{1,9},{2,10},{3,11},{4,12},{5,13},{6,14},{7,15},{8,16},{9,17... | collective-permute-start | bytes 393224 | tf_op jit(solution)/shard_map/ppermute | solution.py:19
  28.6 1.7 %collective-permute-done.9 = bf16[16,4096]{1,0:T(8,128)(2,1)S(1)} collective-permute-done((bf16[16,4096]{1,0:T(8,128)(2,1)S(1)}, bf16[16,4096]{1,0:T(8,128)(2,1)S(1)}, u32[]{:S(2)}, u32[]{:S(2)}) %collective-permute-start.9) | collective-permute-done | bytes 131104 | tf_op jit(solution)/shard_map/ppermute | solution.py:19
  30.3 0.1 add_convert_fusion.1
  30.3 0.1 collective-permute-start.10
  30.5 2.2 %collective-permute-done.11 = bf16[16,4096]{1,0:T(8,128)(2,1)S(1)} collective-permute-done((bf16[16,4096]{1,0:T(8,128)(2,1)S(1)}, bf16[16,4096]{1,0:T(8,128)(2,1)S(1)}, u32[]{:S(2)}, u32[]{:S(2)}) %collective-permute-start.11) | collective-permute-done | bytes 131104 | tf_op jit(solution)/shard_map/ppermute | solution.py:19
  32.7 3.2 %collective-permute-done.12 = bf16[16,4096]{1,0:T(8,128)(2,1)S(1)} collective-permute-done((bf16[16,4096]{1,0:T(8,128)(2,1)S(1)}, bf16[16,4096]{1,0:T(8,128)(2,1)S(1)}, u32[]{:S(2)}, u32[]{:S(2)}) %collective-permute-start.12) | collective-permute-done | bytes 131104 | tf_op jit(solution)/shard_map/ppermute | solution.py:19
  35.9 0.0 collective-permute-done.13
  35.9 0.0 collective-permute-done.14
  35.9 3.7 %collective-permute-done.10 = bf16[16,4096]{1,0:T(8,128)(2,1)S(1)} collective-permute-done((bf16[16,4096]{1,0:T(8,128)(2,1)S(1)}, bf16[16,4096]{1,0:T(8,128)(2,1)S(1)}, u32[]{:S(2)}, u32[]{:S(2)}) %collective-permute-start.10) | collective-permute-done | bytes 131104 | tf_op jit(solution)/shard_map/ppermute | solution.py:19
  39.6 0.7 %fusion = bf16[1,16,4096]{2,1,0:T(8,128)(2,1)} fusion(bf16[16,4096]{1,0:T(8,128)(2,1)S(1)} %collective-permute-done.14, bf16[16,4096]{1,0:T(8,128)(2,1)S(1)} %collective-permute-done.13, bf16[16,4096]{1,0:T(8,128)(2,1)S(1)} %collective-permute-done.12, bf16[16,4096]{1,0:T(8,128)(2,1)S(1)} %collective-permute-done.11, ...), kind=kLoop, calls=%fused_computation.2 | loop fusion | flops 655360 | bytes 786432 | tf_op jit(solution)/shard_map/broadcast_in_dim | solution.py:227
Async XLA Ops:
  0.0 9.3 %collective-permute-start.3 = (bf16[16,4096]{1,0:T(8,128)(2,1)}, bf16[16,4096]{1,0:T(8,128)(2,1)S(1)}, u32[]{:S(2)}, u32[]{:S(2)}) collective-permute-start(bf16[16,4096]{1,0:T(8,128)(2,1)} %bitcast.14), channel_id=1, source_target_pairs={{0,4},{1,5},{2,6},{3,7},{4,0},{5,1},{6,2},{7,3},{8,12},{9,13},{10,... | collective-permute-start | bytes 393224 | tf_op jit(solution)/shard_map/ppermute | solution.py:19
  2.6 9.2 %collective-permute-start.2 = (bf16[16,4096]{1,0:T(8,128)(2,1)}, bf16[16,4096]{1,0:T(8,128)(2,1)S(1)}, u32[]{:S(2)}, u32[]{:S(2)}) collective-permute-start(bf16[16,4096]{1,0:T(8,128)(2,1)} %bitcast.15), channel_id=1, source_target_pairs={{0,3},{1,2},{2,1},{3,0},{4,7},{5,6},{6,5},{7,4},{8,11},{9,10},{10,... | collective-permute-start | bytes 393224 | tf_op jit(solution)/shard_map/ppermute | solution.py:19
  5.1 9.1 %collective-permute-start.1 = (bf16[16,4096]{1,0:T(8,128)(2,1)}, bf16[16,4096]{1,0:T(8,128)(2,1)S(1)}, u32[]{:S(2)}, u32[]{:S(2)}) collective-permute-start(bf16[16,4096]{1,0:T(8,128)(2,1)} %bitcast.16), channel_id=1, source_target_pairs={{0,2},{1,3},{2,0},{3,1},{4,6},{5,7},{6,4},{7,5},{8,10},{9,11},{10,... | collective-permute-start | bytes 393224 | tf_op jit(solution)/shard_map/ppermute | solution.py:19
  5.6 8.7 %collective-permute-start = (bf16[16,4096]{1,0:T(8,128)(2,1)}, bf16[16,4096]{1,0:T(8,128)(2,1)S(1)}, u32[]{:S(2)}, u32[]{:S(2)}) collective-permute-start(bf16[16,4096]{1,0:T(8,128)(2,1)} %bitcast.17), channel_id=1, source_target_pairs={{0,1},{1,0},{2,3},{3,2},{4,5},{5,4},{6,7},{7,6},{8,9},{9,8},{10,11... | collective-permute-start | bytes 393224 | tf_op jit(solution)/shard_map/ppermute | solution.py:19
  6.1 0.9 %copy-start.2 = (bf16[1,16,4096]{2,1,0:T(8,128)(2,1)S(1)}, bf16[1,16,4096]{2,1,0:T(8,128)(2,1)}, u32[]{:S(2)}) copy-start(bf16[1,16,4096]{2,1,0:T(8,128)(2,1)} %param.7) | copy-start | bytes 393220
  7.0 0.8 %copy-start.4 = (f32[1,3,4096]{2,0,1:T(1,128)S(1)}, f32[1,3,4096]{2,0,1:T(1,128)}, u32[]{:S(2)}) copy-start(f32[1,3,4096]{2,0,1:T(1,128)} %param.8) | copy-start | bytes 147460
  7.8 9.4 %copy-start = (bf16[1,4096,3,128]{3,1,2,0:T(8,128)(2,1)S(1)}, bf16[1,4096,3,128]{3,1,2,0:T(8,128)(2,1)}, u32[]{:S(2)}) copy-start(bf16[1,4096,3,128]{3,1,2,0:T(8,128)(2,1)} %param.9) | copy-start | bytes 9437188
  7.8 9.4 %copy-start.5 = (f32[1,3,4096]{2,0,1:T(1,128)S(1)}, f32[1,3,4096]{2,0,1:T(1,128)}, u32[]{:S(2)}) copy-start(f32[1,3,4096]{2,0,1:T(1,128)} %param.8) | copy-start | bytes 147460
  7.8 9.4 %copy-start.7 = (f32[1,2,128]{2,1,0:T(2,128)S(1)}, f32[1,2,128]{2,1,0:T(2,128)}, u32[]{:S(2)}) copy-start(f32[1,2,128]{2,1,0:T(2,128)} %param.10) | copy-start | bytes 3076
  8.1 10.7 %copy-start.1 = (bf16[1,128,4096]{2,1,0:T(8,128)(2,1)S(1)}, bf16[1,128,4096]{2,1,0:T(8,128)(2,1)}, u32[]{:S(2)}) copy-start(bf16[1,128,4096]{2,1,0:T(8,128)(2,1)} %param.11) | copy-start | bytes 3145732
  8.1 10.7 %copy-start.3 = (bf16[1,16,4096]{2,1,0:T(8,128)(2,1)S(1)}, bf16[1,16,4096]{2,1,0:T(8,128)(2,1)}, u32[]{:S(2)}) copy-start(bf16[1,16,4096]{2,1,0:T(8,128)(2,1)} %param.7) | copy-start | bytes 393220
  8.1 10.7 %copy-start.6 = (bf16[1,2,256,128]{3,2,1,0:T(8,128)(2,1)S(1)}, bf16[1,2,256,128]{3,2,1,0:T(8,128)(2,1)}, u32[]{:S(2)}) copy-start(bf16[1,2,256,128]{3,2,1,0:T(8,128)(2,1)} %param.12) | copy-start | bytes 393220
  9.3 8.0 %collective-permute-start.4 = (bf16[16,4096]{1,0:T(8,128)(2,1)S(1)}, bf16[16,4096]{1,0:T(8,128)(2,1)S(1)}, u32[]{:S(2)}, u32[]{:S(2)}) collective-permute-start(bf16[16,4096]{1,0:T(8,128)(2,1)S(1)} %collective-permute-done.3.refs_3_), channel_id=1, source_target_pairs={{0,3},{1,2},{2,1},{3,0},{4,7},{5,6},{6,5},{7,4},{8,11},{9,10},{10,... | collective-permute-start | bytes 393224 | tf_op jit(solution)/shard_map/ppermute | solution.py:19
  10.9 7.6 %collective-permute-start.6 = (bf16[16,4096]{1,0:T(8,128)(2,1)S(1)}, bf16[16,4096]{1,0:T(8,128)(2,1)S(1)}, u32[]{:S(2)}, u32[]{:S(2)}) collective-permute-start(bf16[16,4096]{1,0:T(8,128)(2,1)S(1)} %collective-permute-done.3.refs_3_), channel_id=1, source_target_pairs={{0,1},{1,0},{2,3},{3,2},{4,5},{5,4},{6,7},{7,6},{8,9},{9,8},{10,11... | collective-permute-start | bytes 393224 | tf_op jit(solution)/shard_map/ppermute | solution.py:19
  11.8 7.1 %collective-permute-start.5 = (bf16[16,4096]{1,0:T(8,128)(2,1)S(1)}, bf16[16,4096]{1,0:T(8,128)(2,1)S(1)}, u32[]{:S(2)}, u32[]{:S(2)}) collective-permute-start(bf16[16,4096]{1,0:T(8,128)(2,1)S(1)} %collective-permute-done.3.refs_3_), channel_id=1, source_target_pairs={{0,2},{1,3},{2,0},{3,1},{4,6},{5,7},{6,4},{7,5},{8,10},{9,11},{10,... | collective-permute-start | bytes 393224 | tf_op jit(solution)/shard_map/ppermute | solution.py:19
  20.3 6.0 %collective-permute-start.7 = (bf16[16,4096]{1,0:T(8,128)(2,1)S(1)}, bf16[16,4096]{1,0:T(8,128)(2,1)S(1)}, u32[]{:S(2)}, u32[]{:S(2)}) collective-permute-start(bf16[16,4096]{1,0:T(8,128)(2,1)S(1)} %get-tuple-element.18), channel_id=1, source_target_pairs={{0,1},{1,0},{2,3},{3,2},{4,5},{5,4},{6,7},{7,6},{8,9},{9,8},{10,11... | collective-permute-start | bytes 393224 | tf_op jit(solution)/shard_map/ppermute | solution.py:19
  21.3 5.9 %collective-permute-start.8 = (bf16[16,4096]{1,0:T(8,128)(2,1)S(1)}, bf16[16,4096]{1,0:T(8,128)(2,1)S(1)}, u32[]{:S(2)}, u32[]{:S(2)}) collective-permute-start(bf16[16,4096]{1,0:T(8,128)(2,1)S(1)} %get-tuple-element.19), channel_id=1, source_target_pairs={{0,2},{1,3},{2,0},{3,1},{4,6},{5,7},{6,4},{7,5},{8,10},{9,11},{10,... | collective-permute-start | bytes 393224 | tf_op jit(solution)/shard_map/ppermute | solution.py:19
  22.7 7.5 %collective-permute-start.9 = (bf16[16,4096]{1,0:T(8,128)(2,1)S(1)}, bf16[16,4096]{1,0:T(8,128)(2,1)S(1)}, u32[]{:S(2)}, u32[]{:S(2)}) collective-permute-start(bf16[16,4096]{1,0:T(8,128)(2,1)S(1)} %get-tuple-element.20), channel_id=1, source_target_pairs={{0,3},{1,2},{2,1},{3,0},{4,7},{5,6},{6,5},{7,4},{8,11},{9,10},{10,... | collective-permute-start | bytes 393224 | tf_op jit(solution)/shard_map/ppermute | solution.py:19
  24.3 8.3 %collective-permute-start.11 = (bf16[16,4096]{1,0:T(8,128)(2,1)S(1)}, bf16[16,4096]{1,0:T(8,128)(2,1)S(1)}, u32[]{:S(2)}, u32[]{:S(2)}) collective-permute-start(bf16[16,4096]{1,0:T(8,128)(2,1)S(1)} %get-tuple-element.21), channel_id=1, source_target_pairs={{0,11},{1,10},{2,9},{3,8},{4,15},{5,14},{6,13},{7,12},{8,19},{9,18... | collective-permute-start | bytes 393224 | tf_op jit(solution)/shard_map/ppermute | solution.py:19
  24.3 11.6 %collective-permute-start.12 = (bf16[16,4096]{1,0:T(8,128)(2,1)S(1)}, bf16[16,4096]{1,0:T(8,128)(2,1)S(1)}, u32[]{:S(2)}, u32[]{:S(2)}) collective-permute-start(bf16[16,4096]{1,0:T(8,128)(2,1)S(1)} %get-tuple-element.22), channel_id=1, source_target_pairs={{0,10},{1,11},{2,8},{3,9},{4,14},{5,15},{6,12},{7,13},{8,18},{9,19... | collective-permute-start | bytes 393224 | tf_op jit(solution)/shard_map/ppermute | solution.py:19
  26.4 9.5 %collective-permute-start.13 = (bf16[16,4096]{1,0:T(8,128)(2,1)S(1)}, bf16[16,4096]{1,0:T(8,128)(2,1)S(1)}, u32[]{:S(2)}, u32[]{:S(2)}) collective-permute-start(bf16[16,4096]{1,0:T(8,128)(2,1)S(1)} %get-tuple-element.23), channel_id=1, source_target_pairs={{0,9},{1,8},{2,11},{3,10},{4,13},{5,12},{6,15},{7,14},{8,17},{9,16... | collective-permute-start | bytes 393224 | tf_op jit(solution)/shard_map/ppermute | solution.py:19
  27.3 8.6 %collective-permute-start.14 = (bf16[16,4096]{1,0:T(8,128)(2,1)S(1)}, bf16[16,4096]{1,0:T(8,128)(2,1)S(1)}, u32[]{:S(2)}, u32[]{:S(2)}) collective-permute-start(bf16[16,4096]{1,0:T(8,128)(2,1)S(1)} %get-tuple-element.24), channel_id=1, source_target_pairs={{0,8},{1,9},{2,10},{3,11},{4,12},{5,13},{6,14},{7,15},{8,16},{9,17... | collective-permute-start | bytes 393224 | tf_op jit(solution)/shard_map/ppermute | solution.py:19
  30.3 9.2 %collective-permute-start.10 = (bf16[16,4096]{1,0:T(8,128)(2,1)S(1)}, bf16[16,4096]{1,0:T(8,128)(2,1)S(1)}, u32[]{:S(2)}, u32[]{:S(2)}) collective-permute-start(bf16[16,4096]{1,0:T(8,128)(2,1)S(1)} %add_convert_fusion.1), channel_id=1, source_target_pairs={{0,12},{1,13},{2,14},{3,15},{4,8},{5,9},{6,10},{7,11},{8,20},{9,21... | collective-permute-start | bytes 393224 | tf_op jit(solution)/shard_map/ppermute | solution.py:19

commit v6 on v5

--- a/solution.py
+++ b/solution.py
@@ -192,7 +192,7 @@
     count = lax.axis_size("seq")
     tokens_in = hidden[0]
     rows, width = tokens_in.shape
-    order = [0, 1, 2, 3, 4, 7, 6, 5] if count == 8 else list(range(count))
+    order = [0, 2, 1, 3, 4, 7, 6, 5] if count == 8 else list(range(count))
     mod, own = modulation.transpose(1, 0, 2), tokens_in
     mixed = early_rows(mod, [own])
     blocks = gather(tokens_in, count, mixed)

time: 40.5 us -> 40.5 us (level)
  waiting for transfers between devices: 17.1 us -> 16.4 us
  starting transfers between devices: 16.6 us -> 17.3 us
    ppermute x15, starting transfers between devices: 16.6 us -> 17.3 us  [route(): return lax.ppermute(block, ('section', 'seq'), pairs)]
    ppermute x15, waiting for transfers between devices: 17.1 us -> 16.4 us  [route(): return lax.ppermute(block, ('section', 'seq'), pairs)]
  transfers between devices with their start and end apart: 15 -> 15, of which waited for: 10 -> 11; matrix products, arithmetic and copies ran while one was open for 0% -> 0% of each run, Pallas kernels for 5% -> 5%
where the time goes in v6:
time: 40.5 us; the launch traced here: 40.3 us
  starting transfers between devices  17.3 us (43%)
  waiting for transfers between devices  16.4 us (40%)
  Pallas kernels  3.35 us (8%)
  local copies, waits for them, and re-layouts  1.77 us (4%)
  other arithmetic  0.81 us (2%)
  between operations  0.73 us (2%)
    ppermute x15, starting transfers between devices, route(): return lax.ppermute(block, ('section', 'seq'), pairs)  17.3 us
    ppermute x15, waiting for transfers between devices, route(): return lax.ppermute(block, ('section', 'seq'), pairs)  16.4 us
    unnamed x16, local copies, waits for them, and re-layouts  1.77 us
    pallas_call x1, Pallas kernels, per_device(): pl.pallas_call(functools.partial(layer_kernel, count, first), out_shape=[...  1.49 us
    pallas_call x1, Pallas kernels, middle_heads(): pl.pallas_call(middle_kernel, out_shape=jax.ShapeDtypeStruct((3, tokens,...  1.22 us
  transfers between devices with their start and end apart: 15, of which 11 were waited for; matrix products, arithmetic and copies ran while one was open for 0% of the time, Pallas kernels for 5%

profile of v6, /device:TPU:2, one launch (start us, length us, event | category | flops | bytes accessed | tf_op | source)
XLA Modules:
  0.0 40.3 jit_solution(6104892297498951917)
XLA Ops:
  0.0 2.6 %collective-permute-start.3 = (bf16[16,4096]{1,0:T(8,128)(2,1)}, bf16[16,4096]{1,0:T(8,128)(2,1)S(1)}, u32[]{:S(2)}, u32[]{:S(2)}) collective-permute-start(bf16[16,4096]{1,0:T(8,128)(2,1)} %bitcast.14), channel_id=1, source_target_pairs={{0,4},{1,5},{2,6},{3,7},{4,0},{5,1},{6,2},{7,3},{8,12},{9,13},{10,... | collective-permute-start | bytes 393224 | tf_op jit(solution)/shard_map/ppermute | solution.py:19
  2.6 2.5 %collective-permute-start.2 = (bf16[16,4096]{1,0:T(8,128)(2,1)}, bf16[16,4096]{1,0:T(8,128)(2,1)S(1)}, u32[]{:S(2)}, u32[]{:S(2)}) collective-permute-start(bf16[16,4096]{1,0:T(8,128)(2,1)} %bitcast.15), channel_id=1, source_target_pairs={{0,3},{1,2},{2,1},{3,0},{4,7},{5,6},{6,5},{7,4},{8,11},{9,10},{10,... | collective-permute-start | bytes 393224 | tf_op jit(solution)/shard_map/ppermute | solution.py:19
  5.1 0.5 %collective-permute-start.1 = (bf16[16,4096]{1,0:T(8,128)(2,1)}, bf16[16,4096]{1,0:T(8,128)(2,1)S(1)}, u32[]{:S(2)}, u32[]{:S(2)}) collective-permute-start(bf16[16,4096]{1,0:T(8,128)(2,1)} %bitcast.16), channel_id=1, source_target_pairs={{0,1},{1,0},{2,3},{3,2},{4,5},{5,4},{6,7},{7,6},{8,9},{9,8},{10,11... | collective-permute-start | bytes 393224 | tf_op jit(solution)/shard_map/ppermute | solution.py:19
  5.6 0.4 %collective-permute-start = (bf16[16,4096]{1,0:T(8,128)(2,1)}, bf16[16,4096]{1,0:T(8,128)(2,1)S(1)}, u32[]{:S(2)}, u32[]{:S(2)}) collective-permute-start(bf16[16,4096]{1,0:T(8,128)(2,1)} %bitcast.17), channel_id=1, source_target_pairs={{0,2},{1,3},{2,0},{3,1},{4,6},{5,7},{6,4},{7,5},{8,10},{9,11},{10,... | collective-permute-start | bytes 393224 | tf_op jit(solution)/shard_map/ppermute | solution.py:19
  6.1 0.0 copy-start.2
  6.1 0.9 %copy-done.2 = bf16[1,16,4096]{2,1,0:T(8,128)(2,1)S(1)} copy-done((bf16[1,16,4096]{2,1,0:T(8,128)(2,1)S(1)}, bf16[1,16,4096]{2,1,0:T(8,128)(2,1)}, u32[]{:S(2)}) %copy-start.2) | copy-done | bytes 131096
  7.0 0.0 copy-start.4
  7.0 0.8 %copy-done.4 = f32[1,3,4096]{2,0,1:T(1,128)S(1)} copy-done((f32[1,3,4096]{2,0,1:T(1,128)S(1)}, f32[1,3,4096]{2,0,1:T(1,128)}, u32[]{:S(2)}) %copy-start.4) | copy-done | bytes 49176
  7.8 0.0 copy-start
  7.8 0.0 copy-start.5
  7.8 0.0 copy-start.7
  7.8 0.3 early.1.mixed_ref
  8.1 0.0 copy-start.1
  8.1 0.0 copy-start.3
  8.1 0.0 copy-start.6
  8.1 1.1 %collective-permute-done.3.refs_3_ = bf16[16,4096]{1,0:T(8,128)(2,1)S(1)} collective-permute-done((bf16[16,4096]{1,0:T(8,128)(2,1)}, bf16[16,4096]{1,0:T(8,128)(2,1)S(1)}, u32[]{:S(2)}, u32[]{:S(2)}) %collective-permute-start.3) | collective-permute-done | bytes 131104 | tf_op jit(solution)/shard_map/ppermute | solution.py:19
  9.3 1.7 %collective-permute-start.4 = (bf16[16,4096]{1,0:T(8,128)(2,1)S(1)}, bf16[16,4096]{1,0:T(8,128)(2,1)S(1)}, u32[]{:S(2)}, u32[]{:S(2)}) collective-permute-start(bf16[16,4096]{1,0:T(8,128)(2,1)S(1)} %collective-permute-done.3.refs_3_), channel_id=1, source_target_pairs={{0,3},{1,2},{2,1},{3,0},{4,7},{5,6},{6,5},{7,4},{8,11},{9,10},{10,... | collective-permute-start | bytes 393224 | tf_op jit(solution)/shard_map/ppermute | solution.py:19
  10.9 0.5 %collective-permute-start.6 = (bf16[16,4096]{1,0:T(8,128)(2,1)S(1)}, bf16[16,4096]{1,0:T(8,128)(2,1)S(1)}, u32[]{:S(2)}, u32[]{:S(2)}) collective-permute-start(bf16[16,4096]{1,0:T(8,128)(2,1)S(1)} %collective-permute-done.3.refs_3_), channel_id=1, source_target_pairs={{0,1},{1,0},{2,3},{3,2},{4,5},{5,4},{6,7},{7,6},{8,9},{9,8},{10,11... | collective-permute-start | bytes 393224 | tf_op jit(solution)/shard_map/ppermute | solution.py:19
  11.4 0.0 collective-permute-done.2.refs_2_
  11.4 1.5 %collective-permute-start.5 = (bf16[16,4096]{1,0:T(8,128)(2,1)S(1)}, bf16[16,4096]{1,0:T(8,128)(2,1)S(1)}, u32[]{:S(2)}, u32[]{:S(2)}) collective-permute-start(bf16[16,4096]{1,0:T(8,128)(2,1)S(1)} %collective-permute-done.3.refs_3_), channel_id=1, source_target_pairs={{0,2},{1,3},{2,0},{3,1},{4,6},{5,7},{6,4},{7,5},{8,10},{9,11},{10,... | collective-permute-start | bytes 393224 | tf_op jit(solution)/shard_map/ppermute | solution.py:19
  13.6 0.0 collective-permute-done.1.refs_1_
  13.6 0.6 %collective-permute-done.refs_0_ = bf16[16,4096]{1,0:T(8,128)(2,1)S(1)} collective-permute-done((bf16[16,4096]{1,0:T(8,128)(2,1)}, bf16[16,4096]{1,0:T(8,128)(2,1)S(1)}, u32[]{:S(2)}, u32[]{:S(2)}) %collective-permute-start) | collective-permute-done | bytes 131104 | tf_op jit(solution)/shard_map/ppermute | solution.py:19
  14.2 2.6 %collective-permute-done.4.refs_4_ = bf16[16,4096]{1,0:T(8,128)(2,1)S(1)} collective-permute-done((bf16[16,4096]{1,0:T(8,128)(2,1)S(1)}, bf16[16,4096]{1,0:T(8,128)(2,1)S(1)}, u32[]{:S(2)}, u32[]{:S(2)}) %collective-permute-start.4) | collective-permute-done | bytes 131104 | tf_op jit(solution)/shard_map/ppermute | solution.py:19
  16.8 0.0 copy-done
  16.8 0.0 copy-done.5
  16.8 0.0 copy-done.7
  16.8 1.2 %middle.1.heads_ref = bf16[3,96,128]{2,1,0:T(8,128)(2,1)S(1)} custom-call(f32[3,1,4096]{2,1,0:T(1,128)S(1)} %bitcast.22, f32[2,128]{1,0:T(2,128)S(1)} %bitcast.26, bf16[3,4096,128]{2,1,0:T(8,128)(2,1)S(1)} %bitcast.10, bf16[16,4096]{1,0:T(8,128)(2,1)S(1)} %early.1.mixed_ref, bf16[16,4096]{1,0:T(8,128)(2,1)S(1)} %collective-permute-done.refs_0_, ...), custom_call_target="tpu_custom_call" | custom-call | flops 1000000000 | bytes 3145728 | tf_op jit(solution)/shard_map/middle/pallas_call | solution.py:107
  18.0 0.4 %collective-permute-done.6.refs_1_ = bf16[16,4096]{1,0:T(8,128)(2,1)S(1)} collective-permute-done((bf16[16,4096]{1,0:T(8,128)(2,1)S(1)}, bf16[16,4096]{1,0:T(8,128)(2,1)S(1)}, u32[]{:S(2)}, u32[]{:S(2)}) %collective-permute-start.6) | collective-permute-done | bytes 131104 | tf_op jit(solution)/shard_map/ppermute | solution.py:19
  18.4 0.4 collective-permute-done.5.refs_0_
  18.8 0.0 copy-done.1
  18.8 0.0 copy-done.3
  18.8 0.0 copy-done.6
  18.8 1.5 %layer.1 = (bf16[16,4096]{1,0:T(8,128)(2,1)S(1)}, bf16[16,4096]{1,0:T(8,128)(2,1)S(1)}, bf16[128,128]{1,0:T(8,128)(2,1)S(1)}) custom-call(s32[1]{0:T(128)S(6)} %copy.8.start_ref, f32[3,1,4096]{2,1,0:T(1,128)S(1)} %bitcast.23, bf16[3,4096,128]{2,1,0:T(8,128)(2,1)S(1)} %bitcast.11, bf16[2,256,128]{2,1,0:T(8,128)(2,1)S(1)} %bitcast.25, ...), custom_call_target="tpu_custom_call" | custom-call | tf_op jit(solution)/shard_map/layer/pallas_call | solution.py:208
  20.3 1.0 %collective-permute-start.7 = (bf16[16,4096]{1,0:T(8,128)(2,1)S(1)}, bf16[16,4096]{1,0:T(8,128)(2,1)S(1)}, u32[]{:S(2)}, u32[]{:S(2)}) collective-permute-start(bf16[16,4096]{1,0:T(8,128)(2,1)S(1)} %get-tuple-element.18), channel_id=1, source_target_pairs={{0,1},{1,0},{2,3},{3,2},{4,5},{5,4},{6,7},{7,6},{8,9},{9,8},{10,11... | collective-permute-start | bytes 393224 | tf_op jit(solution)/shard_map/ppermute | solution.py:19
  21.3 1.0 %collective-permute-start.8 = (bf16[16,4096]{1,0:T(8,128)(2,1)S(1)}, bf16[16,4096]{1,0:T(8,128)(2,1)S(1)}, u32[]{:S(2)}, u32[]{:S(2)}) collective-permute-start(bf16[16,4096]{1,0:T(8,128)(2,1)S(1)} %get-tuple-element.19), channel_id=1, source_target_pairs={{0,2},{1,3},{2,0},{3,1},{4,6},{5,7},{6,4},{7,5},{8,10},{9,11},{10,... | collective-permute-start | bytes 393224 | tf_op jit(solution)/shard_map/ppermute | solution.py:19
  22.4 0.4 rest.1
  22.7 1.6 %collective-permute-start.9 = (bf16[16,4096]{1,0:T(8,128)(2,1)S(1)}, bf16[16,4096]{1,0:T(8,128)(2,1)S(1)}, u32[]{:S(2)}, u32[]{:S(2)}) collective-permute-start(bf16[16,4096]{1,0:T(8,128)(2,1)S(1)} %get-tuple-element.20), channel_id=1, source_target_pairs={{0,3},{1,2},{2,1},{3,0},{4,7},{5,6},{6,5},{7,4},{8,11},{9,10},{10,... | collective-permute-start | bytes 393224 | tf_op jit(solution)/shard_map/ppermute | solution.py:19
  24.3 0.0 collective-permute-start.11
  24.3 2.0 %collective-permute-start.12 = (bf16[16,4096]{1,0:T(8,128)(2,1)S(1)}, bf16[16,4096]{1,0:T(8,128)(2,1)S(1)}, u32[]{:S(2)}, u32[]{:S(2)}) collective-permute-start(bf16[16,4096]{1,0:T(8,128)(2,1)S(1)} %get-tuple-element.22), channel_id=1, source_target_pairs={{0,10},{1,11},{2,8},{3,9},{4,14},{5,15},{6,12},{7,13},{8,18},{9,19... | collective-permute-start | bytes 393224 | tf_op jit(solution)/shard_map/ppermute | solution.py:19
  26.4 0.2 collective-permute-done.7
  26.5 0.0 collective-permute-start.13
  26.5 0.6 %collective-permute-done.8 = bf16[16,4096]{1,0:T(8,128)(2,1)S(1)} collective-permute-done((bf16[16,4096]{1,0:T(8,128)(2,1)S(1)}, bf16[16,4096]{1,0:T(8,128)(2,1)S(1)}, u32[]{:S(2)}, u32[]{:S(2)}) %collective-permute-start.8) | collective-permute-done | bytes 131104 | tf_op jit(solution)/shard_map/ppermute | solution.py:19
  27.1 1.5 %collective-permute-start.14 = (bf16[16,4096]{1,0:T(8,128)(2,1)S(1)}, bf16[16,4096]{1,0:T(8,128)(2,1)S(1)}, u32[]{:S(2)}, u32[]{:S(2)}) collective-permute-start(bf16[16,4096]{1,0:T(8,128)(2,1)S(1)} %get-tuple-element.24), channel_id=1, source_target_pairs={{0,8},{1,9},{2,10},{3,11},{4,12},{5,13},{6,14},{7,15},{8,16},{9,17... | collective-permute-start | bytes 393224 | tf_op jit(solution)/shard_map/ppermute | solution.py:19
  28.6 1.5 %collective-permute-done.9 = bf16[16,4096]{1,0:T(8,128)(2,1)S(1)} collective-permute-done((bf16[16,4096]{1,0:T(8,128)(2,1)S(1)}, bf16[16,4096]{1,0:T(8,128)(2,1)S(1)}, u32[]{:S(2)}, u32[]{:S(2)}) %collective-permute-start.9) | collective-permute-done | bytes 131104 | tf_op jit(solution)/shard_map/ppermute | solution.py:19
  30.0 0.1 add_convert_fusion.1
  30.1 0.4 collective-permute-start.10
  30.5 2.2 %collective-permute-done.11 = bf16[16,4096]{1,0:T(8,128)(2,1)S(1)} collective-permute-done((bf16[16,4096]{1,0:T(8,128)(2,1)S(1)}, bf16[16,4096]{1,0:T(8,128)(2,1)S(1)}, u32[]{:S(2)}, u32[]{:S(2)}) %collective-permute-start.11) | collective-permute-done | bytes 131104 | tf_op jit(solution)/shard_map/ppermute | solution.py:19
  32.6 2.9 %collective-permute-done.12 = bf16[16,4096]{1,0:T(8,128)(2,1)S(1)} collective-permute-done((bf16[16,4096]{1,0:T(8,128)(2,1)S(1)}, bf16[16,4096]{1,0:T(8,128)(2,1)S(1)}, u32[]{:S(2)}, u32[]{:S(2)}) %collective-permute-start.12) | collective-permute-done | bytes 131104 | tf_op jit(solution)/shard_map/ppermute | solution.py:19
  35.5 0.0 collective-permute-done.13
  35.6 0.0 collective-permute-done.14
  35.6 4.0 %collective-permute-done.10 = bf16[16,4096]{1,0:T(8,128)(2,1)S(1)} collective-permute-done((bf16[16,4096]{1,0:T(8,128)(2,1)S(1)}, bf16[16,4096]{1,0:T(8,128)(2,1)S(1)}, u32[]{:S(2)}, u32[]{:S(2)}) %collective-permute-start.10) | collective-permute-done | bytes 131104 | tf_op jit(solution)/shard_map/ppermute | solution.py:19
  39.6 0.7 %fusion = bf16[1,16,4096]{2,1,0:T(8,128)(2,1)} fusion(bf16[16,4096]{1,0:T(8,128)(2,1)S(1)} %collective-permute-done.14, bf16[16,4096]{1,0:T(8,128)(2,1)S(1)} %collective-permute-done.13, bf16[16,4096]{1,0:T(8,128)(2,1)S(1)} %collective-permute-done.12, bf16[16,4096]{1,0:T(8,128)(2,1)S(1)} %collective-permute-done.11, ...), kind=kLoop, calls=%fused_computation.2 | loop fusion | flops 655360 | bytes 786432 | tf_op jit(solution)/shard_map/broadcast_in_dim | solution.py:227
Async XLA Ops:
  0.0 9.3 %collective-permute-start.3 = (bf16[16,4096]{1,0:T(8,128)(2,1)}, bf16[16,4096]{1,0:T(8,128)(2,1)S(1)}, u32[]{:S(2)}, u32[]{:S(2)}) collective-permute-start(bf16[16,4096]{1,0:T(8,128)(2,1)} %bitcast.14), channel_id=1, source_target_pairs={{0,4},{1,5},{2,6},{3,7},{4,0},{5,1},{6,2},{7,3},{8,12},{9,13},{10,... | collective-permute-start | bytes 393224 | tf_op jit(solution)/shard_map/ppermute | solution.py:19
  2.6 8.9 %collective-permute-start.2 = (bf16[16,4096]{1,0:T(8,128)(2,1)}, bf16[16,4096]{1,0:T(8,128)(2,1)S(1)}, u32[]{:S(2)}, u32[]{:S(2)}) collective-permute-start(bf16[16,4096]{1,0:T(8,128)(2,1)} %bitcast.15), channel_id=1, source_target_pairs={{0,3},{1,2},{2,1},{3,0},{4,7},{5,6},{6,5},{7,4},{8,11},{9,10},{10,... | collective-permute-start | bytes 393224 | tf_op jit(solution)/shard_map/ppermute | solution.py:19
  5.1 8.5 %collective-permute-start.1 = (bf16[16,4096]{1,0:T(8,128)(2,1)}, bf16[16,4096]{1,0:T(8,128)(2,1)S(1)}, u32[]{:S(2)}, u32[]{:S(2)}) collective-permute-start(bf16[16,4096]{1,0:T(8,128)(2,1)} %bitcast.16), channel_id=1, source_target_pairs={{0,1},{1,0},{2,3},{3,2},{4,5},{5,4},{6,7},{7,6},{8,9},{9,8},{10,11... | collective-permute-start | bytes 393224 | tf_op jit(solution)/shard_map/ppermute | solution.py:19
  5.6 8.6 %collective-permute-start = (bf16[16,4096]{1,0:T(8,128)(2,1)}, bf16[16,4096]{1,0:T(8,128)(2,1)S(1)}, u32[]{:S(2)}, u32[]{:S(2)}) collective-permute-start(bf16[16,4096]{1,0:T(8,128)(2,1)} %bitcast.17), channel_id=1, source_target_pairs={{0,2},{1,3},{2,0},{3,1},{4,6},{5,7},{6,4},{7,5},{8,10},{9,11},{10,... | collective-permute-start | bytes 393224 | tf_op jit(solution)/shard_map/ppermute | solution.py:19
  6.1 0.9 %copy-start.2 = (bf16[1,16,4096]{2,1,0:T(8,128)(2,1)S(1)}, bf16[1,16,4096]{2,1,0:T(8,128)(2,1)}, u32[]{:S(2)}) copy-start(bf16[1,16,4096]{2,1,0:T(8,128)(2,1)} %param.7) | copy-start | bytes 393220
  7.0 0.8 %copy-start.4 = (f32[1,3,4096]{2,0,1:T(1,128)S(1)}, f32[1,3,4096]{2,0,1:T(1,128)}, u32[]{:S(2)}) copy-start(f32[1,3,4096]{2,0,1:T(1,128)} %param.8) | copy-start | bytes 147460
  7.8 9.0 %copy-start = (bf16[1,4096,3,128]{3,1,2,0:T(8,128)(2,1)S(1)}, bf16[1,4096,3,128]{3,1,2,0:T(8,128)(2,1)}, u32[]{:S(2)}) copy-start(bf16[1,4096,3,128]{3,1,2,0:T(8,128)(2,1)} %param.9) | copy-start | bytes 9437188
  7.8 9.0 %copy-start.5 = (f32[1,3,4096]{2,0,1:T(1,128)S(1)}, f32[1,3,4096]{2,0,1:T(1,128)}, u32[]{:S(2)}) copy-start(f32[1,3,4096]{2,0,1:T(1,128)} %param.8) | copy-start | bytes 147460
  7.8 9.0 %copy-start.7 = (f32[1,2,128]{2,1,0:T(2,128)S(1)}, f32[1,2,128]{2,1,0:T(2,128)}, u32[]{:S(2)}) copy-start(f32[1,2,128]{2,1,0:T(2,128)} %param.10) | copy-start | bytes 3076
  8.1 10.7 %copy-start.1 = (bf16[1,128,4096]{2,1,0:T(8,128)(2,1)S(1)}, bf16[1,128,4096]{2,1,0:T(8,128)(2,1)}, u32[]{:S(2)}) copy-start(bf16[1,128,4096]{2,1,0:T(8,128)(2,1)} %param.11) | copy-start | bytes 3145732
  8.1 10.7 %copy-start.3 = (bf16[1,16,4096]{2,1,0:T(8,128)(2,1)S(1)}, bf16[1,16,4096]{2,1,0:T(8,128)(2,1)}, u32[]{:S(2)}) copy-start(bf16[1,16,4096]{2,1,0:T(8,128)(2,1)} %param.7) | copy-start | bytes 393220
  8.1 10.7 %copy-start.6 = (bf16[1,2,256,128]{3,2,1,0:T(8,128)(2,1)S(1)}, bf16[1,2,256,128]{3,2,1,0:T(8,128)(2,1)}, u32[]{:S(2)}) copy-start(bf16[1,2,256,128]{3,2,1,0:T(8,128)(2,1)} %param.12) | copy-start | bytes 393220
  9.3 7.5 %collective-permute-start.4 = (bf16[16,4096]{1,0:T(8,128)(2,1)S(1)}, bf16[16,4096]{1,0:T(8,128)(2,1)S(1)}, u32[]{:S(2)}, u32[]{:S(2)}) collective-permute-start(bf16[16,4096]{1,0:T(8,128)(2,1)S(1)} %collective-permute-done.3.refs_3_), channel_id=1, source_target_pairs={{0,3},{1,2},{2,1},{3,0},{4,7},{5,6},{6,5},{7,4},{8,11},{9,10},{10,... | collective-permute-start | bytes 393224 | tf_op jit(solution)/shard_map/ppermute | solution.py:19
  10.9 7.5 %collective-permute-start.6 = (bf16[16,4096]{1,0:T(8,128)(2,1)S(1)}, bf16[16,4096]{1,0:T(8,128)(2,1)S(1)}, u32[]{:S(2)}, u32[]{:S(2)}) collective-permute-start(bf16[16,4096]{1,0:T(8,128)(2,1)S(1)} %collective-permute-done.3.refs_3_), channel_id=1, source_target_pairs={{0,1},{1,0},{2,3},{3,2},{4,5},{5,4},{6,7},{7,6},{8,9},{9,8},{10,11... | collective-permute-start | bytes 393224 | tf_op jit(solution)/shard_map/ppermute | solution.py:19
  11.4 7.4 %collective-permute-start.5 = (bf16[16,4096]{1,0:T(8,128)(2,1)S(1)}, bf16[16,4096]{1,0:T(8,128)(2,1)S(1)}, u32[]{:S(2)}, u32[]{:S(2)}) collective-permute-start(bf16[16,4096]{1,0:T(8,128)(2,1)S(1)} %collective-permute-done.3.refs_3_), channel_id=1, source_target_pairs={{0,2},{1,3},{2,0},{3,1},{4,6},{5,7},{6,4},{7,5},{8,10},{9,11},{10,... | collective-permute-start | bytes 393224 | tf_op jit(solution)/shard_map/ppermute | solution.py:19
  20.3 6.2 %collective-permute-start.7 = (bf16[16,4096]{1,0:T(8,128)(2,1)S(1)}, bf16[16,4096]{1,0:T(8,128)(2,1)S(1)}, u32[]{:S(2)}, u32[]{:S(2)}) collective-permute-start(bf16[16,4096]{1,0:T(8,128)(2,1)S(1)} %get-tuple-element.18), channel_id=1, source_target_pairs={{0,1},{1,0},{2,3},{3,2},{4,5},{5,4},{6,7},{7,6},{8,9},{9,8},{10,11... | collective-permute-start | bytes 393224 | tf_op jit(solution)/shard_map/ppermute | solution.py:19
  21.3 5.8 %collective-permute-start.8 = (bf16[16,4096]{1,0:T(8,128)(2,1)S(1)}, bf16[16,4096]{1,0:T(8,128)(2,1)S(1)}, u32[]{:S(2)}, u32[]{:S(2)}) collective-permute-start(bf16[16,4096]{1,0:T(8,128)(2,1)S(1)} %get-tuple-element.19), channel_id=1, source_target_pairs={{0,2},{1,3},{2,0},{3,1},{4,6},{5,7},{6,4},{7,5},{8,10},{9,11},{10,... | collective-permute-start | bytes 393224 | tf_op jit(solution)/shard_map/ppermute | solution.py:19
  22.7 7.3 %collective-permute-start.9 = (bf16[16,4096]{1,0:T(8,128)(2,1)S(1)}, bf16[16,4096]{1,0:T(8,128)(2,1)S(1)}, u32[]{:S(2)}, u32[]{:S(2)}) collective-permute-start(bf16[16,4096]{1,0:T(8,128)(2,1)S(1)} %get-tuple-element.20), channel_id=1, source_target_pairs={{0,3},{1,2},{2,1},{3,0},{4,7},{5,6},{6,5},{7,4},{8,11},{9,10},{10,... | collective-permute-start | bytes 393224 | tf_op jit(solution)/shard_map/ppermute | solution.py:19
  24.3 8.3 %collective-permute-start.11 = (bf16[16,4096]{1,0:T(8,128)(2,1)S(1)}, bf16[16,4096]{1,0:T(8,128)(2,1)S(1)}, u32[]{:S(2)}, u32[]{:S(2)}) collective-permute-start(bf16[16,4096]{1,0:T(8,128)(2,1)S(1)} %get-tuple-element.21), channel_id=1, source_target_pairs={{0,11},{1,10},{2,9},{3,8},{4,15},{5,14},{6,13},{7,12},{8,19},{9,18... | collective-permute-start | bytes 393224 | tf_op jit(solution)/shard_map/ppermute | solution.py:19
  24.3 11.2 %collective-permute-start.12 = (bf16[16,4096]{1,0:T(8,128)(2,1)S(1)}, bf16[16,4096]{1,0:T(8,128)(2,1)S(1)}, u32[]{:S(2)}, u32[]{:S(2)}) collective-permute-start(bf16[16,4096]{1,0:T(8,128)(2,1)S(1)} %get-tuple-element.22), channel_id=1, source_target_pairs={{0,10},{1,11},{2,8},{3,9},{4,14},{5,15},{6,12},{7,13},{8,18},{9,19... | collective-permute-start | bytes 393224 | tf_op jit(solution)/shard_map/ppermute | solution.py:19
  26.5 9.0 %collective-permute-start.13 = (bf16[16,4096]{1,0:T(8,128)(2,1)S(1)}, bf16[16,4096]{1,0:T(8,128)(2,1)S(1)}, u32[]{:S(2)}, u32[]{:S(2)}) collective-permute-start(bf16[16,4096]{1,0:T(8,128)(2,1)S(1)} %get-tuple-element.23), channel_id=1, source_target_pairs={{0,9},{1,8},{2,11},{3,10},{4,13},{5,12},{6,15},{7,14},{8,17},{9,16... | collective-permute-start | bytes 393224 | tf_op jit(solution)/shard_map/ppermute | solution.py:19
  27.1 8.5 %collective-permute-start.14 = (bf16[16,4096]{1,0:T(8,128)(2,1)S(1)}, bf16[16,4096]{1,0:T(8,128)(2,1)S(1)}, u32[]{:S(2)}, u32[]{:S(2)}) collective-permute-start(bf16[16,4096]{1,0:T(8,128)(2,1)S(1)} %get-tuple-element.24), channel_id=1, source_target_pairs={{0,8},{1,9},{2,10},{3,11},{4,12},{5,13},{6,14},{7,15},{8,16},{9,17... | collective-permute-start | bytes 393224 | tf_op jit(solution)/shard_map/ppermute | solution.py:19
  30.1 9.5 %collective-permute-start.10 = (bf16[16,4096]{1,0:T(8,128)(2,1)S(1)}, bf16[16,4096]{1,0:T(8,128)(2,1)S(1)}, u32[]{:S(2)}, u32[]{:S(2)}) collective-permute-start(bf16[16,4096]{1,0:T(8,128)(2,1)S(1)} %add_convert_fusion.1), channel_id=1, source_target_pairs={{0,12},{1,13},{2,14},{3,15},{4,8},{5,9},{6,10},{7,11},{8,20},{9,21... | collective-permute-start | bytes 393224 | tf_op jit(solution)/shard_map/ppermute | solution.py:19
